TPU v7x, 32 devices: a whole 2x2x4 slice. The times are simulated.
32 devices in a mesh: dp: 8 (over z, x), tensor: 4 (over y, core).
Axes of the slice: x: 2, y: 2, z: 4, core: 2. Of those that a mesh axis runs over, the one named last changes fastest.
Arguments:
- activations: bfloat16 [3072, 8192], P('dp', 'tensor'), may hold values from -6 to 6
- basis: bfloat16 [8192, 256], replicated, may hold values from -0.0625 to 0.0625
- out_grad: bfloat16 [3072, 14592], P('dp', 'tensor'), may hold values from -0.15625 to 0.15625
- first_moment: float32 [4, 3648, 256], P('tensor', 'dp'), may hold values from -6 to 6
- second_moment: float32 [4, 3648, 256], P('tensor', 'dp'), may hold values from 0.02 to 0.5
Outputs:
- new_first_moment: float32 [4, 3648, 256], P('tensor', 'dp')
- new_second_moment: float32 [4, 3648, 256], P('tensor', 'dp')
- full_update: bfloat16 [4, 3648, 8192], P('tensor', 'dp')
All inputs are finite; a program needn't handle non-finite values.
Results may differ from a plain program's by a relative error of at most 0.005.
Values may be sent and summed in bfloat16 or wider, within the bound.
No kernel may reach another device: no remote copies, remote signals or barrier semaphores. Data moves between devices by JAX's collectives and lax.ppermute only.
A program may use at most 64 MiB of HBM per device.

v0:
```python
import jax
import jax.numpy as jnp
from jax import lax
from jax.sharding import PartitionSpec as P

STEP = 100


def gather_rows(coded_local):
    return lax.all_gather(coded_local, "tensor", axis=0, tiled=True)


def owner_total(term):
    return lax.psum_scatter(term, "dp", scatter_dimension=0, tiled=True)


def on_device(activations, basis, out_grad, first_moment, second_moment):
    feat_count = activations.shape[1]
    feat_start = lax.axis_index("tensor") * feat_count
    basis_rows = lax.dynamic_slice_in_dim(basis, feat_start, feat_count, 0)
    partial_code = jnp.dot(activations, basis_rows, preferred_element_type=jnp.float32)
    coded_local = lax.psum_scatter(partial_code, "tensor", scatter_dimension=0, tiled=True).astype(
        jnp.bfloat16
    )
    contract = (((0,), (0,)), ((), ()))
    coded_rows = gather_rows(coded_local)
    term = lax.dot_general(out_grad, coded_rows, contract, preferred_element_type=jnp.float32)
    coded_grad = owner_total(term)
    coded_grad = coded_grad[None]
    new_first = 0.9 * first_moment + 0.1 * coded_grad
    new_second = 0.999 * second_moment + 0.001 * coded_grad * coded_grad
    first_hat = new_first / (1.0 - 0.9**STEP)
    second_hat = new_second / (1.0 - 0.999**STEP)
    direction = (first_hat / (jnp.sqrt(second_hat) + 1e-08)).astype(jnp.bfloat16)
    update = lax.dot_general(
        direction[0], basis, (((1,), (1,)), ((), ())), preferred_element_type=jnp.float32
    )
    return (new_first, new_second, update.astype(jnp.bfloat16)[None])


def solution(mesh):
    placed = (
        P("dp", "tensor"),
        P(),
        P("dp", "tensor"),
        P("tensor", "dp", None),
        P("tensor", "dp", None),
    )
    return jax.shard_map(
        on_device,
        mesh=mesh,
        in_specs=placed,
        out_specs=(P("tensor", "dp", None), P("tensor", "dp", None), P("tensor", "dp", None)),
        check_vma=False,
    )
```

profile of v0, /device:TPU:0, one launch (start us, length us, event | category | flops | bytes accessed | tf_op | source)
XLA Modules:
  0.0 142.4 jit_solution(8747852603244789183)
XLA Ops:
  7.2 0.0 copy-start
  7.2 0.0 reduce-scatter.7.cloned.1.call-start
  7.2 2.6 %convolution_bitcast_fusion.1 = f32[384,256]{0,1:T(8,128)S(1)} fusion(bf16[384,2048]{1,0:T(8,128)(2,1)} %param.5, bf16[8192,256]{1,0:T(8,128)(2,1)} %param.6, s32[]{:T(128)S(6)} %select_n.3), kind=kOutput, calls=%fused_computation.3 | convolution fusion | flops 402653184 | bytes 3014660 | tf_op jit(solution)/shard_map/dot_general | solution.py:21
  9.9 0.9 copy.10
  10.8 0.0 reduce-scatter.7.cloned.1.call-update
  10.8 0.0 reduce-scatter.5.cloned.1.call-start
  10.9 23.8 %reduce-scatter.7.cloned.1.call-done = f32[96,256]{1,0:T(8,128)} async-done(((f32[384,256]{1,0:T(8,128)}), f32[96,256]{1,0:T(8,128)}) %reduce-scatter.7.cloned.1.call-update) | async-done | bytes 98320 | tf_op jit(solution)/shard_map/reduce_scatter | solution.py:22
  34.6 0.9 convert_element_type.9
  35.5 5.6 %all_gather.3 = bf16[384,256]{1,0:T(8,128)(2,1)S(1)} all-gather(bf16[96,256]{1,0:T(8,128)(2,1)S(1)} %convert_element_type.9), channel_id=1, replica_groups=mesh['dp'=8,'tensor'=4] {'tensor'}, dimensions={0}, use_global_device_ids=true | all-gather | bytes 245760 | tf_op jit(solution)/shard_map/all_gather | solution.py:10
  41.1 0.0 copy-done
  41.1 3.0 %convolution_bitcast_fusion = f32[3648,256]{1,0:T(8,128)} fusion(bf16[384,3648]{0,1:T(8,128)(2,1)S(1)} %copy-done, bf16[384,256]{1,0:T(8,128)(2,1)S(1)} %all_gather.3), kind=kOutput, calls=%fused_computation.2 | convolution fusion | flops 717225984 | bytes 6733824 | tf_op jit(solution)/shard_map/dot_general | solution.py:27
  44.1 0.0 copy-start.3
  44.1 0.0 reduce-scatter.5.cloned.1.call-update
  44.1 82.2 %reduce-scatter.5.cloned.1.call-done = f32[456,256]{1,0:T(8,128)} async-done(((f32[3648,256]{1,0:T(8,128)}), f32[456,256]{1,0:T(8,128)}) %reduce-scatter.5.cloned.1.call-update) | async-done | bytes 466960 | tf_op jit(solution)/shard_map/reduce_scatter | solution.py:14
  126.3 0.0 copy-done.3
  126.3 1.3 fusion.3
  127.7 0.0 copy-start.1
  127.7 0.0 copy-start.2
  127.7 7.8 %fusion = bf16[1,456,8192]{2,1,0:T(8,128)(2,1)} fusion(bf16[8192,256]{1,0:T(8,128)(2,1)} %param.6, f32[1,456,256]{2,1,0:T(8,128)S(1)} %get-tuple-element.3, f32[1,456,256]{2,1,0:T(8,128)S(1)} %get-tuple-element.4), kind=kOutput, calls=%fused_computation.1 | convolution fusion | flops 1916921856 | bytes 12599296 | tf_op jit(solution)/shard_map/dot_general | solution.py:35
  135.5 0.0 copy-done.1
  135.5 0.0 copy-done.2
Async XLA Ops:
  7.2 34.0 %copy-start = (bf16[384,3648]{0,1:T(8,128)(2,1)S(1)}, bf16[384,3648]{0,1:T(8,128)(2,1)}, u32[]{:S(2)}) copy-start(bf16[384,3648]{0,1:T(8,128)(2,1)} %param.7) | copy-start | bytes 8404996
  7.2 27.5 %reduce-scatter.7.cloned.1.call-start = ((), (), s32[]{:S(2)}) async-start(), calls=%async_computation.3 | async-start | bytes 491520 | tf_op jit(solution)/shard_map/reduce_scatter | solution.py:22
  10.8 115.5 %reduce-scatter.5.cloned.1.call-start = ((), (), s32[]{:S(2)}) async-start(), calls=%async_computation.2 | async-start | bytes 4202496 | tf_op jit(solution)/shard_map/reduce_scatter | solution.py:14
  44.1 82.2 %copy-start.3 = (f32[1,456,256]{2,1,0:T(8,128)S(1)}, f32[1,456,256]{2,1,0:T(8,128)}, u32[]{:S(2)}) copy-start(f32[1,456,256]{2,1,0:T(8,128)} %param.9) | copy-start | bytes 1400836
  127.7 7.9 %copy-start.1 = (f32[1,456,256]{2,1,0:T(8,128)}, f32[1,456,256]{2,1,0:T(8,128)S(1)}, u32[]{:S(2)}) copy-start(f32[1,456,256]{2,1,0:T(8,128)S(1)} %get-tuple-element.3) | copy-start | bytes 1400836
  127.7 7.9 %copy-start.2 = (f32[1,456,256]{2,1,0:T(8,128)}, f32[1,456,256]{2,1,0:T(8,128)S(1)}, u32[]{:S(2)}) copy-start(f32[1,456,256]{2,1,0:T(8,128)S(1)} %get-tuple-element.4) | copy-start | bytes 1400836
Sparse Core Ops, SparseCore 0:
  11.1 23.5 reduce-scatter.6
  44.3 82.0 reduce-scatter.4
where the time goes:
time: 143 us; the launch traced here: 142 us
  waiting for transfers between devices  106 us (74%)
  between operations  14.1 us (10%)
  matrix products  13.5 us (9%)
  blocking collectives  5.59 us (4%)
  other arithmetic  2.2 us (2%)
    reduce_scatter x1, waiting for transfers between devices, owner_total(): return lax.psum_scatter(term, 'dp', scatter_dimension=0, tiled=True)  82.2 us
    reduce_scatter x1, waiting for transfers between devices, on_device(): lax.psum_scatter(partial_code, 'tensor', scatter_dimension=0, tiled=True)  23.8 us
    dot_general x1, matrix products, on_device(): lax.dot_general(direction[0], basis, (((1,), (1,)), ((), ())), preferred_...  7.84 us
    all_gather x1, blocking collectives, gather_rows(): return lax.all_gather(coded_local, 'tensor', axis=0, tiled=True)  5.59 us
    dot_general x1, matrix products, on_device(): lax.dot_general(out_grad, coded_rows, contract, preferred_element_type=jn...  2.98 us
  transfers between devices with their start and end apart: 2, of which 2 were waited for; matrix products, arithmetic and copies ran while one was open for 0% of the time, Pallas kernels for 0%

commit v1 on v0

v1 whole, which is shorter than its diff:
```python
import functools

import jax
import jax.numpy as jnp
from jax import lax
from jax.experimental import pallas as pl
from jax.experimental.pallas import tpu as pltpu
from jax.sharding import PartitionSpec as P

STEP = 100
BF = jnp.bfloat16
F32 = jnp.float32


def swap(value, axis, bit, count):
    return lax.ppermute(value, axis, [(i, i ^ bit) for i in range(count)])


DEEP = 4


def partial_code_kernel(activations, basis, keep, send, act_buf, basis_buf, total, sems):
    feats = activations.shape[1]
    start = lax.axis_index("tensor") * feats
    step = feats // DEEP
    copies = []
    for k in range(DEEP):
        copies.append(
            pltpu.make_async_copy(
                basis.at[pl.ds(pl.multiple_of(start + k * step, step), step), :],
                basis_buf.at[k],
                sems.at[0, k],
            )
        )
        copies.append(
            pltpu.make_async_copy(
                activations.at[:, pl.ds(k * step, step)], act_buf.at[k], sems.at[1, k]
            )
        )
    for copy in copies:
        copy.start()
    for k in range(DEEP):
        copies[2 * k].wait()
        copies[2 * k + 1].wait()
        part = jnp.dot(act_buf[k], basis_buf[k], preferred_element_type=F32)
        total[...] = part if k == 0 else total[...] + part
    half = keep.shape[0]
    core = lax.rem(lax.axis_index("tensor"), 2)
    keep[...] = total[pl.ds(pl.multiple_of(core * half, half), half), :]
    send[...] = total[pl.ds(pl.multiple_of((1 - core) * half, half), half), :].astype(BF)


def partial_code(activations, basis):
    rows, feats = activations.shape
    rank = basis.shape[1]
    vmem = pl.BlockSpec(memory_space=pltpu.VMEM)
    hbm = pl.BlockSpec(memory_space=pltpu.HBM)
    return pl.pallas_call(
        partial_code_kernel,
        out_shape=(
            jax.ShapeDtypeStruct((rows // 2, rank), F32),
            jax.ShapeDtypeStruct((rows // 2, rank), BF),
        ),
        in_specs=[hbm, hbm],
        out_specs=(vmem, vmem),
        scratch_shapes=[
            pltpu.VMEM((DEEP, rows, feats // DEEP), BF),
            pltpu.VMEM((DEEP, feats // DEEP, rank), BF),
            pltpu.VMEM((rows, rank), F32),
            pltpu.SemaphoreType.DMA((2, DEEP)),
        ],
        compiler_params=pltpu.CompilerParams(vmem_limit_bytes=53 * 2**20),
        cost_estimate=pl.CostEstimate(
            flops=2 * rows * feats * rank,
            bytes_accessed=2 * feats * (rows + rank),
            transcendentals=0,
        ),
        name="partial_code",
    )(activations, basis)


def coded_total(keep, send, n_tensor):
    core = lax.axis_index("tensor") % 2
    total = keep + swap(send, "tensor", 1, n_tensor).astype(F32)
    bit = 2
    while bit < n_tensor:
        total = total + swap(total.astype(BF), "tensor", bit, n_tensor).astype(F32)
        bit *= 2
    mine = total.astype(BF)
    theirs = swap(mine, "tensor", 1, n_tensor)
    return jnp.where(
        core == 0,
        jnp.concatenate([mine, theirs], 0),
        jnp.concatenate([theirs, mine], 0),
    )


def line_total(grad_rows, coded, n_dp, cuts, spare=8):
    rows = grad_rows.shape[0] // n_dp
    d = lax.axis_index("dp")
    z, x = d // 2, d % 2
    first, second = cuts

    def both(block, code, cut):
        split = grad_rows.reshape(n_dp, rows, -1)
        part = lax.dynamic_slice_in_dim(split, block * 2, 2, 0)[:, cut[0] : cut[1]]
        return lax.dot_general(
            part, code, (((2,), (0,)), ((), ())), preferred_element_type=F32
        )

    def term(block, side, code, cut=(0, rows)):
        start = (block * 2 + side) * rows + cut[0]
        part = lax.dynamic_slice_in_dim(grad_rows, start, cut[1] - cut[0], 0)
        return jnp.dot(part, code, preferred_element_type=F32)

    def parity(value, side):
        return lax.dynamic_index_in_dim(value, side, 0, False).astype(F32)

    def hop(value, bit):
        full = [(i, i ^ (2 * bit)) for i in range(n_dp)]
        return lax.ppermute(value.astype(BF), "dp", full)

    def pair(value):
        return swap(value.astype(BF), "dp", 1, n_dp)

    def piece(value, cut):
        return value[cut[0] : cut[1]].astype(F32)

    def padded(value):
        return jnp.pad(value, ((0, rows - value.shape[0]), (0, 0)))

    got2 = pair(term(z ^ 2, 1 - x, coded))
    near1 = hop(both(z ^ 1, coded, (0, first[1] + spare)), 1)
    got3 = pair(term(z ^ 3, 1 - x, coded))

    sums = [(term(z ^ 2, x, coded, cut) + piece(got2, cut)).astype(BF) for cut in cuts]
    code, sums = lax.optimization_barrier((coded, sums))
    passed = [hop(part, 1) for part in sums]
    out1 = term(z ^ 1, 1 - x, code, second).astype(BF)
    code, out1, near1 = lax.optimization_barrier((code, out1, near1))
    got1 = pair(out1)
    near1 = near1[:, : first[1]]
    own_in = (term(z, 1 - x, code) + padded(parity(near1, 1 - x))).astype(BF)
    code, own_in = lax.optimization_barrier((coded, own_in))
    own = pair(own_in)
    far = []
    for cut, part in zip(cuts, passed):
        total = term(z ^ 3, x, code, cut) + piece(got3, cut) + part.astype(F32)
        code, total = lax.optimization_barrier((code, total.astype(BF)))
        far.append(hop(total, 3))
    late = hop(term(z ^ 1, x, code, second) + got1.astype(F32), 1)
    kept = [term(z, x, code, first) + parity(near1, x), term(z, x, code, second)]
    return kept, own, [(far[0],), (far[1], late)]


WIDE = 2048


def adam_update_kernel(cut, n_terms, n_olds, own, got, first, second, basis, *refs):
    terms, refs = refs[:n_terms], refs[n_terms + n_olds :]
    new_first, new_second, update = refs[:3]
    first_buf, second_buf, direction, blocks, moment_sem, block_sem = refs[3:]
    here = pl.ds(cut[0], cut[1] - cut[0])
    grad = own[...] + got[here, :].astype(F32)
    for term in terms:
        grad = grad + term[...].astype(F32)
    first_buf[...] = 0.9 * first[here, :] + 0.1 * grad
    second_buf[...] = 0.999 * second[here, :] + 0.001 * grad * grad
    moments = [
        pltpu.make_async_copy(first_buf, new_first.at[here, :], moment_sem.at[0]),
        pltpu.make_async_copy(second_buf, new_second.at[here, :], moment_sem.at[1]),
    ]
    for copy in moments:
        copy.start()
    first_hat = first_buf[...] / (1.0 - 0.9**STEP)
    second_hat = second_buf[...] / (1.0 - 0.999**STEP)
    direction[...] = (first_hat / (jnp.sqrt(second_hat) + 1e-08)).astype(BF)

    def out_copy(j):
        return pltpu.make_async_copy(
            blocks.at[j], update.at[here, pl.ds(j * WIDE, WIDE)], block_sem.at[j]
        )

    count = basis.shape[0] // WIDE
    for j in range(count):
        part = lax.dot_general(
            direction[...],
            basis[pl.ds(j * WIDE, WIDE), :],
            (((1,), (1,)), ((), ())),
            preferred_element_type=F32,
        )
        blocks[j] = part.astype(BF)
        out_copy(j).start()
    for j in range(count):
        out_copy(j).wait()
    for copy in moments:
        copy.wait()


def adam_update(cut, own, got, terms, first, second, basis, olds):
    rows, rank = first.shape
    feats = basis.shape[0]
    here = cut[1] - cut[0]
    vmem = pl.BlockSpec(memory_space=pltpu.VMEM)
    hbm = pl.BlockSpec(memory_space=pl.ANY)
    n_inputs = 5 + len(terms)
    return pl.pallas_call(
        functools.partial(adam_update_kernel, cut, len(terms), len(olds)),
        out_shape=(
            jax.ShapeDtypeStruct((rows, rank), F32),
            jax.ShapeDtypeStruct((rows, rank), F32),
            jax.ShapeDtypeStruct((rows, feats), BF),
        ),
        in_specs=[vmem] * n_inputs + [hbm] * len(olds),
        out_specs=(hbm, hbm, hbm),
        input_output_aliases={n_inputs + i: i for i in range(len(olds))},
        scratch_shapes=[
            pltpu.VMEM((here, rank), F32),
            pltpu.VMEM((here, rank), F32),
            pltpu.VMEM((here, rank), BF),
            pltpu.VMEM((feats // WIDE, here, WIDE), BF),
            pltpu.SemaphoreType.DMA((2,)),
            pltpu.SemaphoreType.DMA((feats // WIDE,)),
        ],
        compiler_params=pltpu.CompilerParams(vmem_limit_bytes=24 * 2**20),
        cost_estimate=pl.CostEstimate(
            flops=2 * here * rank * feats,
            bytes_accessed=2 * here * feats + 2 * rank * feats,
            transcendentals=here * rank,
        ),
        name="adam_update",
    )(own, got, first, second, basis, *terms, *olds)


def on_device(activations, basis, out_grad, first_moment, second_moment):
    n_tensor = lax.axis_size("tensor")
    n_dp = lax.axis_size("dp")
    keep, send = partial_code(activations, basis)
    coded_rows = coded_total(keep, send, n_tensor)
    if n_dp == 8:
        rows = first_moment.shape[1]
        middle = rows // 32 * 16
        cuts = ((0, middle), (middle, rows))
        kept, got, fars = line_total(out_grad.T, coded_rows, n_dp, cuts)
        outs = ()
        for cut, own, terms in zip(cuts, kept, fars):
            outs = adam_update(
                cut, own, got, terms, first_moment[0], second_moment[0], basis, outs
            )
        return tuple(out[None] for out in outs)
    term = jnp.dot(out_grad.T, coded_rows, preferred_element_type=F32)
    coded_grad = lax.psum_scatter(term, "dp", scatter_dimension=0, tiled=True)[None]
    new_first = 0.9 * first_moment + 0.1 * coded_grad
    new_second = 0.999 * second_moment + 0.001 * coded_grad * coded_grad
    first_hat = new_first / (1.0 - 0.9**STEP)
    second_hat = new_second / (1.0 - 0.999**STEP)
    direction = (first_hat / (jnp.sqrt(second_hat) + 1e-08)).astype(BF)
    update = lax.dot_general(
        direction[0], basis, (((1,), (1,)), ((), ())), preferred_element_type=F32
    )
    return (new_first, new_second, update.astype(BF)[None])


def solution(mesh):
    placed = (
        P("dp", "tensor"),
        P(),
        P("dp", "tensor"),
        P("tensor", "dp", None),
        P("tensor", "dp", None),
    )
    return jax.shard_map(
        on_device,
        mesh=mesh,
        in_specs=placed,
        out_specs=(P("tensor", "dp", None), P("tensor", "dp", None), P("tensor", "dp", None)),
        check_vma=False,
    )
```

time: 143 us -> 41.6 us (0.29)
  waiting for transfers between devices: 106 us -> 12.3 us
  starting transfers between devices: 0.08 us -> 17.1 us
  between operations: 14.1 us -> 0.95 us
  matrix products: 13.5 us -> 2.79 us
  Pallas kernels: 0 us -> 7.93 us
  blocking collectives: 5.59 us -> 0 us
  other arithmetic: 2.2 us -> 0.21 us
    reduce_scatter x2 -> x0, waiting for transfers between devices: 106 us -> none  [the longest x1 82.2 us: owner_total(): return lax.psum_scatter(term, 'dp', scatter_dimension=0, tiled=True)]
    ppermute x0 -> x13, starting transfers between devices: none -> 17.1 us  [the longest x6 9.34 us: hop(): return lax.ppermute(value.astype(BF), 'dp', full)]
    ppermute x0 -> x13, waiting for transfers between devices: none -> 12.3 us  [the longest x7 9.62 us: swap(): return lax.ppermute(value, axis, [(i, i ^ bit) for i in range(count)])]
    dot_general x3 -> x12, matrix products: 13.5 us -> 2.79 us  [the longest x11 2.51 us: term(): return jnp.dot(part, code, preferred_element_type=F32)]
    pallas_call x0 -> x3, Pallas kernels: none -> 7.93 us  [the longest x2 5.38 us: adam_update(): pl.pallas_call(functools.partial(adam_update_kernel, cut, len(terms), len...]
    all_gather x1 -> x0, blocking collectives: 5.59 us -> none  [gather_rows(): return lax.all_gather(coded_local, 'tensor', axis=0, tiled=True)]
  transfers between devices with their start and end apart: 2 -> 13, of which waited for: 2 -> 8; matrix products, arithmetic and copies ran while one was open for 0% -> 6% of each run, Pallas kernels for 0% -> 7%
where the time goes in v1:
time: 41.6 us; the launch traced here: 41.4 us
  starting transfers between devices  17.1 us (41%)
  waiting for transfers between devices  12.3 us (30%)
  Pallas kernels  7.93 us (19%)
  matrix products  2.79 us (7%)
  between operations  0.95 us (2%)
    ppermute x7, waiting for transfers between devices, swap(): return lax.ppermute(value, axis, [(i, i ^ bit) for i in range(count)])  9.62 us
    ppermute x6, starting transfers between devices, hop(): return lax.ppermute(value.astype(BF), 'dp', full)  9.34 us
    ppermute x7, starting transfers between devices, swap(): return lax.ppermute(value, axis, [(i, i ^ bit) for i in range(count)])  7.77 us
    pallas_call x2, Pallas kernels, adam_update(): pl.pallas_call(functools.partial(adam_update_kernel, cut, len(terms), len...  5.38 us
    ppermute x6, waiting for transfers between devices, hop(): return lax.ppermute(value.astype(BF), 'dp', full)  2.73 us
    pallas_call x1, Pallas kernels, partial_code(): pl.pallas_call(partial_code_kernel, out_shape=(jax.ShapeDtypeStruct((rows...  2.55 us
    dot_general x11, matrix products, term(): return jnp.dot(part, code, preferred_element_type=F32)  2.51 us
  transfers between devices with their start and end apart: 13, of which 8 were waited for; matrix products, arithmetic and copies ran while one was open for 6% of the time, Pallas kernels for 7%

profile of v1, /device:TPU:0, one launch (start us, length us, event | category | flops | bytes accessed | tf_op | source)
XLA Modules:
  0.0 41.4 jit_solution(11896040162027070992)
XLA Ops:
  0.6 2.5 %partial_code.1 = (f32[192,256]{1,0:T(8,128)S(1)}, bf16[192,256]{1,0:T(8,128)(2,1)S(1)}) custom-call(bf16[384,2048]{1,0:T(8,128)(2,1)} %activations.1, bf16[8192,256]{1,0:T(8,128)(2,1)} %basis.5), custom_call_target="tpu_custom_call" | custom-call | flops 402653184 | bytes 2621440 | tf_op jit(solution)/shard_map/partial_code/pallas_call | solution.py:58
  3.2 0.5 %collective-permute-start = (bf16[192,256]{1,0:T(8,128)(2,1)S(1)}, bf16[192,256]{1,0:T(8,128)(2,1)S(1)}, u32[]{:S(2)}, u32[]{:S(2)}) collective-permute-start(bf16[192,256]{1,0:T(8,128)(2,1)S(1)} %get-tuple-element.24), channel_id=1, source_target_pairs={{0,1},{1,0},{2,3},{3,2},{4,5},{5,4},{6,7},{7,6},{8,9},{9,8},{10,11... | collective-permute-start | bytes 294920 | tf_op jit(solution)/shard_map/ppermute | solution.py:16
  3.7 0.9 %collective-permute-done = bf16[192,256]{1,0:T(8,128)(2,1)S(1)} collective-permute-done((bf16[192,256]{1,0:T(8,128)(2,1)S(1)}, bf16[192,256]{1,0:T(8,128)(2,1)S(1)}, u32[]{:S(2)}, u32[]{:S(2)}) %collective-permute-start) | collective-permute-done | bytes 98336 | tf_op jit(solution)/shard_map/ppermute | solution.py:16
  4.7 2.9 %collective-permute-start.1 = (bf16[192,256]{1,0:T(8,128)(2,1)S(1)}, bf16[192,256]{1,0:T(8,128)(2,1)S(1)}, u32[]{:S(2)}, u32[]{:S(2)}) collective-permute-start(bf16[192,256]{1,0:T(8,128)(2,1)S(1)} %fusion.22), channel_id=1, source_target_pairs={{0,2},{1,3},{2,0},{3,1},{4,6},{5,7},{6,4},{7,5},{8,10},{9,11},{10,... | collective-permute-start | bytes 294920 | tf_op jit(solution)/shard_map/ppermute | solution.py:16
  7.6 3.1 %collective-permute-done.1 = bf16[192,256]{1,0:T(8,128)(2,1)S(1)} collective-permute-done((bf16[192,256]{1,0:T(8,128)(2,1)S(1)}, bf16[192,256]{1,0:T(8,128)(2,1)S(1)}, u32[]{:S(2)}, u32[]{:S(2)}) %collective-permute-start.1) | collective-permute-done | bytes 98336 | tf_op jit(solution)/shard_map/ppermute | solution.py:16
  11.0 1.2 %collective-permute-done.2 = bf16[192,256]{1,0:T(8,128)(2,1)S(1)} collective-permute-done((bf16[192,256]{1,0:T(8,128)(2,1)S(1)}, bf16[192,256]{1,0:T(8,128)(2,1)S(1)}, u32[]{:S(2)}, u32[]{:S(2)}) %collective-permute-start.2) | collective-permute-done | bytes 98336 | tf_op jit(solution)/shard_map/ppermute | solution.py:16
  12.2 0.3 convolution_convert_fusion.1
  12.5 0.3 convolution_convert_fusion.2
  12.8 1.8 %collective-permute-start.3 = (bf16[456,256]{1,0:T(8,128)(2,1)S(1)}, bf16[456,256]{1,0:T(8,128)(2,1)S(1)}, u32[]{:S(2)}, u32[]{:S(2)}) collective-permute-start(bf16[456,256]{1,0:T(8,128)(2,1)S(1)} %convolution_convert_fusion.2), channel_id=1, source_target_pairs={{0,4},{4,0},{8,12},{12,8},{16,20},{20,16},{24,28},{28,24},{1,5},{5... | collective-permute-start | bytes 700424 | tf_op jit(solution)/shard_map/ppermute | solution.py:16
  14.6 0.3 collective-permute-start.5
  14.9 0.3 convolution_convert_fusion
  15.1 1.9 %collective-permute-start.4 = (bf16[2,232,256]{2,1,0:T(8,128)(2,1)S(1)}, bf16[2,232,256]{2,1,0:T(8,128)(2,1)S(1)}, u32[]{:S(2)}, u32[]{:S(2)}) collective-permute-start(bf16[2,232,256]{2,1,0:T(8,128)(2,1)S(1)} %convolution_convert_fusion), channel_id=1, source_target_pairs={{0,8},{4,12},{8,0},{12,4},{16,24},{20,28},{24,16},{28,20},{1,9},{5... | collective-permute-start | bytes 712712 | tf_op jit(solution)/shard_map/ppermute | solution.py:121
  17.0 4.4 %collective-permute-done.3 = bf16[456,256]{1,0:T(8,128)(2,1)S(1)} collective-permute-done((bf16[456,256]{1,0:T(8,128)(2,1)S(1)}, bf16[456,256]{1,0:T(8,128)(2,1)S(1)}, u32[]{:S(2)}, u32[]{:S(2)}) %collective-permute-start.3) | collective-permute-done | bytes 233504 | tf_op jit(solution)/shard_map/ppermute | solution.py:16
  21.4 0.2 fusion.1
  21.6 0.2 fusion.2
  21.8 1.9 %collective-permute-start.6 = (bf16[224,256]{1,0:T(8,128)(2,1)S(1)}, bf16[224,256]{1,0:T(8,128)(2,1)S(1)}, u32[]{:S(2)}, u32[]{:S(2)}) collective-permute-start(bf16[224,256]{1,0:T(8,128)(2,1)S(1)} %fusion.2), channel_id=1, source_target_pairs={{0,8},{4,12},{8,0},{12,4},{16,24},{20,28},{24,16},{28,20},{1,9},{5... | collective-permute-start | bytes 344072 | tf_op jit(solution)/shard_map/ppermute | solution.py:121
  23.7 0.2 collective-permute-start.7
  23.9 0.2 convolution_convert_fusion.3
  24.1 1.8 %collective-permute-start.10 = (bf16[232,256]{1,0:T(8,128)(2,1)S(1)}, bf16[232,256]{1,0:T(8,128)(2,1)S(1)}, u32[]{:S(2)}, u32[]{:S(2)}) collective-permute-start(bf16[232,256]{1,0:T(8,128)(2,1)S(1)} %convolution_convert_fusion.3), channel_id=1, source_target_pairs={{0,4},{4,0},{8,12},{12,8},{16,20},{20,16},{24,28},{28,24},{1,5},{5... | collective-permute-start | bytes 356360 | tf_op jit(solution)/shard_map/ppermute | solution.py:16
  26.0 0.3 fusion
  26.3 0.4 collective-permute-start.8
  27.1 3.7 %collective-permute-start.12 = (bf16[224,256]{1,0:T(8,128)(2,1)S(1)}, bf16[224,256]{1,0:T(8,128)(2,1)S(1)}, u32[]{:S(2)}, u32[]{:S(2)}) collective-permute-start(bf16[224,256]{1,0:T(8,128)(2,1)S(1)} %add_convert_fusion.2), channel_id=1, source_target_pairs={{0,24},{4,28},{8,16},{12,20},{16,8},{20,12},{24,0},{28,4},{1,25},{... | collective-permute-start | bytes 344072 | tf_op jit(solution)/shard_map/ppermute | solution.py:121
  30.8 0.2 fusion.12
  31.1 0.9 %collective-permute-start.9 = (bf16[232,256]{1,0:T(8,128)(2,1)S(1)}, bf16[232,256]{1,0:T(8,128)(2,1)S(1)}, u32[]{:S(2)}, u32[]{:S(2)}) collective-permute-start(bf16[232,256]{1,0:T(8,128)(2,1)S(1)} %add_convert_fusion.1), channel_id=1, source_target_pairs={{0,24},{4,28},{8,16},{12,20},{16,8},{20,12},{24,0},{28,4},{1,25},{... | collective-permute-start | bytes 356360 | tf_op jit(solution)/shard_map/ppermute | solution.py:121
  32.0 0.2 fusion.16.own
  32.2 0.2 add_convert_fusion
  32.4 0.8 %collective-permute-start.11 = (bf16[232,256]{1,0:T(8,128)(2,1)S(1)}, bf16[232,256]{1,0:T(8,128)(2,1)S(1)}, u32[]{:S(2)}, u32[]{:S(2)}) collective-permute-start(bf16[232,256]{1,0:T(8,128)(2,1)S(1)} %add_convert_fusion), channel_id=1, source_target_pairs={{0,8},{4,12},{8,0},{12,4},{16,24},{20,28},{24,16},{28,20},{1,9},{5... | collective-permute-start | bytes 356360 | tf_op jit(solution)/shard_map/ppermute | solution.py:121
  33.4 0.9 %collective-permute-done.12.refs_0_ = bf16[224,256]{1,0:T(8,128)(2,1)S(1)} collective-permute-done((bf16[224,256]{1,0:T(8,128)(2,1)S(1)}, bf16[224,256]{1,0:T(8,128)(2,1)S(1)}, u32[]{:S(2)}, u32[]{:S(2)}) %collective-permute-start.12) | collective-permute-done | bytes 114720 | tf_op jit(solution)/shard_map/ppermute | solution.py:121
  34.4 2.7 %adam_update.2 = (f32[456,256]{1,0:T(8,128)}, f32[456,256]{1,0:T(8,128)}, bf16[456,8192]{1,0:T(8,128)(2,1)}) custom-call(f32[224,256]{1,0:T(8,128)S(1)} %convolution_add_fusion.2.own, bf16[456,256]{1,0:T(8,128)(2,1)S(1)} %collective-permute-done.8.got, f32[456,256]{1,0:T(8,128)S(1)} %bitcast.28, f32[456,256]{1,0:T(8,128)S(1)} %bitcast.30, ...), custom_call_target="tpu_custom_call" | custom-call | flops 939524096 | bytes 7864320 | tf_op jit(solution)/shard_map/adam_update/pallas_call | solution.py:207
  37.1 0.9 %collective-permute-done.9.refs_0_ = bf16[232,256]{1,0:T(8,128)(2,1)S(1)} collective-permute-done((bf16[232,256]{1,0:T(8,128)(2,1)S(1)}, bf16[232,256]{1,0:T(8,128)(2,1)S(1)}, u32[]{:S(2)}, u32[]{:S(2)}) %collective-permute-start.9) | collective-permute-done | bytes 118816 | tf_op jit(solution)/shard_map/ppermute | solution.py:121
  38.0 0.8 %collective-permute-done.11.refs_1_ = bf16[232,256]{1,0:T(8,128)(2,1)S(1)} collective-permute-done((bf16[232,256]{1,0:T(8,128)(2,1)S(1)}, bf16[232,256]{1,0:T(8,128)(2,1)S(1)}, u32[]{:S(2)}, u32[]{:S(2)}) %collective-permute-start.11) | collective-permute-done | bytes 118816 | tf_op jit(solution)/shard_map/ppermute | solution.py:121
  38.7 2.7 %adam_update.3 = (f32[456,256]{1,0:T(8,128)}, f32[456,256]{1,0:T(8,128)}, bf16[456,8192]{1,0:T(8,128)(2,1)}) custom-call(f32[232,256]{1,0:T(8,128)S(1)} %fusion.16.own, bf16[456,256]{1,0:T(8,128)(2,1)S(1)} %collective-permute-done.8.got, f32[456,256]{1,0:T(8,128)S(1)} %bitcast.29, ...), custom_call_target="tpu_custom_call", output_to_operand_aliasing={{0}: (7, {}), {1}: (8, {}), {2}: (9, {})} | custom-call | flops 973078528 | bytes 7995392 | tf_op jit(solution)/shard_map/adam_update/pallas_call | solution.py:207
  (24 shorter events, 0.9 us)
Async XLA Ops:
  0.6 11.6 %copy-start = (bf16[384,3648]{0,1:T(8,128)(2,1)S(1)}, bf16[384,3648]{0,1:T(8,128)(2,1)}, u32[]{:S(2)}) copy-start(bf16[384,3648]{0,1:T(8,128)(2,1)} %param.7) | copy-start | bytes 8404996
  3.2 1.5 %collective-permute-start = (bf16[192,256]{1,0:T(8,128)(2,1)S(1)}, bf16[192,256]{1,0:T(8,128)(2,1)S(1)}, u32[]{:S(2)}, u32[]{:S(2)}) collective-permute-start(bf16[192,256]{1,0:T(8,128)(2,1)S(1)} %get-tuple-element.24), channel_id=1, source_target_pairs={{0,1},{1,0},{2,3},{3,2},{4,5},{5,4},{6,7},{7,6},{8,9},{9,8},{10,11... | collective-permute-start | bytes 294920 | tf_op jit(solution)/shard_map/ppermute | solution.py:16
  4.7 6.0 %collective-permute-start.1 = (bf16[192,256]{1,0:T(8,128)(2,1)S(1)}, bf16[192,256]{1,0:T(8,128)(2,1)S(1)}, u32[]{:S(2)}, u32[]{:S(2)}) collective-permute-start(bf16[192,256]{1,0:T(8,128)(2,1)S(1)} %fusion.22), channel_id=1, source_target_pairs={{0,2},{1,3},{2,0},{3,1},{4,6},{5,7},{6,4},{7,5},{8,10},{9,11},{10,... | collective-permute-start | bytes 294920 | tf_op jit(solution)/shard_map/ppermute | solution.py:16
  10.8 1.4 %collective-permute-start.2 = (bf16[192,256]{1,0:T(8,128)(2,1)S(1)}, bf16[192,256]{1,0:T(8,128)(2,1)S(1)}, u32[]{:S(2)}, u32[]{:S(2)}) collective-permute-start(bf16[192,256]{1,0:T(8,128)(2,1)S(1)} %add_convert_fusion.3), channel_id=1, source_target_pairs={{0,1},{1,0},{2,3},{3,2},{4,5},{5,4},{6,7},{7,6},{8,9},{9,8},{10,11... | collective-permute-start | bytes 294920 | tf_op jit(solution)/shard_map/ppermute | solution.py:16
  12.8 8.6 %collective-permute-start.3 = (bf16[456,256]{1,0:T(8,128)(2,1)S(1)}, bf16[456,256]{1,0:T(8,128)(2,1)S(1)}, u32[]{:S(2)}, u32[]{:S(2)}) collective-permute-start(bf16[456,256]{1,0:T(8,128)(2,1)S(1)} %convolution_convert_fusion.2), channel_id=1, source_target_pairs={{0,4},{4,0},{8,12},{12,8},{16,20},{20,16},{24,28},{28,24},{1,5},{5... | collective-permute-start | bytes 700424 | tf_op jit(solution)/shard_map/ppermute | solution.py:16
  14.6 12.3 %collective-permute-start.5 = (bf16[456,256]{1,0:T(8,128)(2,1)S(1)}, bf16[456,256]{1,0:T(8,128)(2,1)S(1)}, u32[]{:S(2)}, u32[]{:S(2)}) collective-permute-start(bf16[456,256]{1,0:T(8,128)(2,1)S(1)} %convolution_convert_fusion.1), channel_id=1, source_target_pairs={{0,4},{4,0},{8,12},{12,8},{16,20},{20,16},{24,28},{28,24},{1,5},{5... | collective-permute-start | bytes 700424 | tf_op jit(solution)/shard_map/ppermute | solution.py:16
  15.1 9.0 %collective-permute-start.4 = (bf16[2,232,256]{2,1,0:T(8,128)(2,1)S(1)}, bf16[2,232,256]{2,1,0:T(8,128)(2,1)S(1)}, u32[]{:S(2)}, u32[]{:S(2)}) collective-permute-start(bf16[2,232,256]{2,1,0:T(8,128)(2,1)S(1)} %convolution_convert_fusion), channel_id=1, source_target_pairs={{0,8},{4,12},{8,0},{12,4},{16,24},{20,28},{24,16},{28,20},{1,9},{5... | collective-permute-start | bytes 712712 | tf_op jit(solution)/shard_map/ppermute | solution.py:121
  21.8 5.2 %collective-permute-start.6 = (bf16[224,256]{1,0:T(8,128)(2,1)S(1)}, bf16[224,256]{1,0:T(8,128)(2,1)S(1)}, u32[]{:S(2)}, u32[]{:S(2)}) collective-permute-start(bf16[224,256]{1,0:T(8,128)(2,1)S(1)} %fusion.2), channel_id=1, source_target_pairs={{0,8},{4,12},{8,0},{12,4},{16,24},{20,28},{24,16},{28,20},{1,9},{5... | collective-permute-start | bytes 344072 | tf_op jit(solution)/shard_map/ppermute | solution.py:121
  23.7 7.4 %collective-permute-start.7 = (bf16[232,256]{1,0:T(8,128)(2,1)S(1)}, bf16[232,256]{1,0:T(8,128)(2,1)S(1)}, u32[]{:S(2)}, u32[]{:S(2)}) collective-permute-start(bf16[232,256]{1,0:T(8,128)(2,1)S(1)} %fusion.1), channel_id=1, source_target_pairs={{0,8},{4,12},{8,0},{12,4},{16,24},{20,28},{24,16},{28,20},{1,9},{5... | collective-permute-start | bytes 356360 | tf_op jit(solution)/shard_map/ppermute | solution.py:121
  24.1 8.0 %collective-permute-start.10 = (bf16[232,256]{1,0:T(8,128)(2,1)S(1)}, bf16[232,256]{1,0:T(8,128)(2,1)S(1)}, u32[]{:S(2)}, u32[]{:S(2)}) collective-permute-start(bf16[232,256]{1,0:T(8,128)(2,1)S(1)} %convolution_convert_fusion.3), channel_id=1, source_target_pairs={{0,4},{4,0},{8,12},{12,8},{16,20},{20,16},{24,28},{28,24},{1,5},{5... | collective-permute-start | bytes 356360 | tf_op jit(solution)/shard_map/ppermute | solution.py:16
  25.9 8.4 %copy-start.1 = (bf16[8192,256]{1,0:T(8,128)(2,1)S(1)}, bf16[8192,256]{1,0:T(8,128)(2,1)}, u32[]{:S(2)}) copy-start(bf16[8192,256]{1,0:T(8,128)(2,1)} %basis.5) | copy-start | bytes 12582916
  26.0 8.4 %copy-start.2 = (f32[1,456,256]{2,1,0:T(8,128)S(1)}, f32[1,456,256]{2,1,0:T(8,128)}, u32[]{:S(2)}) copy-start(f32[1,456,256]{2,1,0:T(8,128)} %param.8) | copy-start | bytes 1400836
  26.0 8.4 %copy-start.3 = (f32[1,456,256]{2,1,0:T(8,128)S(1)}, f32[1,456,256]{2,1,0:T(8,128)}, u32[]{:S(2)}) copy-start(f32[1,456,256]{2,1,0:T(8,128)} %param.9) | copy-start | bytes 1400836
  26.3 8.1 %collective-permute-start.8 = (bf16[456,256]{1,0:T(8,128)(2,1)S(1)}, bf16[456,256]{1,0:T(8,128)(2,1)S(1)}, u32[]{:S(2)}, u32[]{:S(2)}) collective-permute-start(bf16[456,256]{1,0:T(8,128)(2,1)S(1)} %fusion), channel_id=1, source_target_pairs={{0,4},{4,0},{8,12},{12,8},{16,20},{20,16},{24,28},{28,24},{1,5},{5... | collective-permute-start | bytes 700424 | tf_op jit(solution)/shard_map/ppermute | solution.py:16
  27.1 7.3 %collective-permute-start.12 = (bf16[224,256]{1,0:T(8,128)(2,1)S(1)}, bf16[224,256]{1,0:T(8,128)(2,1)S(1)}, u32[]{:S(2)}, u32[]{:S(2)}) collective-permute-start(bf16[224,256]{1,0:T(8,128)(2,1)S(1)} %add_convert_fusion.2), channel_id=1, source_target_pairs={{0,24},{4,28},{8,16},{12,20},{16,8},{20,12},{24,0},{28,4},{1,25},{... | collective-permute-start | bytes 344072 | tf_op jit(solution)/shard_map/ppermute | solution.py:121
  31.1 6.9 %collective-permute-start.9 = (bf16[232,256]{1,0:T(8,128)(2,1)S(1)}, bf16[232,256]{1,0:T(8,128)(2,1)S(1)}, u32[]{:S(2)}, u32[]{:S(2)}) collective-permute-start(bf16[232,256]{1,0:T(8,128)(2,1)S(1)} %add_convert_fusion.1), channel_id=1, source_target_pairs={{0,24},{4,28},{8,16},{12,20},{16,8},{20,12},{24,0},{28,4},{1,25},{... | collective-permute-start | bytes 356360 | tf_op jit(solution)/shard_map/ppermute | solution.py:121
  32.4 6.3 %collective-permute-start.11 = (bf16[232,256]{1,0:T(8,128)(2,1)S(1)}, bf16[232,256]{1,0:T(8,128)(2,1)S(1)}, u32[]{:S(2)}, u32[]{:S(2)}) collective-permute-start(bf16[232,256]{1,0:T(8,128)(2,1)S(1)} %add_convert_fusion), channel_id=1, source_target_pairs={{0,8},{4,12},{8,0},{12,4},{16,24},{20,28},{24,16},{28,20},{1,9},{5... | collective-permute-start | bytes 356360 | tf_op jit(solution)/shard_map/ppermute | solution.py:121

commit v2 on v1

--- a/solution.py
+++ b/solution.py
@@ -130,8 +130,10 @@
         return jnp.pad(value, ((0, rows - value.shape[0]), (0, 0)))
 
     got2 = pair(term(z ^ 2, 1 - x, coded))
-    near1 = hop(both(z ^ 1, coded, (0, first[1] + spare)), 1)
-    got3 = pair(term(z ^ 3, 1 - x, coded))
+    out1 = both(z ^ 1, coded, (0, first[1] + spare)).astype(BF)
+    code, out1 = lax.optimization_barrier((coded, out1))
+    near1 = hop(out1, 1)
+    got3 = pair(term(z ^ 3, 1 - x, code))
 
     sums = [(term(z ^ 2, x, coded, cut) + piece(got2, cut)).astype(BF) for cut in cuts]
     code, sums = lax.optimization_barrier((coded, sums))
@@ -143,17 +145,22 @@
     own_in = (term(z, 1 - x, code) + padded(parity(near1, 1 - x))).astype(BF)
     code, own_in = lax.optimization_barrier((coded, own_in))
     own = pair(own_in)
-    far = []
-    for cut, part in zip(cuts, passed):
-        total = term(z ^ 3, x, code, cut) + piece(got3, cut) + part.astype(F32)
-        code, total = lax.optimization_barrier((code, total.astype(BF)))
-        far.append(hop(total, 3))
-    late = hop(term(z ^ 1, x, code, second) + got1.astype(F32), 1)
+    def total(cut, part, code):
+        value = term(z ^ 3, x, code, cut) + piece(got3, cut) + part.astype(F32)
+        return lax.optimization_barrier((code, value.astype(BF)))
+
+    code, total_a = total(first, passed[0], code)
+    far_a = hop(total_a, 3)
+    late = (term(z ^ 1, x, code, second) + got1.astype(F32)).astype(BF)
+    code, late = lax.optimization_barrier((code, late))
+    late = hop(late, 1)
+    code, total_b = total(second, passed[1], code)
+    far_b = hop(total_b, 3)
     kept = [term(z, x, code, first) + parity(near1, x), term(z, x, code, second)]
-    return kept, own, [(far[0],), (far[1], late)]
-
-
-WIDE = 2048
+    return kept, own, [(far_a,), (late, far_b)]
+
+
+WIDE = 512
 
 
 def adam_update_kernel(cut, n_terms, n_olds, own, got, first, second, basis, *refs):

time: 41.6 us -> 42.2 us (1.014)
  starting transfers between devices: 17.1 us -> 19.4 us
  waiting for transfers between devices: 12.3 us -> 10.9 us
    ppermute x6, starting transfers between devices: 9.34 us -> 11.6 us  [hop(): return lax.ppermute(value.astype(BF), 'dp', full)]
    ppermute x6, waiting for transfers between devices: 2.73 us -> 1.32 us  [hop(): return lax.ppermute(value.astype(BF), 'dp', full)]
  transfers between devices with their start and end apart: 13 -> 13, of which waited for: 8 -> 6; matrix products, arithmetic and copies ran while one was open for 6% -> 6% of each run, Pallas kernels for 7% -> 6%
where the time goes in v2:
time: 42.2 us; the launch traced here: 42 us
  starting transfers between devices  19.4 us (46%)
  waiting for transfers between devices  10.9 us (26%)
  Pallas kernels  7.65 us (18%)
  matrix products  2.79 us (7%)
  between operations  0.98 us (2%)
    ppermute x6, starting transfers between devices, hop(): return lax.ppermute(value.astype(BF), 'dp', full)  11.6 us
    ppermute x7, waiting for transfers between devices, swap(): return lax.ppermute(value, axis, [(i, i ^ bit) for i in range(count)])  9.61 us
    ppermute x7, starting transfers between devices, swap(): return lax.ppermute(value, axis, [(i, i ^ bit) for i in range(count)])  7.84 us
    pallas_call x2, Pallas kernels, adam_update(): pl.pallas_call(functools.partial(adam_update_kernel, cut, len(terms), len...  5.1 us
    pallas_call x1, Pallas kernels, partial_code(): pl.pallas_call(partial_code_kernel, out_shape=(jax.ShapeDtypeStruct((rows...  2.55 us
    dot_general x11, matrix products, term(): return jnp.dot(part, code, preferred_element_type=F32)  2.52 us
    ppermute x6, waiting for transfers between devices, hop(): return lax.ppermute(value.astype(BF), 'dp', full)  1.32 us
  transfers between devices with their start and end apart: 13, of which 6 were waited for; matrix products, arithmetic and copies ran while one was open for 6% of the time, Pallas kernels for 6%

profile of v2, /device:TPU:0, one launch (start us, length us, event | category | flops | bytes accessed | tf_op | source)
XLA Modules:
  0.0 42.0 jit_solution(17987088706138061474)
XLA Ops:
  0.6 2.5 %partial_code.1 = (f32[192,256]{1,0:T(8,128)S(1)}, bf16[192,256]{1,0:T(8,128)(2,1)S(1)}) custom-call(bf16[384,2048]{1,0:T(8,128)(2,1)} %activations.1, bf16[8192,256]{1,0:T(8,128)(2,1)} %basis.5), custom_call_target="tpu_custom_call" | custom-call | flops 402653184 | bytes 2621440 | tf_op jit(solution)/shard_map/partial_code/pallas_call | solution.py:58
  3.2 0.5 %collective-permute-start = (bf16[192,256]{1,0:T(8,128)(2,1)S(1)}, bf16[192,256]{1,0:T(8,128)(2,1)S(1)}, u32[]{:S(2)}, u32[]{:S(2)}) collective-permute-start(bf16[192,256]{1,0:T(8,128)(2,1)S(1)} %get-tuple-element.28), channel_id=1, source_target_pairs={{0,1},{1,0},{2,3},{3,2},{4,5},{5,4},{6,7},{7,6},{8,9},{9,8},{10,11... | collective-permute-start | bytes 294920 | tf_op jit(solution)/shard_map/ppermute | solution.py:16
  3.7 0.9 %collective-permute-done = bf16[192,256]{1,0:T(8,128)(2,1)S(1)} collective-permute-done((bf16[192,256]{1,0:T(8,128)(2,1)S(1)}, bf16[192,256]{1,0:T(8,128)(2,1)S(1)}, u32[]{:S(2)}, u32[]{:S(2)}) %collective-permute-start) | collective-permute-done | bytes 98336 | tf_op jit(solution)/shard_map/ppermute | solution.py:16
  4.7 2.9 %collective-permute-start.1 = (bf16[192,256]{1,0:T(8,128)(2,1)S(1)}, bf16[192,256]{1,0:T(8,128)(2,1)S(1)}, u32[]{:S(2)}, u32[]{:S(2)}) collective-permute-start(bf16[192,256]{1,0:T(8,128)(2,1)S(1)} %fusion.22), channel_id=1, source_target_pairs={{0,2},{1,3},{2,0},{3,1},{4,6},{5,7},{6,4},{7,5},{8,10},{9,11},{10,... | collective-permute-start | bytes 294920 | tf_op jit(solution)/shard_map/ppermute | solution.py:16
  7.6 3.1 %collective-permute-done.1 = bf16[192,256]{1,0:T(8,128)(2,1)S(1)} collective-permute-done((bf16[192,256]{1,0:T(8,128)(2,1)S(1)}, bf16[192,256]{1,0:T(8,128)(2,1)S(1)}, u32[]{:S(2)}, u32[]{:S(2)}) %collective-permute-start.1) | collective-permute-done | bytes 98336 | tf_op jit(solution)/shard_map/ppermute | solution.py:16
  11.0 1.2 %collective-permute-done.2 = bf16[192,256]{1,0:T(8,128)(2,1)S(1)} collective-permute-done((bf16[192,256]{1,0:T(8,128)(2,1)S(1)}, bf16[192,256]{1,0:T(8,128)(2,1)S(1)}, u32[]{:S(2)}, u32[]{:S(2)}) %collective-permute-start.2) | collective-permute-done | bytes 98336 | tf_op jit(solution)/shard_map/ppermute | solution.py:16
  12.2 0.3 convolution_convert_fusion.2
  12.5 0.3 convolution_convert_fusion
  12.8 1.8 %collective-permute-start.3 = (bf16[456,256]{1,0:T(8,128)(2,1)S(1)}, bf16[456,256]{1,0:T(8,128)(2,1)S(1)}, u32[]{:S(2)}, u32[]{:S(2)}) collective-permute-start(bf16[456,256]{1,0:T(8,128)(2,1)S(1)} %convolution_convert_fusion.2), channel_id=1, source_target_pairs={{0,4},{4,0},{8,12},{12,8},{16,20},{20,16},{24,28},{28,24},{1,5},{5... | collective-permute-start | bytes 700424 | tf_op jit(solution)/shard_map/ppermute | solution.py:16
  14.6 0.3 convolution_convert_fusion.1
  14.8 0.4 collective-permute-start.5
  15.2 1.8 %collective-permute-start.4 = (bf16[2,232,256]{2,1,0:T(8,128)(2,1)S(1)}, bf16[2,232,256]{2,1,0:T(8,128)(2,1)S(1)}, u32[]{:S(2)}, u32[]{:S(2)}) collective-permute-start(bf16[2,232,256]{2,1,0:T(8,128)(2,1)S(1)} %convolution_convert_fusion), channel_id=1, source_target_pairs={{0,8},{4,12},{8,0},{12,4},{16,24},{20,28},{24,16},{28,20},{1,9},{5... | collective-permute-start | bytes 712712 | tf_op jit(solution)/shard_map/ppermute | solution.py:121
  17.0 4.4 %collective-permute-done.3 = bf16[456,256]{1,0:T(8,128)(2,1)S(1)} collective-permute-done((bf16[456,256]{1,0:T(8,128)(2,1)S(1)}, bf16[456,256]{1,0:T(8,128)(2,1)S(1)}, u32[]{:S(2)}, u32[]{:S(2)}) %collective-permute-start.3) | collective-permute-done | bytes 233504 | tf_op jit(solution)/shard_map/ppermute | solution.py:16
  21.4 0.2 fusion.1
  21.6 0.2 fusion.2
  21.8 1.9 %collective-permute-start.6 = (bf16[224,256]{1,0:T(8,128)(2,1)S(1)}, bf16[224,256]{1,0:T(8,128)(2,1)S(1)}, u32[]{:S(2)}, u32[]{:S(2)}) collective-permute-start(bf16[224,256]{1,0:T(8,128)(2,1)S(1)} %fusion.2), channel_id=1, source_target_pairs={{0,8},{4,12},{8,0},{12,4},{16,24},{20,28},{24,16},{28,20},{1,9},{5... | collective-permute-start | bytes 344072 | tf_op jit(solution)/shard_map/ppermute | solution.py:121
  23.7 0.2 collective-permute-start.8
  23.9 0.2 convolution_convert_fusion.3
  24.1 1.8 %collective-permute-start.7 = (bf16[232,256]{1,0:T(8,128)(2,1)S(1)}, bf16[232,256]{1,0:T(8,128)(2,1)S(1)}, u32[]{:S(2)}, u32[]{:S(2)}) collective-permute-start(bf16[232,256]{1,0:T(8,128)(2,1)S(1)} %convolution_convert_fusion.3), channel_id=1, source_target_pairs={{0,4},{4,0},{8,12},{12,8},{16,20},{20,16},{24,28},{28,24},{1,5},{5... | collective-permute-start | bytes 356360 | tf_op jit(solution)/shard_map/ppermute | solution.py:16
  26.0 0.3 fusion
  26.3 0.4 collective-permute-start.9
  26.7 0.2 fusion.19
  27.1 3.7 %collective-permute-start.12 = (bf16[224,256]{1,0:T(8,128)(2,1)S(1)}, bf16[224,256]{1,0:T(8,128)(2,1)S(1)}, u32[]{:S(2)}, u32[]{:S(2)}) collective-permute-start(bf16[224,256]{1,0:T(8,128)(2,1)S(1)} %add_convert_fusion.2), channel_id=1, source_target_pairs={{0,24},{4,28},{8,16},{12,20},{16,8},{20,12},{24,0},{28,4},{1,25},{... | collective-permute-start | bytes 344072 | tf_op jit(solution)/shard_map/ppermute | solution.py:121
  30.8 0.2 add_convert_fusion.1
  31.1 1.4 %collective-permute-start.10 = (bf16[232,256]{1,0:T(8,128)(2,1)S(1)}, bf16[232,256]{1,0:T(8,128)(2,1)S(1)}, u32[]{:S(2)}, u32[]{:S(2)}) collective-permute-start(bf16[232,256]{1,0:T(8,128)(2,1)S(1)} %add_convert_fusion.1), channel_id=1, source_target_pairs={{0,8},{4,12},{8,0},{12,4},{16,24},{20,28},{24,16},{28,20},{1,9},{5... | collective-permute-start | bytes 356360 | tf_op jit(solution)/shard_map/ppermute | solution.py:121
  32.5 0.2 fusion.8
  32.7 2.5 %collective-permute-start.11 = (bf16[232,256]{1,0:T(8,128)(2,1)S(1)}, bf16[232,256]{1,0:T(8,128)(2,1)S(1)}, u32[]{:S(2)}, u32[]{:S(2)}) collective-permute-start(bf16[232,256]{1,0:T(8,128)(2,1)S(1)} %add_convert_fusion), channel_id=1, source_target_pairs={{0,24},{4,28},{8,16},{12,20},{16,8},{20,12},{24,0},{28,4},{1,25},{... | collective-permute-start | bytes 356360 | tf_op jit(solution)/shard_map/ppermute | solution.py:121
  35.3 0.2 fusion.16.own
  35.5 0.2 convolution_add_fusion.2.own
  35.8 2.5 %adam_update.2 = (f32[456,256]{1,0:T(8,128)}, f32[456,256]{1,0:T(8,128)}, bf16[456,8192]{1,0:T(8,128)(2,1)}) custom-call(f32[224,256]{1,0:T(8,128)S(1)} %convolution_add_fusion.2.own, bf16[456,256]{1,0:T(8,128)(2,1)S(1)} %collective-permute-done.9.got, f32[456,256]{1,0:T(8,128)S(1)} %bitcast.28, f32[456,256]{1,0:T(8,128)S(1)} %bitcast.30, ...), custom_call_target="tpu_custom_call" | custom-call | flops 939524096 | bytes 7864320 | tf_op jit(solution)/shard_map/adam_update/pallas_call | solution.py:214
  38.3 1.2 %collective-permute-done.11.refs_1_ = bf16[232,256]{1,0:T(8,128)(2,1)S(1)} collective-permute-done((bf16[232,256]{1,0:T(8,128)(2,1)S(1)}, bf16[232,256]{1,0:T(8,128)(2,1)S(1)}, u32[]{:S(2)}, u32[]{:S(2)}) %collective-permute-start.11) | collective-permute-done | bytes 118816 | tf_op jit(solution)/shard_map/ppermute | solution.py:121
  39.5 2.6 %adam_update.3 = (f32[456,256]{1,0:T(8,128)}, f32[456,256]{1,0:T(8,128)}, bf16[456,8192]{1,0:T(8,128)(2,1)}) custom-call(f32[232,256]{1,0:T(8,128)S(1)} %fusion.16.own, bf16[456,256]{1,0:T(8,128)(2,1)S(1)} %collective-permute-done.9.got, f32[456,256]{1,0:T(8,128)S(1)} %bitcast.29, ...), custom_call_target="tpu_custom_call", output_to_operand_aliasing={{0}: (7, {}), {1}: (8, {}), {2}: (9, {})} | custom-call | flops 973078528 | bytes 7995392 | tf_op jit(solution)/shard_map/adam_update/pallas_call | solution.py:214
  (24 shorter events, 0.5 us)
Async XLA Ops:
  0.6 11.6 %copy-start = (bf16[384,3648]{0,1:T(8,128)(2,1)S(1)}, bf16[384,3648]{0,1:T(8,128)(2,1)}, u32[]{:S(2)}) copy-start(bf16[384,3648]{0,1:T(8,128)(2,1)} %param.7) | copy-start | bytes 8404996
  3.2 1.5 %collective-permute-start = (bf16[192,256]{1,0:T(8,128)(2,1)S(1)}, bf16[192,256]{1,0:T(8,128)(2,1)S(1)}, u32[]{:S(2)}, u32[]{:S(2)}) collective-permute-start(bf16[192,256]{1,0:T(8,128)(2,1)S(1)} %get-tuple-element.28), channel_id=1, source_target_pairs={{0,1},{1,0},{2,3},{3,2},{4,5},{5,4},{6,7},{7,6},{8,9},{9,8},{10,11... | collective-permute-start | bytes 294920 | tf_op jit(solution)/shard_map/ppermute | solution.py:16
  4.7 6.0 %collective-permute-start.1 = (bf16[192,256]{1,0:T(8,128)(2,1)S(1)}, bf16[192,256]{1,0:T(8,128)(2,1)S(1)}, u32[]{:S(2)}, u32[]{:S(2)}) collective-permute-start(bf16[192,256]{1,0:T(8,128)(2,1)S(1)} %fusion.22), channel_id=1, source_target_pairs={{0,2},{1,3},{2,0},{3,1},{4,6},{5,7},{6,4},{7,5},{8,10},{9,11},{10,... | collective-permute-start | bytes 294920 | tf_op jit(solution)/shard_map/ppermute | solution.py:16
  10.8 1.4 %collective-permute-start.2 = (bf16[192,256]{1,0:T(8,128)(2,1)S(1)}, bf16[192,256]{1,0:T(8,128)(2,1)S(1)}, u32[]{:S(2)}, u32[]{:S(2)}) collective-permute-start(bf16[192,256]{1,0:T(8,128)(2,1)S(1)} %add_convert_fusion.3), channel_id=1, source_target_pairs={{0,1},{1,0},{2,3},{3,2},{4,5},{5,4},{6,7},{7,6},{8,9},{9,8},{10,11... | collective-permute-start | bytes 294920 | tf_op jit(solution)/shard_map/ppermute | solution.py:16
  12.8 8.6 %collective-permute-start.3 = (bf16[456,256]{1,0:T(8,128)(2,1)S(1)}, bf16[456,256]{1,0:T(8,128)(2,1)S(1)}, u32[]{:S(2)}, u32[]{:S(2)}) collective-permute-start(bf16[456,256]{1,0:T(8,128)(2,1)S(1)} %convolution_convert_fusion.2), channel_id=1, source_target_pairs={{0,4},{4,0},{8,12},{12,8},{16,20},{20,16},{24,28},{28,24},{1,5},{5... | collective-permute-start | bytes 700424 | tf_op jit(solution)/shard_map/ppermute | solution.py:16
  14.8 12.0 %collective-permute-start.5 = (bf16[456,256]{1,0:T(8,128)(2,1)S(1)}, bf16[456,256]{1,0:T(8,128)(2,1)S(1)}, u32[]{:S(2)}, u32[]{:S(2)}) collective-permute-start(bf16[456,256]{1,0:T(8,128)(2,1)S(1)} %convolution_convert_fusion.1), channel_id=1, source_target_pairs={{0,4},{4,0},{8,12},{12,8},{16,20},{20,16},{24,28},{28,24},{1,5},{5... | collective-permute-start | bytes 700424 | tf_op jit(solution)/shard_map/ppermute | solution.py:16
  15.2 8.9 %collective-permute-start.4 = (bf16[2,232,256]{2,1,0:T(8,128)(2,1)S(1)}, bf16[2,232,256]{2,1,0:T(8,128)(2,1)S(1)}, u32[]{:S(2)}, u32[]{:S(2)}) collective-permute-start(bf16[2,232,256]{2,1,0:T(8,128)(2,1)S(1)} %convolution_convert_fusion), channel_id=1, source_target_pairs={{0,8},{4,12},{8,0},{12,4},{16,24},{20,28},{24,16},{28,20},{1,9},{5... | collective-permute-start | bytes 712712 | tf_op jit(solution)/shard_map/ppermute | solution.py:121
  21.8 5.2 %collective-permute-start.6 = (bf16[224,256]{1,0:T(8,128)(2,1)S(1)}, bf16[224,256]{1,0:T(8,128)(2,1)S(1)}, u32[]{:S(2)}, u32[]{:S(2)}) collective-permute-start(bf16[224,256]{1,0:T(8,128)(2,1)S(1)} %fusion.2), channel_id=1, source_target_pairs={{0,8},{4,12},{8,0},{12,4},{16,24},{20,28},{24,16},{28,20},{1,9},{5... | collective-permute-start | bytes 344072 | tf_op jit(solution)/shard_map/ppermute | solution.py:121
  23.7 9.0 %collective-permute-start.8 = (bf16[232,256]{1,0:T(8,128)(2,1)S(1)}, bf16[232,256]{1,0:T(8,128)(2,1)S(1)}, u32[]{:S(2)}, u32[]{:S(2)}) collective-permute-start(bf16[232,256]{1,0:T(8,128)(2,1)S(1)} %fusion.1), channel_id=1, source_target_pairs={{0,8},{4,12},{8,0},{12,4},{16,24},{20,28},{24,16},{28,20},{1,9},{5... | collective-permute-start | bytes 356360 | tf_op jit(solution)/shard_map/ppermute | solution.py:121
  24.1 6.7 %collective-permute-start.7 = (bf16[232,256]{1,0:T(8,128)(2,1)S(1)}, bf16[232,256]{1,0:T(8,128)(2,1)S(1)}, u32[]{:S(2)}, u32[]{:S(2)}) collective-permute-start(bf16[232,256]{1,0:T(8,128)(2,1)S(1)} %convolution_convert_fusion.3), channel_id=1, source_target_pairs={{0,4},{4,0},{8,12},{12,8},{16,20},{20,16},{24,28},{28,24},{1,5},{5... | collective-permute-start | bytes 356360 | tf_op jit(solution)/shard_map/ppermute | solution.py:16
  25.9 9.8 %copy-start.1 = (bf16[8192,256]{1,0:T(8,128)(2,1)S(1)}, bf16[8192,256]{1,0:T(8,128)(2,1)}, u32[]{:S(2)}) copy-start(bf16[8192,256]{1,0:T(8,128)(2,1)} %basis.5) | copy-start | bytes 12582916
  26.0 9.8 %copy-start.2 = (f32[1,456,256]{2,1,0:T(8,128)S(1)}, f32[1,456,256]{2,1,0:T(8,128)}, u32[]{:S(2)}) copy-start(f32[1,456,256]{2,1,0:T(8,128)} %param.8) | copy-start | bytes 1400836
  26.0 9.8 %copy-start.3 = (f32[1,456,256]{2,1,0:T(8,128)S(1)}, f32[1,456,256]{2,1,0:T(8,128)}, u32[]{:S(2)}) copy-start(f32[1,456,256]{2,1,0:T(8,128)} %param.9) | copy-start | bytes 1400836
  26.3 9.4 %collective-permute-start.9 = (bf16[456,256]{1,0:T(8,128)(2,1)S(1)}, bf16[456,256]{1,0:T(8,128)(2,1)S(1)}, u32[]{:S(2)}, u32[]{:S(2)}) collective-permute-start(bf16[456,256]{1,0:T(8,128)(2,1)S(1)} %fusion), channel_id=1, source_target_pairs={{0,4},{4,0},{8,12},{12,8},{16,20},{20,16},{24,28},{28,24},{1,5},{5... | collective-permute-start | bytes 700424 | tf_op jit(solution)/shard_map/ppermute | solution.py:16
  27.1 8.6 %collective-permute-start.12 = (bf16[224,256]{1,0:T(8,128)(2,1)S(1)}, bf16[224,256]{1,0:T(8,128)(2,1)S(1)}, u32[]{:S(2)}, u32[]{:S(2)}) collective-permute-start(bf16[224,256]{1,0:T(8,128)(2,1)S(1)} %add_convert_fusion.2), channel_id=1, source_target_pairs={{0,24},{4,28},{8,16},{12,20},{16,8},{20,12},{24,0},{28,4},{1,25},{... | collective-permute-start | bytes 344072 | tf_op jit(solution)/shard_map/ppermute | solution.py:121
  31.1 7.3 %collective-permute-start.10 = (bf16[232,256]{1,0:T(8,128)(2,1)S(1)}, bf16[232,256]{1,0:T(8,128)(2,1)S(1)}, u32[]{:S(2)}, u32[]{:S(2)}) collective-permute-start(bf16[232,256]{1,0:T(8,128)(2,1)S(1)} %add_convert_fusion.1), channel_id=1, source_target_pairs={{0,8},{4,12},{8,0},{12,4},{16,24},{20,28},{24,16},{28,20},{1,9},{5... | collective-permute-start | bytes 356360 | tf_op jit(solution)/shard_map/ppermute | solution.py:121
  32.7 6.7 %collective-permute-start.11 = (bf16[232,256]{1,0:T(8,128)(2,1)S(1)}, bf16[232,256]{1,0:T(8,128)(2,1)S(1)}, u32[]{:S(2)}, u32[]{:S(2)}) collective-permute-start(bf16[232,256]{1,0:T(8,128)(2,1)S(1)} %add_convert_fusion), channel_id=1, source_target_pairs={{0,24},{4,28},{8,16},{12,20},{16,8},{20,12},{24,0},{28,4},{1,25},{... | collective-permute-start | bytes 356360 | tf_op jit(solution)/shard_map/ppermute | solution.py:121

commit v3 on v2

--- a/solution.py
+++ b/solution.py
@@ -77,6 +77,41 @@
         ),
         name="partial_code",
     )(activations, basis)
+
+
+PARTS = 8
+
+
+def transposed_kernel(source, target, parts, sems):
+    rows = parts.shape[1]
+    copies = [
+        pltpu.make_async_copy(source.at[pl.ds(k * rows, rows), :], parts.at[k], sems.at[k])
+        for k in range(PARTS)
+    ]
+    for copy in copies:
+        copy.start()
+    for k in range(PARTS):
+        copies[k].wait()
+        target[:, pl.ds(k * rows, rows)] = parts[k].T
+
+
+def transposed(array):
+    rows, cols = array.shape
+    return pl.pallas_call(
+        transposed_kernel,
+        out_shape=jax.ShapeDtypeStruct((cols, rows), array.dtype),
+        in_specs=[pl.BlockSpec(memory_space=pltpu.HBM)],
+        out_specs=pl.BlockSpec(memory_space=pltpu.VMEM),
+        scratch_shapes=[
+            pltpu.VMEM((PARTS, rows // PARTS, cols), array.dtype),
+            pltpu.SemaphoreType.DMA((PARTS,)),
+        ],
+        compiler_params=pltpu.CompilerParams(vmem_limit_bytes=48 * 2**20),
+        cost_estimate=pl.CostEstimate(
+            flops=0, bytes_accessed=4 * array.size, transcendentals=0
+        ),
+        name="transposed",
+    )(array)
 
 
 def coded_total(keep, send, n_tensor):
@@ -95,7 +130,7 @@
     )
 
 
-def line_total(grad_rows, coded, n_dp, cuts, spare=8):
+def line_total(grad_rows, coded, basis, n_dp, cuts, spare=8):
     rows = grad_rows.shape[0] // n_dp
     d = lax.axis_index("dp")
     z, x = d // 2, d % 2
@@ -133,7 +168,11 @@
     out1 = both(z ^ 1, coded, (0, first[1] + spare)).astype(BF)
     code, out1 = lax.optimization_barrier((coded, out1))
     near1 = hop(out1, 1)
-    got3 = pair(term(z ^ 3, 1 - x, code))
+    out3 = term(z ^ 3, 1 - x, code).astype(BF)
+    out3, basis = lax.optimization_barrier((out3, basis))
+    got3 = pair(out3)
+    basis_t = transposed(basis)
+    coded, basis_t = lax.optimization_barrier((coded, basis_t))
 
     sums = [(term(z ^ 2, x, coded, cut) + piece(got2, cut)).astype(BF) for cut in cuts]
     code, sums = lax.optimization_barrier((coded, sums))
@@ -151,19 +190,17 @@
 
     code, total_a = total(first, passed[0], code)
     far_a = hop(total_a, 3)
-    late = (term(z ^ 1, x, code, second) + got1.astype(F32)).astype(BF)
-    code, late = lax.optimization_barrier((code, late))
-    late = hop(late, 1)
     code, total_b = total(second, passed[1], code)
     far_b = hop(total_b, 3)
+    late = hop(term(z ^ 1, x, code, second) + got1.astype(F32), 1)
     kept = [term(z, x, code, first) + parity(near1, x), term(z, x, code, second)]
-    return kept, own, [(far_a,), (late, far_b)]
+    return kept, own, [(far_a,), (far_b, late)], basis_t
 
 
 WIDE = 512
 
 
-def adam_update_kernel(cut, n_terms, n_olds, own, got, first, second, basis, *refs):
+def adam_update_kernel(cut, n_terms, n_olds, own, got, first, second, basis_t, *refs):
     terms, refs = refs[:n_terms], refs[n_terms + n_olds :]
     new_first, new_second, update = refs[:3]
     first_buf, second_buf, direction, blocks, moment_sem, block_sem = refs[3:]
@@ -188,12 +225,11 @@
             blocks.at[j], update.at[here, pl.ds(j * WIDE, WIDE)], block_sem.at[j]
         )
 
-    count = basis.shape[0] // WIDE
+    count = basis_t.shape[1] // WIDE
     for j in range(count):
-        part = lax.dot_general(
+        part = jnp.dot(
             direction[...],
-            basis[pl.ds(j * WIDE, WIDE), :],
-            (((1,), (1,)), ((), ())),
+            basis_t[:, pl.ds(j * WIDE, WIDE)],
             preferred_element_type=F32,
         )
         blocks[j] = part.astype(BF)
@@ -204,9 +240,9 @@
         copy.wait()
 
 
-def adam_update(cut, own, got, terms, first, second, basis, olds):
+def adam_update(cut, own, got, terms, first, second, basis_t, olds):
     rows, rank = first.shape
-    feats = basis.shape[0]
+    feats = basis_t.shape[1]
     here = cut[1] - cut[0]
     vmem = pl.BlockSpec(memory_space=pltpu.VMEM)
     hbm = pl.BlockSpec(memory_space=pl.ANY)
@@ -236,7 +272,7 @@
             transcendentals=here * rank,
         ),
         name="adam_update",
-    )(own, got, first, second, basis, *terms, *olds)
+    )(own, got, first, second, basis_t, *terms, *olds)
 
 
 def on_device(activations, basis, out_grad, first_moment, second_moment):
@@ -244,18 +280,19 @@
     n_dp = lax.axis_size("dp")
     keep, send = partial_code(activations, basis)
     coded_rows = coded_total(keep, send, n_tensor)
+    grad_rows = out_grad.T
     if n_dp == 8:
         rows = first_moment.shape[1]
         middle = rows // 32 * 16
         cuts = ((0, middle), (middle, rows))
-        kept, got, fars = line_total(out_grad.T, coded_rows, n_dp, cuts)
+        kept, got, fars, basis_t = line_total(grad_rows, coded_rows, basis, n_dp, cuts)
         outs = ()
         for cut, own, terms in zip(cuts, kept, fars):
             outs = adam_update(
-                cut, own, got, terms, first_moment[0], second_moment[0], basis, outs
+                cut, own, got, terms, first_moment[0], second_moment[0], basis_t, outs
             )
         return tuple(out[None] for out in outs)
-    term = jnp.dot(out_grad.T, coded_rows, preferred_element_type=F32)
+    term = jnp.dot(grad_rows, coded_rows, preferred_element_type=F32)
     coded_grad = lax.psum_scatter(term, "dp", scatter_dimension=0, tiled=True)[None]
     new_first = 0.9 * first_moment + 0.1 * coded_grad
     new_second = 0.999 * second_moment + 0.001 * coded_grad * coded_grad

time: 42.2 us -> 41.6 us (0.986)
  Pallas kernels: 7.65 us -> 10.3 us
  starting transfers between devices: 19.4 us -> 17.3 us
  waiting for transfers between devices: 10.9 us -> 9.84 us
    ppermute x7, waiting for transfers between devices: 9.61 us -> 6.9 us  [swap(): return lax.ppermute(value, axis, [(i, i ^ bit) for i in range(count)])]
    pallas_call x0 -> x1, Pallas kernels: none -> 2.71 us  [transposed(): pl.pallas_call(transposed_kernel, out_shape=jax.ShapeDtypeStruct((cols, r...]
    ppermute x6, starting transfers between devices: 11.6 us -> 9.51 us  [hop(): return lax.ppermute(value.astype(BF), 'dp', full)]
    ppermute x6, waiting for transfers between devices: 1.32 us -> 2.94 us  [hop(): return lax.ppermute(value.astype(BF), 'dp', full)]
  transfers between devices with their start and end apart: 13 -> 13, of which waited for: 6 -> 8; matrix products, arithmetic and copies ran while one was open for 6% -> 6% of each run, Pallas kernels for 6% -> 13%
where the time goes in v3:
time: 41.6 us; the launch traced here: 41.5 us
  starting transfers between devices  17.3 us (42%)
  Pallas kernels  10.3 us (25%)
  waiting for transfers between devices  9.84 us (24%)
  matrix products  2.8 us (7%)
  between operations  0.93 us (2%)
    ppermute x6, starting transfers between devices, hop(): return lax.ppermute(value.astype(BF), 'dp', full)  9.51 us
    ppermute x7, starting transfers between devices, swap(): return lax.ppermute(value, axis, [(i, i ^ bit) for i in range(count)])  7.84 us
    ppermute x7, waiting for transfers between devices, swap(): return lax.ppermute(value, axis, [(i, i ^ bit) for i in range(count)])  6.9 us
    pallas_call x2, Pallas kernels, adam_update(): pl.pallas_call(functools.partial(adam_update_kernel, cut, len(terms), len...  5.08 us
    ppermute x6, waiting for transfers between devices, hop(): return lax.ppermute(value.astype(BF), 'dp', full)  2.94 us
    pallas_call x1, Pallas kernels, transposed(): pl.pallas_call(transposed_kernel, out_shape=jax.ShapeDtypeStruct((cols, r...  2.71 us
    pallas_call x1, Pallas kernels, partial_code(): pl.pallas_call(partial_code_kernel, out_shape=(jax.ShapeDtypeStruct((rows...  2.55 us
    dot_general x11, matrix products, term(): return jnp.dot(part, code, preferred_element_type=F32)  2.52 us
  transfers between devices with their start and end apart: 13, of which 8 were waited for; matrix products, arithmetic and copies ran while one was open for 6% of the time, Pallas kernels for 13%

profile of v3, /device:TPU:0, one launch (start us, length us, event | category | flops | bytes accessed | tf_op | source)
XLA Modules:
  0.0 41.5 jit_solution(5811192036026723070)
XLA Ops:
  0.6 2.5 %partial_code.1 = (f32[192,256]{1,0:T(8,128)S(1)}, bf16[192,256]{1,0:T(8,128)(2,1)S(1)}) custom-call(bf16[384,2048]{1,0:T(8,128)(2,1)} %activations.1, bf16[8192,256]{1,0:T(8,128)(2,1)} %source), custom_call_target="tpu_custom_call" | custom-call | flops 402653184 | bytes 2621440 | tf_op jit(solution)/shard_map/partial_code/pallas_call | solution.py:58
  3.2 0.5 %collective-permute-start = (bf16[192,256]{1,0:T(8,128)(2,1)S(1)}, bf16[192,256]{1,0:T(8,128)(2,1)S(1)}, u32[]{:S(2)}, u32[]{:S(2)}) collective-permute-start(bf16[192,256]{1,0:T(8,128)(2,1)S(1)} %get-tuple-element.30), channel_id=1, source_target_pairs={{0,1},{1,0},{2,3},{3,2},{4,5},{5,4},{6,7},{7,6},{8,9},{9,8},{10,11... | collective-permute-start | bytes 294920 | tf_op jit(solution)/shard_map/ppermute | solution.py:16
  3.7 0.9 %collective-permute-done = bf16[192,256]{1,0:T(8,128)(2,1)S(1)} collective-permute-done((bf16[192,256]{1,0:T(8,128)(2,1)S(1)}, bf16[192,256]{1,0:T(8,128)(2,1)S(1)}, u32[]{:S(2)}, u32[]{:S(2)}) %collective-permute-start) | collective-permute-done | bytes 98336 | tf_op jit(solution)/shard_map/ppermute | solution.py:16
  4.7 2.9 %collective-permute-start.1 = (bf16[192,256]{1,0:T(8,128)(2,1)S(1)}, bf16[192,256]{1,0:T(8,128)(2,1)S(1)}, u32[]{:S(2)}, u32[]{:S(2)}) collective-permute-start(bf16[192,256]{1,0:T(8,128)(2,1)S(1)} %fusion.28), channel_id=1, source_target_pairs={{0,2},{1,3},{2,0},{3,1},{4,6},{5,7},{6,4},{7,5},{8,10},{9,11},{10,... | collective-permute-start | bytes 294920 | tf_op jit(solution)/shard_map/ppermute | solution.py:16
  7.6 3.1 %collective-permute-done.1 = bf16[192,256]{1,0:T(8,128)(2,1)S(1)} collective-permute-done((bf16[192,256]{1,0:T(8,128)(2,1)S(1)}, bf16[192,256]{1,0:T(8,128)(2,1)S(1)}, u32[]{:S(2)}, u32[]{:S(2)}) %collective-permute-start.1) | collective-permute-done | bytes 98336 | tf_op jit(solution)/shard_map/ppermute | solution.py:16
  11.0 1.2 %collective-permute-done.2 = bf16[192,256]{1,0:T(8,128)(2,1)S(1)} collective-permute-done((bf16[192,256]{1,0:T(8,128)(2,1)S(1)}, bf16[192,256]{1,0:T(8,128)(2,1)S(1)}, u32[]{:S(2)}, u32[]{:S(2)}) %collective-permute-start.2) | collective-permute-done | bytes 98336 | tf_op jit(solution)/shard_map/ppermute | solution.py:16
  12.2 0.3 convolution_convert_fusion.1
  12.5 0.3 convolution_convert_fusion
  12.8 1.8 %collective-permute-start.3 = (bf16[456,256]{1,0:T(8,128)(2,1)S(1)}, bf16[456,256]{1,0:T(8,128)(2,1)S(1)}, u32[]{:S(2)}, u32[]{:S(2)}) collective-permute-start(bf16[456,256]{1,0:T(8,128)(2,1)S(1)} %convolution_convert_fusion.1), channel_id=1, source_target_pairs={{0,4},{4,0},{8,12},{12,8},{16,20},{20,16},{24,28},{28,24},{1,5},{5... | collective-permute-start | bytes 700424 | tf_op jit(solution)/shard_map/ppermute | solution.py:16
  14.6 0.3 convolution_convert_fusion.2
  14.8 0.4 collective-permute-start.5
  15.2 1.8 %collective-permute-start.4 = (bf16[2,232,256]{2,1,0:T(8,128)(2,1)S(1)}, bf16[2,232,256]{2,1,0:T(8,128)(2,1)S(1)}, u32[]{:S(2)}, u32[]{:S(2)}) collective-permute-start(bf16[2,232,256]{2,1,0:T(8,128)(2,1)S(1)} %convolution_convert_fusion), channel_id=1, source_target_pairs={{0,8},{4,12},{8,0},{12,4},{16,24},{20,28},{24,16},{28,20},{1,9},{5... | collective-permute-start | bytes 712712 | tf_op jit(solution)/shard_map/ppermute | solution.py:156
  17.0 2.7 %transposed.1.basis_t = bf16[256,8192]{1,0:T(8,128)(2,1)S(1)} custom-call(bf16[8192,256]{1,0:T(8,128)(2,1)} %source), custom_call_target="tpu_custom_call" | custom-call | bytes 8388608 | tf_op jit(solution)/shard_map/transposed/pallas_call | solution.py:100
  19.7 1.7 %collective-permute-done.3 = bf16[456,256]{1,0:T(8,128)(2,1)S(1)} collective-permute-done((bf16[456,256]{1,0:T(8,128)(2,1)S(1)}, bf16[456,256]{1,0:T(8,128)(2,1)S(1)}, u32[]{:S(2)}, u32[]{:S(2)}) %collective-permute-start.3) | collective-permute-done | bytes 233504 | tf_op jit(solution)/shard_map/ppermute | solution.py:16
  21.4 0.2 add_convert_fusion.2
  21.6 0.2 add_convert_fusion.4
  21.8 1.9 %collective-permute-start.6 = (bf16[224,256]{1,0:T(8,128)(2,1)S(1)}, bf16[224,256]{1,0:T(8,128)(2,1)S(1)}, u32[]{:S(2)}, u32[]{:S(2)}) collective-permute-start(bf16[224,256]{1,0:T(8,128)(2,1)S(1)} %add_convert_fusion.4), channel_id=1, source_target_pairs={{0,8},{4,12},{8,0},{12,4},{16,24},{20,28},{24,16},{28,20},{1,9},{5... | collective-permute-start | bytes 344072 | tf_op jit(solution)/shard_map/ppermute | solution.py:156
  23.7 0.2 collective-permute-start.7
  24.2 1.8 %collective-permute-start.10 = (bf16[232,256]{1,0:T(8,128)(2,1)S(1)}, bf16[232,256]{1,0:T(8,128)(2,1)S(1)}, u32[]{:S(2)}, u32[]{:S(2)}) collective-permute-start(bf16[232,256]{1,0:T(8,128)(2,1)S(1)} %convolution_convert_fusion.3), channel_id=1, source_target_pairs={{0,4},{4,0},{8,12},{12,8},{16,20},{20,16},{24,28},{28,24},{1,5},{5... | collective-permute-start | bytes 356360 | tf_op jit(solution)/shard_map/ppermute | solution.py:16
  26.0 0.3 fusion
  26.3 0.4 collective-permute-start.8
  27.1 3.7 %collective-permute-start.12 = (bf16[224,256]{1,0:T(8,128)(2,1)S(1)}, bf16[224,256]{1,0:T(8,128)(2,1)S(1)}, u32[]{:S(2)}, u32[]{:S(2)}) collective-permute-start(bf16[224,256]{1,0:T(8,128)(2,1)S(1)} %add_convert_fusion.3), channel_id=1, source_target_pairs={{0,24},{4,28},{8,16},{12,20},{16,8},{20,12},{24,0},{28,4},{1,25},{... | collective-permute-start | bytes 344072 | tf_op jit(solution)/shard_map/ppermute | solution.py:156
  30.8 0.2 add_convert_fusion.1
  31.0 1.1 %collective-permute-start.9 = (bf16[232,256]{1,0:T(8,128)(2,1)S(1)}, bf16[232,256]{1,0:T(8,128)(2,1)S(1)}, u32[]{:S(2)}, u32[]{:S(2)}) collective-permute-start(bf16[232,256]{1,0:T(8,128)(2,1)S(1)} %add_convert_fusion.1), channel_id=1, source_target_pairs={{0,24},{4,28},{8,16},{12,20},{16,8},{20,12},{24,0},{28,4},{1,25},{... | collective-permute-start | bytes 356360 | tf_op jit(solution)/shard_map/ppermute | solution.py:156
  32.4 0.2 add_convert_fusion
  32.6 0.8 %collective-permute-start.11 = (bf16[232,256]{1,0:T(8,128)(2,1)S(1)}, bf16[232,256]{1,0:T(8,128)(2,1)S(1)}, u32[]{:S(2)}, u32[]{:S(2)}) collective-permute-start(bf16[232,256]{1,0:T(8,128)(2,1)S(1)} %add_convert_fusion), channel_id=1, source_target_pairs={{0,8},{4,12},{8,0},{12,4},{16,24},{20,28},{24,16},{28,20},{1,9},{5... | collective-permute-start | bytes 356360 | tf_op jit(solution)/shard_map/ppermute | solution.py:156
  33.4 0.2 convolution_add_fusion.1.own
  33.6 0.9 %collective-permute-done.12.refs_0_ = bf16[224,256]{1,0:T(8,128)(2,1)S(1)} collective-permute-done((bf16[224,256]{1,0:T(8,128)(2,1)S(1)}, bf16[224,256]{1,0:T(8,128)(2,1)S(1)}, u32[]{:S(2)}, u32[]{:S(2)}) %collective-permute-start.12) | collective-permute-done | bytes 114720 | tf_op jit(solution)/shard_map/ppermute | solution.py:156
  34.5 2.5 %adam_update.2 = (f32[456,256]{1,0:T(8,128)}, f32[456,256]{1,0:T(8,128)}, bf16[456,8192]{1,0:T(8,128)(2,1)}) custom-call(f32[224,256]{1,0:T(8,128)S(1)} %convolution_add_fusion.1.own, bf16[456,256]{1,0:T(8,128)(2,1)S(1)} %collective-permute-done.8.got, f32[456,256]{1,0:T(8,128)S(1)} %bitcast.28, f32[456,256]{1,0:T(8,128)S(1)} %bitcast.30, ...), custom_call_target="tpu_custom_call" | custom-call | flops 939524096 | bytes 7864320 | tf_op jit(solution)/shard_map/adam_update/pallas_call | solution.py:250
  37.0 0.9 %collective-permute-done.9.refs_0_ = bf16[232,256]{1,0:T(8,128)(2,1)S(1)} collective-permute-done((bf16[232,256]{1,0:T(8,128)(2,1)S(1)}, bf16[232,256]{1,0:T(8,128)(2,1)S(1)}, u32[]{:S(2)}, u32[]{:S(2)}) %collective-permute-start.9) | collective-permute-done | bytes 118816 | tf_op jit(solution)/shard_map/ppermute | solution.py:156
  37.9 1.0 %collective-permute-done.11.refs_1_ = bf16[232,256]{1,0:T(8,128)(2,1)S(1)} collective-permute-done((bf16[232,256]{1,0:T(8,128)(2,1)S(1)}, bf16[232,256]{1,0:T(8,128)(2,1)S(1)}, u32[]{:S(2)}, u32[]{:S(2)}) %collective-permute-start.11) | collective-permute-done | bytes 118816 | tf_op jit(solution)/shard_map/ppermute | solution.py:156
  38.9 2.6 %adam_update.3 = (f32[456,256]{1,0:T(8,128)}, f32[456,256]{1,0:T(8,128)}, bf16[456,8192]{1,0:T(8,128)(2,1)}) custom-call(f32[232,256]{1,0:T(8,128)S(1)} %fusion.19.own, bf16[456,256]{1,0:T(8,128)(2,1)S(1)} %collective-permute-done.8.got, f32[456,256]{1,0:T(8,128)S(1)} %bitcast.29, ...), custom_call_target="tpu_custom_call", output_to_operand_aliasing={{0}: (7, {}), {1}: (8, {}), {2}: (9, {})} | custom-call | flops 973078528 | bytes 7995392 | tf_op jit(solution)/shard_map/adam_update/pallas_call | solution.py:250
  (22 shorter events, 1.1 us)
Async XLA Ops:
  0.6 11.6 %copy-start = (bf16[384,3648]{0,1:T(8,128)(2,1)S(1)}, bf16[384,3648]{0,1:T(8,128)(2,1)}, u32[]{:S(2)}) copy-start(bf16[384,3648]{0,1:T(8,128)(2,1)} %param.7) | copy-start | bytes 8404996
  3.2 1.5 %collective-permute-start = (bf16[192,256]{1,0:T(8,128)(2,1)S(1)}, bf16[192,256]{1,0:T(8,128)(2,1)S(1)}, u32[]{:S(2)}, u32[]{:S(2)}) collective-permute-start(bf16[192,256]{1,0:T(8,128)(2,1)S(1)} %get-tuple-element.30), channel_id=1, source_target_pairs={{0,1},{1,0},{2,3},{3,2},{4,5},{5,4},{6,7},{7,6},{8,9},{9,8},{10,11... | collective-permute-start | bytes 294920 | tf_op jit(solution)/shard_map/ppermute | solution.py:16
  4.7 6.0 %collective-permute-start.1 = (bf16[192,256]{1,0:T(8,128)(2,1)S(1)}, bf16[192,256]{1,0:T(8,128)(2,1)S(1)}, u32[]{:S(2)}, u32[]{:S(2)}) collective-permute-start(bf16[192,256]{1,0:T(8,128)(2,1)S(1)} %fusion.28), channel_id=1, source_target_pairs={{0,2},{1,3},{2,0},{3,1},{4,6},{5,7},{6,4},{7,5},{8,10},{9,11},{10,... | collective-permute-start | bytes 294920 | tf_op jit(solution)/shard_map/ppermute | solution.py:16
  10.8 1.4 %collective-permute-start.2 = (bf16[192,256]{1,0:T(8,128)(2,1)S(1)}, bf16[192,256]{1,0:T(8,128)(2,1)S(1)}, u32[]{:S(2)}, u32[]{:S(2)}) collective-permute-start(bf16[192,256]{1,0:T(8,128)(2,1)S(1)} %add_convert_fusion.5), channel_id=1, source_target_pairs={{0,1},{1,0},{2,3},{3,2},{4,5},{5,4},{6,7},{7,6},{8,9},{9,8},{10,11... | collective-permute-start | bytes 294920 | tf_op jit(solution)/shard_map/ppermute | solution.py:16
  12.8 8.6 %collective-permute-start.3 = (bf16[456,256]{1,0:T(8,128)(2,1)S(1)}, bf16[456,256]{1,0:T(8,128)(2,1)S(1)}, u32[]{:S(2)}, u32[]{:S(2)}) collective-permute-start(bf16[456,256]{1,0:T(8,128)(2,1)S(1)} %convolution_convert_fusion.1), channel_id=1, source_target_pairs={{0,4},{4,0},{8,12},{12,8},{16,20},{20,16},{24,28},{28,24},{1,5},{5... | collective-permute-start | bytes 700424 | tf_op jit(solution)/shard_map/ppermute | solution.py:16
  14.8 12.0 %collective-permute-start.5 = (bf16[456,256]{1,0:T(8,128)(2,1)S(1)}, bf16[456,256]{1,0:T(8,128)(2,1)S(1)}, u32[]{:S(2)}, u32[]{:S(2)}) collective-permute-start(bf16[456,256]{1,0:T(8,128)(2,1)S(1)} %convolution_convert_fusion.2), channel_id=1, source_target_pairs={{0,4},{4,0},{8,12},{12,8},{16,20},{20,16},{24,28},{28,24},{1,5},{5... | collective-permute-start | bytes 700424 | tf_op jit(solution)/shard_map/ppermute | solution.py:16
  15.2 8.9 %collective-permute-start.4 = (bf16[2,232,256]{2,1,0:T(8,128)(2,1)S(1)}, bf16[2,232,256]{2,1,0:T(8,128)(2,1)S(1)}, u32[]{:S(2)}, u32[]{:S(2)}) collective-permute-start(bf16[2,232,256]{2,1,0:T(8,128)(2,1)S(1)} %convolution_convert_fusion), channel_id=1, source_target_pairs={{0,8},{4,12},{8,0},{12,4},{16,24},{20,28},{24,16},{28,20},{1,9},{5... | collective-permute-start | bytes 712712 | tf_op jit(solution)/shard_map/ppermute | solution.py:156
  21.8 5.2 %collective-permute-start.6 = (bf16[224,256]{1,0:T(8,128)(2,1)S(1)}, bf16[224,256]{1,0:T(8,128)(2,1)S(1)}, u32[]{:S(2)}, u32[]{:S(2)}) collective-permute-start(bf16[224,256]{1,0:T(8,128)(2,1)S(1)} %add_convert_fusion.4), channel_id=1, source_target_pairs={{0,8},{4,12},{8,0},{12,4},{16,24},{20,28},{24,16},{28,20},{1,9},{5... | collective-permute-start | bytes 344072 | tf_op jit(solution)/shard_map/ppermute | solution.py:156
  23.7 7.1 %collective-permute-start.7 = (bf16[232,256]{1,0:T(8,128)(2,1)S(1)}, bf16[232,256]{1,0:T(8,128)(2,1)S(1)}, u32[]{:S(2)}, u32[]{:S(2)}) collective-permute-start(bf16[232,256]{1,0:T(8,128)(2,1)S(1)} %add_convert_fusion.2), channel_id=1, source_target_pairs={{0,8},{4,12},{8,0},{12,4},{16,24},{20,28},{24,16},{28,20},{1,9},{5... | collective-permute-start | bytes 356360 | tf_op jit(solution)/shard_map/ppermute | solution.py:156
  24.1 10.3 %copy-start.1 = (f32[1,456,256]{2,1,0:T(8,128)S(1)}, f32[1,456,256]{2,1,0:T(8,128)}, u32[]{:S(2)}) copy-start(f32[1,456,256]{2,1,0:T(8,128)} %param.8) | copy-start | bytes 1400836
  24.1 10.3 %copy-start.2 = (f32[1,456,256]{2,1,0:T(8,128)S(1)}, f32[1,456,256]{2,1,0:T(8,128)}, u32[]{:S(2)}) copy-start(f32[1,456,256]{2,1,0:T(8,128)} %param.9) | copy-start | bytes 1400836
  24.2 8.2 %collective-permute-start.10 = (bf16[232,256]{1,0:T(8,128)(2,1)S(1)}, bf16[232,256]{1,0:T(8,128)(2,1)S(1)}, u32[]{:S(2)}, u32[]{:S(2)}) collective-permute-start(bf16[232,256]{1,0:T(8,128)(2,1)S(1)} %convolution_convert_fusion.3), channel_id=1, source_target_pairs={{0,4},{4,0},{8,12},{12,8},{16,20},{20,16},{24,28},{28,24},{1,5},{5... | collective-permute-start | bytes 356360 | tf_op jit(solution)/shard_map/ppermute | solution.py:16
  26.3 8.2 %collective-permute-start.8 = (bf16[456,256]{1,0:T(8,128)(2,1)S(1)}, bf16[456,256]{1,0:T(8,128)(2,1)S(1)}, u32[]{:S(2)}, u32[]{:S(2)}) collective-permute-start(bf16[456,256]{1,0:T(8,128)(2,1)S(1)} %fusion), channel_id=1, source_target_pairs={{0,4},{4,0},{8,12},{12,8},{16,20},{20,16},{24,28},{28,24},{1,5},{5... | collective-permute-start | bytes 700424 | tf_op jit(solution)/shard_map/ppermute | solution.py:16
  27.1 7.4 %collective-permute-start.12 = (bf16[224,256]{1,0:T(8,128)(2,1)S(1)}, bf16[224,256]{1,0:T(8,128)(2,1)S(1)}, u32[]{:S(2)}, u32[]{:S(2)}) collective-permute-start(bf16[224,256]{1,0:T(8,128)(2,1)S(1)} %add_convert_fusion.3), channel_id=1, source_target_pairs={{0,24},{4,28},{8,16},{12,20},{16,8},{20,12},{24,0},{28,4},{1,25},{... | collective-permute-start | bytes 344072 | tf_op jit(solution)/shard_map/ppermute | solution.py:156
  31.0 6.9 %collective-permute-start.9 = (bf16[232,256]{1,0:T(8,128)(2,1)S(1)}, bf16[232,256]{1,0:T(8,128)(2,1)S(1)}, u32[]{:S(2)}, u32[]{:S(2)}) collective-permute-start(bf16[232,256]{1,0:T(8,128)(2,1)S(1)} %add_convert_fusion.1), channel_id=1, source_target_pairs={{0,24},{4,28},{8,16},{12,20},{16,8},{20,12},{24,0},{28,4},{1,25},{... | collective-permute-start | bytes 356360 | tf_op jit(solution)/shard_map/ppermute | solution.py:156
  32.6 6.3 %collective-permute-start.11 = (bf16[232,256]{1,0:T(8,128)(2,1)S(1)}, bf16[232,256]{1,0:T(8,128)(2,1)S(1)}, u32[]{:S(2)}, u32[]{:S(2)}) collective-permute-start(bf16[232,256]{1,0:T(8,128)(2,1)S(1)} %add_convert_fusion), channel_id=1, source_target_pairs={{0,8},{4,12},{8,0},{12,4},{16,24},{20,28},{24,16},{28,20},{1,9},{5... | collective-permute-start | bytes 356360 | tf_op jit(solution)/shard_map/ppermute | solution.py:156

commit v4 on v2

--- a/solution.py
+++ b/solution.py
@@ -79,20 +79,56 @@
     )(activations, basis)
 
 
-def coded_total(keep, send, n_tensor):
+def load_kernel(source, target, sems):
+    count = DEEP if source.shape[0] % (16 * DEEP) == 0 else 1
+    rows = source.shape[0] // count
+    copies = [
+        pltpu.make_async_copy(
+            source.at[pl.ds(k * rows, rows), :], target.at[pl.ds(k * rows, rows), :], sems.at[k]
+        )
+        for k in range(count)
+    ]
+    for copy in copies:
+        copy.start()
+    for copy in copies:
+        copy.wait()
+
+
+def load(array):
+    return pl.pallas_call(
+        load_kernel,
+        out_shape=jax.ShapeDtypeStruct(array.shape, array.dtype),
+        in_specs=[pl.BlockSpec(memory_space=pltpu.HBM)],
+        out_specs=pl.BlockSpec(memory_space=pltpu.VMEM),
+        scratch_shapes=[pltpu.SemaphoreType.DMA((DEEP,))],
+        compiler_params=pltpu.CompilerParams(vmem_limit_bytes=50 * 2**20),
+        cost_estimate=pl.CostEstimate(
+            flops=0, bytes_accessed=4 * array.size, transcendentals=0
+        ),
+        name="load",
+    )(array)
+
+
+def coded_total(keep, send, grad_rows, n_tensor):
     core = lax.axis_index("tensor") % 2
     total = keep + swap(send, "tensor", 1, n_tensor).astype(F32)
     bit = 2
     while bit < n_tensor:
-        total = total + swap(total.astype(BF), "tensor", bit, n_tensor).astype(F32)
+        total_in = total.astype(BF)
+        if bit == 2:
+            total_in, grad_rows = lax.optimization_barrier((total_in, grad_rows))
+            grad_rows = load(grad_rows)
+        total = total + swap(total_in, "tensor", bit, n_tensor).astype(F32)
+        total, grad_rows = lax.optimization_barrier((total, grad_rows))
         bit *= 2
     mine = total.astype(BF)
     theirs = swap(mine, "tensor", 1, n_tensor)
-    return jnp.where(
+    coded = jnp.where(
         core == 0,
         jnp.concatenate([mine, theirs], 0),
         jnp.concatenate([theirs, mine], 0),
     )
+    return coded, grad_rows
 
 
 def line_total(grad_rows, coded, n_dp, cuts, spare=8):
@@ -133,7 +169,8 @@
     out1 = both(z ^ 1, coded, (0, first[1] + spare)).astype(BF)
     code, out1 = lax.optimization_barrier((coded, out1))
     near1 = hop(out1, 1)
-    got3 = pair(term(z ^ 3, 1 - x, code))
+    out3 = term(z ^ 3, 1 - x, code).astype(BF)
+    got3 = pair(out3)
 
     sums = [(term(z ^ 2, x, coded, cut) + piece(got2, cut)).astype(BF) for cut in cuts]
     code, sums = lax.optimization_barrier((coded, sums))
@@ -151,13 +188,11 @@
 
     code, total_a = total(first, passed[0], code)
     far_a = hop(total_a, 3)
-    late = (term(z ^ 1, x, code, second) + got1.astype(F32)).astype(BF)
-    code, late = lax.optimization_barrier((code, late))
-    late = hop(late, 1)
     code, total_b = total(second, passed[1], code)
     far_b = hop(total_b, 3)
+    late = hop(term(z ^ 1, x, code, second) + got1.astype(F32), 1)
     kept = [term(z, x, code, first) + parity(near1, x), term(z, x, code, second)]
-    return kept, own, [(far_a,), (late, far_b)]
+    return kept, own, [(far_a,), (far_b, late)]
 
 
 WIDE = 512
@@ -243,19 +278,19 @@
     n_tensor = lax.axis_size("tensor")
     n_dp = lax.axis_size("dp")
     keep, send = partial_code(activations, basis)
-    coded_rows = coded_total(keep, send, n_tensor)
+    coded_rows, grad_rows = coded_total(keep, send, out_grad.T, n_tensor)
     if n_dp == 8:
         rows = first_moment.shape[1]
         middle = rows // 32 * 16
         cuts = ((0, middle), (middle, rows))
-        kept, got, fars = line_total(out_grad.T, coded_rows, n_dp, cuts)
+        kept, got, fars = line_total(grad_rows, coded_rows, n_dp, cuts)
         outs = ()
         for cut, own, terms in zip(cuts, kept, fars):
             outs = adam_update(
                 cut, own, got, terms, first_moment[0], second_moment[0], basis, outs
             )
         return tuple(out[None] for out in outs)
-    term = jnp.dot(out_grad.T, coded_rows, preferred_element_type=F32)
+    term = jnp.dot(grad_rows, coded_rows, preferred_element_type=F32)
     coded_grad = lax.psum_scatter(term, "dp", scatter_dimension=0, tiled=True)[None]
     new_first = 0.9 * first_moment + 0.1 * coded_grad
     new_second = 0.999 * second_moment + 0.001 * coded_grad * coded_grad

time: 42.2 us -> 41.3 us (0.979)
  starting transfers between devices: 19.4 us -> 17.1 us
  Pallas kernels: 7.65 us -> 9.27 us
    ppermute x6, starting transfers between devices: 11.6 us -> 9.29 us  [hop(): return lax.ppermute(value.astype(BF), 'dp', full)]
    ppermute x7, waiting for transfers between devices: 9.61 us -> 7.83 us  [swap(): return lax.ppermute(value, axis, [(i, i ^ bit) for i in range(count)])]
    pallas_call x0 -> x1, Pallas kernels: none -> 1.77 us  [load(): pl.pallas_call(load_kernel, out_shape=jax.ShapeDtypeStruct(array.shape, a...]
    ppermute x6, waiting for transfers between devices: 1.32 us -> 2.89 us  [hop(): return lax.ppermute(value.astype(BF), 'dp', full)]
  transfers between devices with their start and end apart: 13 -> 13, of which waited for: 6 -> 8; matrix products, arithmetic and copies ran while one was open for 6% -> 6% of each run, Pallas kernels for 6% -> 10%
where the time goes in v4:
time: 41.3 us; the launch traced here: 41.1 us
  starting transfers between devices  17.1 us (41%)
  waiting for transfers between devices  10.7 us (26%)
  Pallas kernels  9.27 us (22%)
  matrix products  2.79 us (7%)
  between operations  0.94 us (2%)
    ppermute x6, starting transfers between devices, hop(): return lax.ppermute(value.astype(BF), 'dp', full)  9.29 us
    ppermute x7, starting transfers between devices, swap(): return lax.ppermute(value, axis, [(i, i ^ bit) for i in range(count)])  7.84 us
    ppermute x7, waiting for transfers between devices, swap(): return lax.ppermute(value, axis, [(i, i ^ bit) for i in range(count)])  7.83 us
    pallas_call x2, Pallas kernels, adam_update(): pl.pallas_call(functools.partial(adam_update_kernel, cut, len(terms), len...  5.1 us
    ppermute x6, waiting for transfers between devices, hop(): return lax.ppermute(value.astype(BF), 'dp', full)  2.89 us
    dot_general x11, matrix products, term(): return jnp.dot(part, code, preferred_element_type=F32)  2.52 us
    pallas_call x1, Pallas kernels, partial_code(): pl.pallas_call(partial_code_kernel, out_shape=(jax.ShapeDtypeStruct((rows...  2.4 us
    pallas_call x1, Pallas kernels, load(): pl.pallas_call(load_kernel, out_shape=jax.ShapeDtypeStruct(array.shape, a...  1.77 us
  transfers between devices with their start and end apart: 13, of which 8 were waited for; matrix products, arithmetic and copies ran while one was open for 6% of the time, Pallas kernels for 10%

profile of v4, /device:TPU:0, one launch (start us, length us, event | category | flops | bytes accessed | tf_op | source)
XLA Modules:
  0.0 41.1 jit_solution(4913702135396654281)
XLA Ops:
  0.6 2.4 %partial_code.1 = (f32[192,256]{1,0:T(8,128)S(1)}, bf16[192,256]{1,0:T(8,128)(2,1)S(1)}) custom-call(bf16[384,2048]{1,0:T(8,128)(2,1)} %activations.1, bf16[8192,256]{1,0:T(8,128)(2,1)} %basis.5), custom_call_target="tpu_custom_call" | custom-call | flops 402653184 | bytes 2621440 | tf_op jit(solution)/shard_map/partial_code/pallas_call | solution.py:58
  3.0 0.5 %collective-permute-start = (bf16[192,256]{1,0:T(8,128)(2,1)S(1)}, bf16[192,256]{1,0:T(8,128)(2,1)S(1)}, u32[]{:S(2)}, u32[]{:S(2)}) collective-permute-start(bf16[192,256]{1,0:T(8,128)(2,1)S(1)} %get-tuple-element.30), channel_id=1, source_target_pairs={{0,1},{1,0},{2,3},{3,2},{4,5},{5,4},{6,7},{7,6},{8,9},{9,8},{10,11... | collective-permute-start | bytes 294920 | tf_op jit(solution)/shard_map/ppermute | solution.py:16
  3.6 0.9 %collective-permute-done = bf16[192,256]{1,0:T(8,128)(2,1)S(1)} collective-permute-done((bf16[192,256]{1,0:T(8,128)(2,1)S(1)}, bf16[192,256]{1,0:T(8,128)(2,1)S(1)}, u32[]{:S(2)}, u32[]{:S(2)}) %collective-permute-start) | collective-permute-done | bytes 98336 | tf_op jit(solution)/shard_map/ppermute | solution.py:16
  4.5 2.9 %collective-permute-start.1 = (bf16[192,256]{1,0:T(8,128)(2,1)S(1)}, bf16[192,256]{1,0:T(8,128)(2,1)S(1)}, u32[]{:S(2)}, u32[]{:S(2)}) collective-permute-start(bf16[192,256]{1,0:T(8,128)(2,1)S(1)} %fusion.22), channel_id=1, source_target_pairs={{0,2},{1,3},{2,0},{3,1},{4,6},{5,7},{6,4},{7,5},{8,10},{9,11},{10,... | collective-permute-start | bytes 294920 | tf_op jit(solution)/shard_map/ppermute | solution.py:16
  7.5 1.8 %load.1 = bf16[3648,384]{1,0:T(8,128)(2,1)S(1)} custom-call(bf16[3648,384]{1,0:T(8,128)(2,1)} %bitcast.32), custom_call_target="tpu_custom_call" | custom-call | bytes 5603328 | tf_op jit(solution)/shard_map/load/pallas_call | solution.py:98
  9.2 1.3 %collective-permute-done.1 = bf16[192,256]{1,0:T(8,128)(2,1)S(1)} collective-permute-done((bf16[192,256]{1,0:T(8,128)(2,1)S(1)}, bf16[192,256]{1,0:T(8,128)(2,1)S(1)}, u32[]{:S(2)}, u32[]{:S(2)}) %collective-permute-start.1) | collective-permute-done | bytes 98336 | tf_op jit(solution)/shard_map/ppermute | solution.py:16
  10.8 1.2 %collective-permute-done.2 = bf16[192,256]{1,0:T(8,128)(2,1)S(1)} collective-permute-done((bf16[192,256]{1,0:T(8,128)(2,1)S(1)}, bf16[192,256]{1,0:T(8,128)(2,1)S(1)}, u32[]{:S(2)}, u32[]{:S(2)}) %collective-permute-start.2) | collective-permute-done | bytes 98336 | tf_op jit(solution)/shard_map/ppermute | solution.py:16
  12.0 0.3 convolution_convert_fusion.2
  12.3 0.3 convolution_convert_fusion
  12.6 1.8 %collective-permute-start.3 = (bf16[456,256]{1,0:T(8,128)(2,1)S(1)}, bf16[456,256]{1,0:T(8,128)(2,1)S(1)}, u32[]{:S(2)}, u32[]{:S(2)}) collective-permute-start(bf16[456,256]{1,0:T(8,128)(2,1)S(1)} %convolution_convert_fusion.2), channel_id=1, source_target_pairs={{0,4},{4,0},{8,12},{12,8},{16,20},{20,16},{24,28},{28,24},{1,5},{5... | collective-permute-start | bytes 700424 | tf_op jit(solution)/shard_map/ppermute | solution.py:16
  14.4 0.3 convolution_convert_fusion.1
  14.7 0.4 collective-permute-start.5
  15.0 1.8 %collective-permute-start.4 = (bf16[2,232,256]{2,1,0:T(8,128)(2,1)S(1)}, bf16[2,232,256]{2,1,0:T(8,128)(2,1)S(1)}, u32[]{:S(2)}, u32[]{:S(2)}) collective-permute-start(bf16[2,232,256]{2,1,0:T(8,128)(2,1)S(1)} %convolution_convert_fusion), channel_id=1, source_target_pairs={{0,8},{4,12},{8,0},{12,4},{16,24},{20,28},{24,16},{28,20},{1,9},{5... | collective-permute-start | bytes 712712 | tf_op jit(solution)/shard_map/ppermute | solution.py:157
  16.8 4.4 %collective-permute-done.3 = bf16[456,256]{1,0:T(8,128)(2,1)S(1)} collective-permute-done((bf16[456,256]{1,0:T(8,128)(2,1)S(1)}, bf16[456,256]{1,0:T(8,128)(2,1)S(1)}, u32[]{:S(2)}, u32[]{:S(2)}) %collective-permute-start.3) | collective-permute-done | bytes 233504 | tf_op jit(solution)/shard_map/ppermute | solution.py:16
  21.2 0.2 fusion.1
  21.4 0.2 fusion.2
  21.6 1.9 %collective-permute-start.6 = (bf16[224,256]{1,0:T(8,128)(2,1)S(1)}, bf16[224,256]{1,0:T(8,128)(2,1)S(1)}, u32[]{:S(2)}, u32[]{:S(2)}) collective-permute-start(bf16[224,256]{1,0:T(8,128)(2,1)S(1)} %fusion.2), channel_id=1, source_target_pairs={{0,8},{4,12},{8,0},{12,4},{16,24},{20,28},{24,16},{28,20},{1,9},{5... | collective-permute-start | bytes 344072 | tf_op jit(solution)/shard_map/ppermute | solution.py:157
  23.5 0.2 collective-permute-start.7
  23.7 0.2 convolution_convert_fusion.3
  24.0 1.8 %collective-permute-start.10 = (bf16[232,256]{1,0:T(8,128)(2,1)S(1)}, bf16[232,256]{1,0:T(8,128)(2,1)S(1)}, u32[]{:S(2)}, u32[]{:S(2)}) collective-permute-start(bf16[232,256]{1,0:T(8,128)(2,1)S(1)} %convolution_convert_fusion.3), channel_id=1, source_target_pairs={{0,4},{4,0},{8,12},{12,8},{16,20},{20,16},{24,28},{28,24},{1,5},{5... | collective-permute-start | bytes 356360 | tf_op jit(solution)/shard_map/ppermute | solution.py:16
  25.8 0.3 fusion
  26.1 0.4 collective-permute-start.8
  26.9 3.8 %collective-permute-start.12 = (bf16[224,256]{1,0:T(8,128)(2,1)S(1)}, bf16[224,256]{1,0:T(8,128)(2,1)S(1)}, u32[]{:S(2)}, u32[]{:S(2)}) collective-permute-start(bf16[224,256]{1,0:T(8,128)(2,1)S(1)} %add_convert_fusion.2), channel_id=1, source_target_pairs={{0,24},{4,28},{8,16},{12,20},{16,8},{20,12},{24,0},{28,4},{1,25},{... | collective-permute-start | bytes 344072 | tf_op jit(solution)/shard_map/ppermute | solution.py:157
  30.7 0.2 fusion.12
  30.9 0.8 %collective-permute-start.9 = (bf16[232,256]{1,0:T(8,128)(2,1)S(1)}, bf16[232,256]{1,0:T(8,128)(2,1)S(1)}, u32[]{:S(2)}, u32[]{:S(2)}) collective-permute-start(bf16[232,256]{1,0:T(8,128)(2,1)S(1)} %add_convert_fusion.1), channel_id=1, source_target_pairs={{0,24},{4,28},{8,16},{12,20},{16,8},{20,12},{24,0},{28,4},{1,25},{... | collective-permute-start | bytes 356360 | tf_op jit(solution)/shard_map/ppermute | solution.py:157
  32.0 0.2 add_convert_fusion
  32.2 0.8 %collective-permute-start.11 = (bf16[232,256]{1,0:T(8,128)(2,1)S(1)}, bf16[232,256]{1,0:T(8,128)(2,1)S(1)}, u32[]{:S(2)}, u32[]{:S(2)}) collective-permute-start(bf16[232,256]{1,0:T(8,128)(2,1)S(1)} %add_convert_fusion), channel_id=1, source_target_pairs={{0,8},{4,12},{8,0},{12,4},{16,24},{20,28},{24,16},{28,20},{1,9},{5... | collective-permute-start | bytes 356360 | tf_op jit(solution)/shard_map/ppermute | solution.py:157
  33.2 0.9 %collective-permute-done.12.refs_0_ = bf16[224,256]{1,0:T(8,128)(2,1)S(1)} collective-permute-done((bf16[224,256]{1,0:T(8,128)(2,1)S(1)}, bf16[224,256]{1,0:T(8,128)(2,1)S(1)}, u32[]{:S(2)}, u32[]{:S(2)}) %collective-permute-start.12) | collective-permute-done | bytes 114720 | tf_op jit(solution)/shard_map/ppermute | solution.py:157
  34.2 2.5 %adam_update.2 = (f32[456,256]{1,0:T(8,128)}, f32[456,256]{1,0:T(8,128)}, bf16[456,8192]{1,0:T(8,128)(2,1)}) custom-call(f32[224,256]{1,0:T(8,128)S(1)} %convolution_add_fusion.2.own, bf16[456,256]{1,0:T(8,128)(2,1)S(1)} %collective-permute-done.8.got, f32[456,256]{1,0:T(8,128)S(1)} %bitcast.27, f32[456,256]{1,0:T(8,128)S(1)} %bitcast.29, ...), custom_call_target="tpu_custom_call" | custom-call | flops 939524096 | bytes 7864320 | tf_op jit(solution)/shard_map/adam_update/pallas_call | solution.py:249
  36.7 1.1 %collective-permute-done.9.refs_0_ = bf16[232,256]{1,0:T(8,128)(2,1)S(1)} collective-permute-done((bf16[232,256]{1,0:T(8,128)(2,1)S(1)}, bf16[232,256]{1,0:T(8,128)(2,1)S(1)}, u32[]{:S(2)}, u32[]{:S(2)}) %collective-permute-start.9) | collective-permute-done | bytes 118816 | tf_op jit(solution)/shard_map/ppermute | solution.py:157
  37.8 0.8 %collective-permute-done.11.refs_1_ = bf16[232,256]{1,0:T(8,128)(2,1)S(1)} collective-permute-done((bf16[232,256]{1,0:T(8,128)(2,1)S(1)}, bf16[232,256]{1,0:T(8,128)(2,1)S(1)}, u32[]{:S(2)}, u32[]{:S(2)}) %collective-permute-start.11) | collective-permute-done | bytes 118816 | tf_op jit(solution)/shard_map/ppermute | solution.py:157
  38.6 2.6 %adam_update.3 = (f32[456,256]{1,0:T(8,128)}, f32[456,256]{1,0:T(8,128)}, bf16[456,8192]{1,0:T(8,128)(2,1)}) custom-call(f32[232,256]{1,0:T(8,128)S(1)} %fusion.16.own, bf16[456,256]{1,0:T(8,128)(2,1)S(1)} %collective-permute-done.8.got, f32[456,256]{1,0:T(8,128)S(1)} %bitcast.28, ...), custom_call_target="tpu_custom_call", output_to_operand_aliasing={{0}: (7, {}), {1}: (8, {}), {2}: (9, {})} | custom-call | flops 973078528 | bytes 7995392 | tf_op jit(solution)/shard_map/adam_update/pallas_call | solution.py:249
  (23 shorter events, 1.1 us)
Async XLA Ops:
  3.0 1.5 %collective-permute-start = (bf16[192,256]{1,0:T(8,128)(2,1)S(1)}, bf16[192,256]{1,0:T(8,128)(2,1)S(1)}, u32[]{:S(2)}, u32[]{:S(2)}) collective-permute-start(bf16[192,256]{1,0:T(8,128)(2,1)S(1)} %get-tuple-element.30), channel_id=1, source_target_pairs={{0,1},{1,0},{2,3},{3,2},{4,5},{5,4},{6,7},{7,6},{8,9},{9,8},{10,11... | collective-permute-start | bytes 294920 | tf_op jit(solution)/shard_map/ppermute | solution.py:16
  4.5 6.0 %collective-permute-start.1 = (bf16[192,256]{1,0:T(8,128)(2,1)S(1)}, bf16[192,256]{1,0:T(8,128)(2,1)S(1)}, u32[]{:S(2)}, u32[]{:S(2)}) collective-permute-start(bf16[192,256]{1,0:T(8,128)(2,1)S(1)} %fusion.22), channel_id=1, source_target_pairs={{0,2},{1,3},{2,0},{3,1},{4,6},{5,7},{6,4},{7,5},{8,10},{9,11},{10,... | collective-permute-start | bytes 294920 | tf_op jit(solution)/shard_map/ppermute | solution.py:16
  10.6 1.4 %collective-permute-start.2 = (bf16[192,256]{1,0:T(8,128)(2,1)S(1)}, bf16[192,256]{1,0:T(8,128)(2,1)S(1)}, u32[]{:S(2)}, u32[]{:S(2)}) collective-permute-start(bf16[192,256]{1,0:T(8,128)(2,1)S(1)} %convert_add_fusion), channel_id=1, source_target_pairs={{0,1},{1,0},{2,3},{3,2},{4,5},{5,4},{6,7},{7,6},{8,9},{9,8},{10,11... | collective-permute-start | bytes 294920 | tf_op jit(solution)/shard_map/ppermute | solution.py:16
  12.6 8.6 %collective-permute-start.3 = (bf16[456,256]{1,0:T(8,128)(2,1)S(1)}, bf16[456,256]{1,0:T(8,128)(2,1)S(1)}, u32[]{:S(2)}, u32[]{:S(2)}) collective-permute-start(bf16[456,256]{1,0:T(8,128)(2,1)S(1)} %convolution_convert_fusion.2), channel_id=1, source_target_pairs={{0,4},{4,0},{8,12},{12,8},{16,20},{20,16},{24,28},{28,24},{1,5},{5... | collective-permute-start | bytes 700424 | tf_op jit(solution)/shard_map/ppermute | solution.py:16
  14.7 12.0 %collective-permute-start.5 = (bf16[456,256]{1,0:T(8,128)(2,1)S(1)}, bf16[456,256]{1,0:T(8,128)(2,1)S(1)}, u32[]{:S(2)}, u32[]{:S(2)}) collective-permute-start(bf16[456,256]{1,0:T(8,128)(2,1)S(1)} %convolution_convert_fusion.1), channel_id=1, source_target_pairs={{0,4},{4,0},{8,12},{12,8},{16,20},{20,16},{24,28},{28,24},{1,5},{5... | collective-permute-start | bytes 700424 | tf_op jit(solution)/shard_map/ppermute | solution.py:16
  15.0 8.9 %collective-permute-start.4 = (bf16[2,232,256]{2,1,0:T(8,128)(2,1)S(1)}, bf16[2,232,256]{2,1,0:T(8,128)(2,1)S(1)}, u32[]{:S(2)}, u32[]{:S(2)}) collective-permute-start(bf16[2,232,256]{2,1,0:T(8,128)(2,1)S(1)} %convolution_convert_fusion), channel_id=1, source_target_pairs={{0,8},{4,12},{8,0},{12,4},{16,24},{20,28},{24,16},{28,20},{1,9},{5... | collective-permute-start | bytes 712712 | tf_op jit(solution)/shard_map/ppermute | solution.py:157
  21.6 5.2 %collective-permute-start.6 = (bf16[224,256]{1,0:T(8,128)(2,1)S(1)}, bf16[224,256]{1,0:T(8,128)(2,1)S(1)}, u32[]{:S(2)}, u32[]{:S(2)}) collective-permute-start(bf16[224,256]{1,0:T(8,128)(2,1)S(1)} %fusion.2), channel_id=1, source_target_pairs={{0,8},{4,12},{8,0},{12,4},{16,24},{20,28},{24,16},{28,20},{1,9},{5... | collective-permute-start | bytes 344072 | tf_op jit(solution)/shard_map/ppermute | solution.py:157
  23.5 7.4 %collective-permute-start.7 = (bf16[232,256]{1,0:T(8,128)(2,1)S(1)}, bf16[232,256]{1,0:T(8,128)(2,1)S(1)}, u32[]{:S(2)}, u32[]{:S(2)}) collective-permute-start(bf16[232,256]{1,0:T(8,128)(2,1)S(1)} %fusion.1), channel_id=1, source_target_pairs={{0,8},{4,12},{8,0},{12,4},{16,24},{20,28},{24,16},{28,20},{1,9},{5... | collective-permute-start | bytes 356360 | tf_op jit(solution)/shard_map/ppermute | solution.py:157
  24.0 8.0 %collective-permute-start.10 = (bf16[232,256]{1,0:T(8,128)(2,1)S(1)}, bf16[232,256]{1,0:T(8,128)(2,1)S(1)}, u32[]{:S(2)}, u32[]{:S(2)}) collective-permute-start(bf16[232,256]{1,0:T(8,128)(2,1)S(1)} %convolution_convert_fusion.3), channel_id=1, source_target_pairs={{0,4},{4,0},{8,12},{12,8},{16,20},{20,16},{24,28},{28,24},{1,5},{5... | collective-permute-start | bytes 356360 | tf_op jit(solution)/shard_map/ppermute | solution.py:16
  25.8 8.4 %copy-start = (bf16[8192,256]{1,0:T(8,128)(2,1)S(1)}, bf16[8192,256]{1,0:T(8,128)(2,1)}, u32[]{:S(2)}) copy-start(bf16[8192,256]{1,0:T(8,128)(2,1)} %basis.5) | copy-start | bytes 12582916
  25.8 8.4 %copy-start.1 = (f32[1,456,256]{2,1,0:T(8,128)S(1)}, f32[1,456,256]{2,1,0:T(8,128)}, u32[]{:S(2)}) copy-start(f32[1,456,256]{2,1,0:T(8,128)} %param.8) | copy-start | bytes 1400836
  25.8 8.4 %copy-start.2 = (f32[1,456,256]{2,1,0:T(8,128)S(1)}, f32[1,456,256]{2,1,0:T(8,128)}, u32[]{:S(2)}) copy-start(f32[1,456,256]{2,1,0:T(8,128)} %param.9) | copy-start | bytes 1400836
  26.1 8.1 %collective-permute-start.8 = (bf16[456,256]{1,0:T(8,128)(2,1)S(1)}, bf16[456,256]{1,0:T(8,128)(2,1)S(1)}, u32[]{:S(2)}, u32[]{:S(2)}) collective-permute-start(bf16[456,256]{1,0:T(8,128)(2,1)S(1)} %fusion), channel_id=1, source_target_pairs={{0,4},{4,0},{8,12},{12,8},{16,20},{20,16},{24,28},{28,24},{1,5},{5... | collective-permute-start | bytes 700424 | tf_op jit(solution)/shard_map/ppermute | solution.py:16
  26.9 7.2 %collective-permute-start.12 = (bf16[224,256]{1,0:T(8,128)(2,1)S(1)}, bf16[224,256]{1,0:T(8,128)(2,1)S(1)}, u32[]{:S(2)}, u32[]{:S(2)}) collective-permute-start(bf16[224,256]{1,0:T(8,128)(2,1)S(1)} %add_convert_fusion.2), channel_id=1, source_target_pairs={{0,24},{4,28},{8,16},{12,20},{16,8},{20,12},{24,0},{28,4},{1,25},{... | collective-permute-start | bytes 344072 | tf_op jit(solution)/shard_map/ppermute | solution.py:157
  30.9 6.9 %collective-permute-start.9 = (bf16[232,256]{1,0:T(8,128)(2,1)S(1)}, bf16[232,256]{1,0:T(8,128)(2,1)S(1)}, u32[]{:S(2)}, u32[]{:S(2)}) collective-permute-start(bf16[232,256]{1,0:T(8,128)(2,1)S(1)} %add_convert_fusion.1), channel_id=1, source_target_pairs={{0,24},{4,28},{8,16},{12,20},{16,8},{20,12},{24,0},{28,4},{1,25},{... | collective-permute-start | bytes 356360 | tf_op jit(solution)/shard_map/ppermute | solution.py:157
  32.2 6.3 %collective-permute-start.11 = (bf16[232,256]{1,0:T(8,128)(2,1)S(1)}, bf16[232,256]{1,0:T(8,128)(2,1)S(1)}, u32[]{:S(2)}, u32[]{:S(2)}) collective-permute-start(bf16[232,256]{1,0:T(8,128)(2,1)S(1)} %add_convert_fusion), channel_id=1, source_target_pairs={{0,8},{4,12},{8,0},{12,4},{16,24},{20,28},{24,16},{28,20},{1,9},{5... | collective-permute-start | bytes 356360 | tf_op jit(solution)/shard_map/ppermute | solution.py:157

commit v5 on v2

--- a/solution.py
+++ b/solution.py
@@ -133,28 +133,34 @@
     out1 = both(z ^ 1, coded, (0, first[1] + spare)).astype(BF)
     code, out1 = lax.optimization_barrier((coded, out1))
     near1 = hop(out1, 1)
-    got3 = pair(term(z ^ 3, 1 - x, code))
+    n_first = first[1]
+    got31 = jnp.concatenate(
+        [term(z ^ 3, 1 - x, code, first), term(z ^ 1, 1 - x, code, second)]
+    )
+    got31 = pair(got31)
 
     sums = [(term(z ^ 2, x, coded, cut) + piece(got2, cut)).astype(BF) for cut in cuts]
     code, sums = lax.optimization_barrier((coded, sums))
     passed = [hop(part, 1) for part in sums]
-    out1 = term(z ^ 1, 1 - x, code, second).astype(BF)
-    code, out1, near1 = lax.optimization_barrier((code, out1, near1))
-    got1 = pair(out1)
+    out3 = term(z ^ 3, 1 - x, code, second).astype(BF)
+    code, out3, near1 = lax.optimization_barrier((code, out3, near1))
+    got3 = pair(out3)
     near1 = near1[:, : first[1]]
     own_in = (term(z, 1 - x, code) + padded(parity(near1, 1 - x))).astype(BF)
     code, own_in = lax.optimization_barrier((coded, own_in))
     own = pair(own_in)
-    def total(cut, part, code):
-        value = term(z ^ 3, x, code, cut) + piece(got3, cut) + part.astype(F32)
+
+    def total(block, cut, code, *parts):
+        value = term(block, x, code, cut)
+        for part in parts:
+            value = value + part.astype(F32)
         return lax.optimization_barrier((code, value.astype(BF)))
 
-    code, total_a = total(first, passed[0], code)
+    code, total_a = total(z ^ 3, first, code, got31[:n_first], passed[0])
     far_a = hop(total_a, 3)
-    late = (term(z ^ 1, x, code, second) + got1.astype(F32)).astype(BF)
-    code, late = lax.optimization_barrier((code, late))
+    code, late = total(z ^ 1, second, code, got31[n_first:])
     late = hop(late, 1)
-    code, total_b = total(second, passed[1], code)
+    code, total_b = total(z ^ 3, second, code, got3, passed[1])
     far_b = hop(total_b, 3)
     kept = [term(z, x, code, first) + parity(near1, x), term(z, x, code, second)]
     return kept, own, [(far_a,), (late, far_b)]

time: 42.2 us -> 41 us (0.972)
  starting transfers between devices: 19.4 us -> 18.4 us
    ppermute x6, starting transfers between devices: 11.6 us -> 10.6 us  [hop(): return lax.ppermute(value.astype(BF), 'dp', full)]
    dot_general x11 -> x12, matrix products: 2.52 us -> 2.67 us  [term(): return jnp.dot(part, code, preferred_element_type=F32)]
  transfers between devices with their start and end apart: 13 -> 13, of which waited for: 6 -> 7; matrix products, arithmetic and copies ran while one was open for 6% -> 6% of each run, Pallas kernels for 6% -> 6%
where the time goes in v5:
time: 41 us; the launch traced here: 40.8 us
  starting transfers between devices  18.4 us (45%)
  waiting for transfers between devices  10.5 us (26%)
  Pallas kernels  7.65 us (19%)
  matrix products  2.94 us (7%)
  between operations  0.98 us (2%)
    ppermute x6, starting transfers between devices, hop(): return lax.ppermute(value.astype(BF), 'dp', full)  10.6 us
    ppermute x7, waiting for transfers between devices, swap(): return lax.ppermute(value, axis, [(i, i ^ bit) for i in range(count)])  9.43 us
    ppermute x7, starting transfers between devices, swap(): return lax.ppermute(value, axis, [(i, i ^ bit) for i in range(count)])  7.84 us
    pallas_call x2, Pallas kernels, adam_update(): pl.pallas_call(functools.partial(adam_update_kernel, cut, len(terms), len...  5.11 us
    dot_general x12, matrix products, term(): return jnp.dot(part, code, preferred_element_type=F32)  2.67 us
    pallas_call x1, Pallas kernels, partial_code(): pl.pallas_call(partial_code_kernel, out_shape=(jax.ShapeDtypeStruct((rows...  2.55 us
    ppermute x6, waiting for transfers between devices, hop(): return lax.ppermute(value.astype(BF), 'dp', full)  1.07 us
  transfers between devices with their start and end apart: 13, of which 7 were waited for; matrix products, arithmetic and copies ran while one was open for 6% of the time, Pallas kernels for 6%

profile of v5, /device:TPU:0, one launch (start us, length us, event | category | flops | bytes accessed | tf_op | source)
XLA Modules:
  0.0 40.8 jit_solution(9444227939008496292)
XLA Ops:
  0.6 2.5 %partial_code.1 = (f32[192,256]{1,0:T(8,128)S(1)}, bf16[192,256]{1,0:T(8,128)(2,1)S(1)}) custom-call(bf16[384,2048]{1,0:T(8,128)(2,1)} %activations.1, bf16[8192,256]{1,0:T(8,128)(2,1)} %basis.5), custom_call_target="tpu_custom_call" | custom-call | flops 402653184 | bytes 2621440 | tf_op jit(solution)/shard_map/partial_code/pallas_call | solution.py:58
  3.2 0.5 %collective-permute-start = (bf16[192,256]{1,0:T(8,128)(2,1)S(1)}, bf16[192,256]{1,0:T(8,128)(2,1)S(1)}, u32[]{:S(2)}, u32[]{:S(2)}) collective-permute-start(bf16[192,256]{1,0:T(8,128)(2,1)S(1)} %get-tuple-element.28), channel_id=1, source_target_pairs={{0,1},{1,0},{2,3},{3,2},{4,5},{5,4},{6,7},{7,6},{8,9},{9,8},{10,11... | collective-permute-start | bytes 294920 | tf_op jit(solution)/shard_map/ppermute | solution.py:16
  3.7 0.9 %collective-permute-done = bf16[192,256]{1,0:T(8,128)(2,1)S(1)} collective-permute-done((bf16[192,256]{1,0:T(8,128)(2,1)S(1)}, bf16[192,256]{1,0:T(8,128)(2,1)S(1)}, u32[]{:S(2)}, u32[]{:S(2)}) %collective-permute-start) | collective-permute-done | bytes 98336 | tf_op jit(solution)/shard_map/ppermute | solution.py:16
  4.7 2.9 %collective-permute-start.1 = (bf16[192,256]{1,0:T(8,128)(2,1)S(1)}, bf16[192,256]{1,0:T(8,128)(2,1)S(1)}, u32[]{:S(2)}, u32[]{:S(2)}) collective-permute-start(bf16[192,256]{1,0:T(8,128)(2,1)S(1)} %fusion.23), channel_id=1, source_target_pairs={{0,2},{1,3},{2,0},{3,1},{4,6},{5,7},{6,4},{7,5},{8,10},{9,11},{10,... | collective-permute-start | bytes 294920 | tf_op jit(solution)/shard_map/ppermute | solution.py:16
  7.6 3.1 %collective-permute-done.1 = bf16[192,256]{1,0:T(8,128)(2,1)S(1)} collective-permute-done((bf16[192,256]{1,0:T(8,128)(2,1)S(1)}, bf16[192,256]{1,0:T(8,128)(2,1)S(1)}, u32[]{:S(2)}, u32[]{:S(2)}) %collective-permute-start.1) | collective-permute-done | bytes 98336 | tf_op jit(solution)/shard_map/ppermute | solution.py:16
  11.0 1.2 %collective-permute-done.2 = bf16[192,256]{1,0:T(8,128)(2,1)S(1)} collective-permute-done((bf16[192,256]{1,0:T(8,128)(2,1)S(1)}, bf16[192,256]{1,0:T(8,128)(2,1)S(1)}, u32[]{:S(2)}, u32[]{:S(2)}) %collective-permute-start.2) | collective-permute-done | bytes 98336 | tf_op jit(solution)/shard_map/ppermute | solution.py:16
  12.2 0.3 convolution_convert_fusion.1
  12.5 0.3 convolution_convert_fusion
  12.8 1.8 %collective-permute-start.3 = (bf16[456,256]{1,0:T(8,128)(2,1)S(1)}, bf16[456,256]{1,0:T(8,128)(2,1)S(1)}, u32[]{:S(2)}, u32[]{:S(2)}) collective-permute-start(bf16[456,256]{1,0:T(8,128)(2,1)S(1)} %convolution_convert_fusion.1), channel_id=1, source_target_pairs={{0,4},{4,0},{8,12},{12,8},{16,20},{20,16},{24,28},{28,24},{1,5},{5... | collective-permute-start | bytes 700424 | tf_op jit(solution)/shard_map/ppermute | solution.py:16
  14.6 0.2 convolution_convert_fusion.2
  14.8 0.2 convolution_convert_fusion.4
  15.0 0.4 collective-permute-start.5
  15.4 1.8 %collective-permute-start.4 = (bf16[2,232,256]{2,1,0:T(8,128)(2,1)S(1)}, bf16[2,232,256]{2,1,0:T(8,128)(2,1)S(1)}, u32[]{:S(2)}, u32[]{:S(2)}) collective-permute-start(bf16[2,232,256]{2,1,0:T(8,128)(2,1)S(1)} %convolution_convert_fusion), channel_id=1, source_target_pairs={{0,8},{4,12},{8,0},{12,4},{16,24},{20,28},{24,16},{28,20},{1,9},{5... | collective-permute-start | bytes 712712 | tf_op jit(solution)/shard_map/ppermute | solution.py:121
  17.2 4.2 %collective-permute-done.3 = bf16[456,256]{1,0:T(8,128)(2,1)S(1)} collective-permute-done((bf16[456,256]{1,0:T(8,128)(2,1)S(1)}, bf16[456,256]{1,0:T(8,128)(2,1)S(1)}, u32[]{:S(2)}, u32[]{:S(2)}) %collective-permute-start.3) | collective-permute-done | bytes 233504 | tf_op jit(solution)/shard_map/ppermute | solution.py:16
  21.4 0.2 fusion.1
  21.6 0.2 fusion.2
  21.8 1.9 %collective-permute-start.6 = (bf16[224,256]{1,0:T(8,128)(2,1)S(1)}, bf16[224,256]{1,0:T(8,128)(2,1)S(1)}, u32[]{:S(2)}, u32[]{:S(2)}) collective-permute-start(bf16[224,256]{1,0:T(8,128)(2,1)S(1)} %fusion.2), channel_id=1, source_target_pairs={{0,8},{4,12},{8,0},{12,4},{16,24},{20,28},{24,16},{28,20},{1,9},{5... | collective-permute-start | bytes 344072 | tf_op jit(solution)/shard_map/ppermute | solution.py:121
  23.7 0.2 collective-permute-start.8
  23.9 0.2 convolution_convert_fusion.3
  24.1 1.8 %collective-permute-start.7 = (bf16[232,256]{1,0:T(8,128)(2,1)S(1)}, bf16[232,256]{1,0:T(8,128)(2,1)S(1)}, u32[]{:S(2)}, u32[]{:S(2)}) collective-permute-start(bf16[232,256]{1,0:T(8,128)(2,1)S(1)} %convolution_convert_fusion.3), channel_id=1, source_target_pairs={{0,4},{4,0},{8,12},{12,8},{16,20},{20,16},{24,28},{28,24},{1,5},{5... | collective-permute-start | bytes 356360 | tf_op jit(solution)/shard_map/ppermute | solution.py:16
  26.0 0.3 fusion
  26.3 0.4 collective-permute-start.9
  27.1 0.2 add_convert_fusion.1
  27.3 3.7 %collective-permute-start.12 = (bf16[224,256]{1,0:T(8,128)(2,1)S(1)}, bf16[224,256]{1,0:T(8,128)(2,1)S(1)}, u32[]{:S(2)}, u32[]{:S(2)}) collective-permute-start(bf16[224,256]{1,0:T(8,128)(2,1)S(1)} %add_convert_fusion.2), channel_id=1, source_target_pairs={{0,24},{4,28},{8,16},{12,20},{16,8},{20,12},{24,0},{28,4},{1,25},{... | collective-permute-start | bytes 344072 | tf_op jit(solution)/shard_map/ppermute | solution.py:121
  31.1 0.2 fusion.7
  31.3 3.0 %collective-permute-start.11 = (bf16[232,256]{1,0:T(8,128)(2,1)S(1)}, bf16[232,256]{1,0:T(8,128)(2,1)S(1)}, u32[]{:S(2)}, u32[]{:S(2)}) collective-permute-start(bf16[232,256]{1,0:T(8,128)(2,1)S(1)} %add_convert_fusion), channel_id=1, source_target_pairs={{0,24},{4,28},{8,16},{12,20},{16,8},{20,12},{24,0},{28,4},{1,25},{... | collective-permute-start | bytes 356360 | tf_op jit(solution)/shard_map/ppermute | solution.py:121
  34.3 0.2 fusion.16.own
  34.5 0.2 convolution_add_fusion.2.own
  34.7 0.4 %collective-permute-done.12.refs_0_ = bf16[224,256]{1,0:T(8,128)(2,1)S(1)} collective-permute-done((bf16[224,256]{1,0:T(8,128)(2,1)S(1)}, bf16[224,256]{1,0:T(8,128)(2,1)S(1)}, u32[]{:S(2)}, u32[]{:S(2)}) %collective-permute-start.12) | collective-permute-done | bytes 114720 | tf_op jit(solution)/shard_map/ppermute | solution.py:121
  35.2 2.5 %adam_update.2 = (f32[456,256]{1,0:T(8,128)}, f32[456,256]{1,0:T(8,128)}, bf16[456,8192]{1,0:T(8,128)(2,1)}) custom-call(f32[224,256]{1,0:T(8,128)S(1)} %convolution_add_fusion.2.own, bf16[456,256]{1,0:T(8,128)(2,1)S(1)} %collective-permute-done.9.got, f32[456,256]{1,0:T(8,128)S(1)} %bitcast.29, f32[456,256]{1,0:T(8,128)S(1)} %bitcast.31, ...), custom_call_target="tpu_custom_call" | custom-call | flops 939524096 | bytes 7864320 | tf_op jit(solution)/shard_map/adam_update/pallas_call | solution.py:220
  37.7 0.5 %collective-permute-done.11.refs_1_ = bf16[232,256]{1,0:T(8,128)(2,1)S(1)} collective-permute-done((bf16[232,256]{1,0:T(8,128)(2,1)S(1)}, bf16[232,256]{1,0:T(8,128)(2,1)S(1)}, u32[]{:S(2)}, u32[]{:S(2)}) %collective-permute-start.11) | collective-permute-done | bytes 118816 | tf_op jit(solution)/shard_map/ppermute | solution.py:121
  38.2 2.6 %adam_update.3 = (f32[456,256]{1,0:T(8,128)}, f32[456,256]{1,0:T(8,128)}, bf16[456,8192]{1,0:T(8,128)(2,1)}) custom-call(f32[232,256]{1,0:T(8,128)S(1)} %fusion.16.own, bf16[456,256]{1,0:T(8,128)(2,1)S(1)} %collective-permute-done.9.got, f32[456,256]{1,0:T(8,128)S(1)} %bitcast.30, ...), custom_call_target="tpu_custom_call", output_to_operand_aliasing={{0}: (7, {}), {1}: (8, {}), {2}: (9, {})} | custom-call | flops 973078528 | bytes 7995392 | tf_op jit(solution)/shard_map/adam_update/pallas_call | solution.py:220
  (26 shorter events, 0.7 us)
Async XLA Ops:
  0.6 11.6 %copy-start = (bf16[384,3648]{0,1:T(8,128)(2,1)S(1)}, bf16[384,3648]{0,1:T(8,128)(2,1)}, u32[]{:S(2)}) copy-start(bf16[384,3648]{0,1:T(8,128)(2,1)} %param.7) | copy-start | bytes 8404996
  3.2 1.5 %collective-permute-start = (bf16[192,256]{1,0:T(8,128)(2,1)S(1)}, bf16[192,256]{1,0:T(8,128)(2,1)S(1)}, u32[]{:S(2)}, u32[]{:S(2)}) collective-permute-start(bf16[192,256]{1,0:T(8,128)(2,1)S(1)} %get-tuple-element.28), channel_id=1, source_target_pairs={{0,1},{1,0},{2,3},{3,2},{4,5},{5,4},{6,7},{7,6},{8,9},{9,8},{10,11... | collective-permute-start | bytes 294920 | tf_op jit(solution)/shard_map/ppermute | solution.py:16
  4.7 6.0 %collective-permute-start.1 = (bf16[192,256]{1,0:T(8,128)(2,1)S(1)}, bf16[192,256]{1,0:T(8,128)(2,1)S(1)}, u32[]{:S(2)}, u32[]{:S(2)}) collective-permute-start(bf16[192,256]{1,0:T(8,128)(2,1)S(1)} %fusion.23), channel_id=1, source_target_pairs={{0,2},{1,3},{2,0},{3,1},{4,6},{5,7},{6,4},{7,5},{8,10},{9,11},{10,... | collective-permute-start | bytes 294920 | tf_op jit(solution)/shard_map/ppermute | solution.py:16
  10.8 1.4 %collective-permute-start.2 = (bf16[192,256]{1,0:T(8,128)(2,1)S(1)}, bf16[192,256]{1,0:T(8,128)(2,1)S(1)}, u32[]{:S(2)}, u32[]{:S(2)}) collective-permute-start(bf16[192,256]{1,0:T(8,128)(2,1)S(1)} %add_convert_fusion.3), channel_id=1, source_target_pairs={{0,1},{1,0},{2,3},{3,2},{4,5},{5,4},{6,7},{7,6},{8,9},{9,8},{10,11... | collective-permute-start | bytes 294920 | tf_op jit(solution)/shard_map/ppermute | solution.py:16
  12.8 8.6 %collective-permute-start.3 = (bf16[456,256]{1,0:T(8,128)(2,1)S(1)}, bf16[456,256]{1,0:T(8,128)(2,1)S(1)}, u32[]{:S(2)}, u32[]{:S(2)}) collective-permute-start(bf16[456,256]{1,0:T(8,128)(2,1)S(1)} %convolution_convert_fusion.1), channel_id=1, source_target_pairs={{0,4},{4,0},{8,12},{12,8},{16,20},{20,16},{24,28},{28,24},{1,5},{5... | collective-permute-start | bytes 700424 | tf_op jit(solution)/shard_map/ppermute | solution.py:16
  15.0 11.9 %collective-permute-start.5 = (bf16[456,256]{1,0:T(8,128)(2,1)S(1)}, bf16[456,256]{1,0:T(8,128)(2,1)S(1)}, u32[]{:S(2)}, u32[]{:S(2)}) collective-permute-start(bf16[456,256]{1,0:T(8,128)(2,1)S(1)} %pad_maximum_fusion), channel_id=1, source_target_pairs={{0,4},{4,0},{8,12},{12,8},{16,20},{20,16},{24,28},{28,24},{1,5},{5... | collective-permute-start | bytes 700424 | tf_op jit(solution)/shard_map/ppermute | solution.py:16
  15.4 8.7 %collective-permute-start.4 = (bf16[2,232,256]{2,1,0:T(8,128)(2,1)S(1)}, bf16[2,232,256]{2,1,0:T(8,128)(2,1)S(1)}, u32[]{:S(2)}, u32[]{:S(2)}) collective-permute-start(bf16[2,232,256]{2,1,0:T(8,128)(2,1)S(1)} %convolution_convert_fusion), channel_id=1, source_target_pairs={{0,8},{4,12},{8,0},{12,4},{16,24},{20,28},{24,16},{28,20},{1,9},{5... | collective-permute-start | bytes 712712 | tf_op jit(solution)/shard_map/ppermute | solution.py:121
  21.8 5.2 %collective-permute-start.6 = (bf16[224,256]{1,0:T(8,128)(2,1)S(1)}, bf16[224,256]{1,0:T(8,128)(2,1)S(1)}, u32[]{:S(2)}, u32[]{:S(2)}) collective-permute-start(bf16[224,256]{1,0:T(8,128)(2,1)S(1)} %fusion.2), channel_id=1, source_target_pairs={{0,8},{4,12},{8,0},{12,4},{16,24},{20,28},{24,16},{28,20},{1,9},{5... | collective-permute-start | bytes 344072 | tf_op jit(solution)/shard_map/ppermute | solution.py:121
  23.7 7.6 %collective-permute-start.8 = (bf16[232,256]{1,0:T(8,128)(2,1)S(1)}, bf16[232,256]{1,0:T(8,128)(2,1)S(1)}, u32[]{:S(2)}, u32[]{:S(2)}) collective-permute-start(bf16[232,256]{1,0:T(8,128)(2,1)S(1)} %fusion.1), channel_id=1, source_target_pairs={{0,8},{4,12},{8,0},{12,4},{16,24},{20,28},{24,16},{28,20},{1,9},{5... | collective-permute-start | bytes 356360 | tf_op jit(solution)/shard_map/ppermute | solution.py:121
  24.1 7.1 %collective-permute-start.7 = (bf16[232,256]{1,0:T(8,128)(2,1)S(1)}, bf16[232,256]{1,0:T(8,128)(2,1)S(1)}, u32[]{:S(2)}, u32[]{:S(2)}) collective-permute-start(bf16[232,256]{1,0:T(8,128)(2,1)S(1)} %convolution_convert_fusion.3), channel_id=1, source_target_pairs={{0,4},{4,0},{8,12},{12,8},{16,20},{20,16},{24,28},{28,24},{1,5},{5... | collective-permute-start | bytes 356360 | tf_op jit(solution)/shard_map/ppermute | solution.py:16
  25.9 9.2 %copy-start.1 = (bf16[8192,256]{1,0:T(8,128)(2,1)S(1)}, bf16[8192,256]{1,0:T(8,128)(2,1)}, u32[]{:S(2)}) copy-start(bf16[8192,256]{1,0:T(8,128)(2,1)} %basis.5) | copy-start | bytes 12582916
  26.0 9.2 %copy-start.2 = (f32[1,456,256]{2,1,0:T(8,128)S(1)}, f32[1,456,256]{2,1,0:T(8,128)}, u32[]{:S(2)}) copy-start(f32[1,456,256]{2,1,0:T(8,128)} %param.8) | copy-start | bytes 1400836
  26.0 9.2 %copy-start.3 = (f32[1,456,256]{2,1,0:T(8,128)S(1)}, f32[1,456,256]{2,1,0:T(8,128)}, u32[]{:S(2)}) copy-start(f32[1,456,256]{2,1,0:T(8,128)} %param.9) | copy-start | bytes 1400836
  26.3 8.9 %collective-permute-start.9 = (bf16[456,256]{1,0:T(8,128)(2,1)S(1)}, bf16[456,256]{1,0:T(8,128)(2,1)S(1)}, u32[]{:S(2)}, u32[]{:S(2)}) collective-permute-start(bf16[456,256]{1,0:T(8,128)(2,1)S(1)} %fusion), channel_id=1, source_target_pairs={{0,4},{4,0},{8,12},{12,8},{16,20},{20,16},{24,28},{28,24},{1,5},{5... | collective-permute-start | bytes 700424 | tf_op jit(solution)/shard_map/ppermute | solution.py:16
  27.3 7.9 %collective-permute-start.12 = (bf16[224,256]{1,0:T(8,128)(2,1)S(1)}, bf16[224,256]{1,0:T(8,128)(2,1)S(1)}, u32[]{:S(2)}, u32[]{:S(2)}) collective-permute-start(bf16[224,256]{1,0:T(8,128)(2,1)S(1)} %add_convert_fusion.2), channel_id=1, source_target_pairs={{0,24},{4,28},{8,16},{12,20},{16,8},{20,12},{24,0},{28,4},{1,25},{... | collective-permute-start | bytes 344072 | tf_op jit(solution)/shard_map/ppermute | solution.py:121
  31.0 6.7 %collective-permute-start.10 = (bf16[232,256]{1,0:T(8,128)(2,1)S(1)}, bf16[232,256]{1,0:T(8,128)(2,1)S(1)}, u32[]{:S(2)}, u32[]{:S(2)}) collective-permute-start(bf16[232,256]{1,0:T(8,128)(2,1)S(1)} %add_convert_fusion.1), channel_id=1, source_target_pairs={{0,8},{4,12},{8,0},{12,4},{16,24},{20,28},{24,16},{28,20},{1,9},{5... | collective-permute-start | bytes 356360 | tf_op jit(solution)/shard_map/ppermute | solution.py:121
  31.3 6.9 %collective-permute-start.11 = (bf16[232,256]{1,0:T(8,128)(2,1)S(1)}, bf16[232,256]{1,0:T(8,128)(2,1)S(1)}, u32[]{:S(2)}, u32[]{:S(2)}) collective-permute-start(bf16[232,256]{1,0:T(8,128)(2,1)S(1)} %add_convert_fusion), channel_id=1, source_target_pairs={{0,24},{4,28},{8,16},{12,20},{16,8},{20,12},{24,0},{28,4},{1,25},{... | collective-permute-start | bytes 356360 | tf_op jit(solution)/shard_map/ppermute | solution.py:121

commit v6 on v5

--- a/solution.py
+++ b/solution.py
@@ -139,11 +139,16 @@
     )
     got31 = pair(got31)
 
-    sums = [(term(z ^ 2, x, coded, cut) + piece(got2, cut)).astype(BF) for cut in cuts]
-    code, sums = lax.optimization_barrier((coded, sums))
-    passed = [hop(part, 1) for part in sums]
+    def near_sum(cut, code):
+        value = (term(z ^ 2, x, code, cut) + piece(got2, cut)).astype(BF)
+        return lax.optimization_barrier((code, value))
+
+    code, sum_a = near_sum(first, coded)
+    passed = [hop(sum_a, 1)]
     out3 = term(z ^ 3, 1 - x, code, second).astype(BF)
     code, out3, near1 = lax.optimization_barrier((code, out3, near1))
+    code, sum_b = near_sum(second, code)
+    passed.append(hop(sum_b, 1))
     got3 = pair(out3)
     near1 = near1[:, : first[1]]
     own_in = (term(z, 1 - x, code) + padded(parity(near1, 1 - x))).astype(BF)

time: 41 us -> 41.6 us (1.015)
  waiting for transfers between devices: 10.5 us -> 11 us
    ppermute x6, waiting for transfers between devices: 1.07 us -> 1.61 us  [hop(): return lax.ppermute(value.astype(BF), 'dp', full)]
where the time goes in v6:
time: 41.6 us; the launch traced here: 41.5 us
  starting transfers between devices  18.6 us (45%)
  waiting for transfers between devices  11 us (26%)
  Pallas kernels  7.65 us (18%)
  matrix products  2.94 us (7%)
  between operations  0.98 us (2%)
    ppermute x6, starting transfers between devices, hop(): return lax.ppermute(value.astype(BF), 'dp', full)  10.8 us
    ppermute x7, waiting for transfers between devices, swap(): return lax.ppermute(value, axis, [(i, i ^ bit) for i in range(count)])  9.43 us
    ppermute x7, starting transfers between devices, swap(): return lax.ppermute(value, axis, [(i, i ^ bit) for i in range(count)])  7.71 us
    pallas_call x2, Pallas kernels, adam_update(): pl.pallas_call(functools.partial(adam_update_kernel, cut, len(terms), len...  5.11 us
    dot_general x12, matrix products, term(): return jnp.dot(part, code, preferred_element_type=F32)  2.67 us
    pallas_call x1, Pallas kernels, partial_code(): pl.pallas_call(partial_code_kernel, out_shape=(jax.ShapeDtypeStruct((rows...  2.55 us
    ppermute x6, waiting for transfers between devices, hop(): return lax.ppermute(value.astype(BF), 'dp', full)  1.61 us
  transfers between devices with their start and end apart: 13, of which 7 were waited for; matrix products, arithmetic and copies ran while one was open for 6% of the time, Pallas kernels for 6%

profile of v6, /device:TPU:0, one launch (start us, length us, event | category | flops | bytes accessed | tf_op | source)
XLA Modules:
  0.0 41.5 jit_solution(12349874032432588155)
XLA Ops:
  0.6 2.5 %partial_code.1 = (f32[192,256]{1,0:T(8,128)S(1)}, bf16[192,256]{1,0:T(8,128)(2,1)S(1)}) custom-call(bf16[384,2048]{1,0:T(8,128)(2,1)} %activations.1, bf16[8192,256]{1,0:T(8,128)(2,1)} %basis.5), custom_call_target="tpu_custom_call" | custom-call | flops 402653184 | bytes 2621440 | tf_op jit(solution)/shard_map/partial_code/pallas_call | solution.py:58
  3.2 0.5 %collective-permute-start = (bf16[192,256]{1,0:T(8,128)(2,1)S(1)}, bf16[192,256]{1,0:T(8,128)(2,1)S(1)}, u32[]{:S(2)}, u32[]{:S(2)}) collective-permute-start(bf16[192,256]{1,0:T(8,128)(2,1)S(1)} %get-tuple-element.29), channel_id=1, source_target_pairs={{0,1},{1,0},{2,3},{3,2},{4,5},{5,4},{6,7},{7,6},{8,9},{9,8},{10,11... | collective-permute-start | bytes 294920 | tf_op jit(solution)/shard_map/ppermute | solution.py:16
  3.7 0.9 %collective-permute-done = bf16[192,256]{1,0:T(8,128)(2,1)S(1)} collective-permute-done((bf16[192,256]{1,0:T(8,128)(2,1)S(1)}, bf16[192,256]{1,0:T(8,128)(2,1)S(1)}, u32[]{:S(2)}, u32[]{:S(2)}) %collective-permute-start) | collective-permute-done | bytes 98336 | tf_op jit(solution)/shard_map/ppermute | solution.py:16
  4.7 2.9 %collective-permute-start.1 = (bf16[192,256]{1,0:T(8,128)(2,1)S(1)}, bf16[192,256]{1,0:T(8,128)(2,1)S(1)}, u32[]{:S(2)}, u32[]{:S(2)}) collective-permute-start(bf16[192,256]{1,0:T(8,128)(2,1)S(1)} %fusion.23), channel_id=1, source_target_pairs={{0,2},{1,3},{2,0},{3,1},{4,6},{5,7},{6,4},{7,5},{8,10},{9,11},{10,... | collective-permute-start | bytes 294920 | tf_op jit(solution)/shard_map/ppermute | solution.py:16
  7.6 3.1 %collective-permute-done.1 = bf16[192,256]{1,0:T(8,128)(2,1)S(1)} collective-permute-done((bf16[192,256]{1,0:T(8,128)(2,1)S(1)}, bf16[192,256]{1,0:T(8,128)(2,1)S(1)}, u32[]{:S(2)}, u32[]{:S(2)}) %collective-permute-start.1) | collective-permute-done | bytes 98336 | tf_op jit(solution)/shard_map/ppermute | solution.py:16
  11.0 1.2 %collective-permute-done.2 = bf16[192,256]{1,0:T(8,128)(2,1)S(1)} collective-permute-done((bf16[192,256]{1,0:T(8,128)(2,1)S(1)}, bf16[192,256]{1,0:T(8,128)(2,1)S(1)}, u32[]{:S(2)}, u32[]{:S(2)}) %collective-permute-start.2) | collective-permute-done | bytes 98336 | tf_op jit(solution)/shard_map/ppermute | solution.py:16
  12.2 0.3 convolution_convert_fusion.1
  12.5 0.3 convolution_convert_fusion
  12.8 1.8 %collective-permute-start.3 = (bf16[456,256]{1,0:T(8,128)(2,1)S(1)}, bf16[456,256]{1,0:T(8,128)(2,1)S(1)}, u32[]{:S(2)}, u32[]{:S(2)}) collective-permute-start(bf16[456,256]{1,0:T(8,128)(2,1)S(1)} %convolution_convert_fusion.1), channel_id=1, source_target_pairs={{0,4},{4,0},{8,12},{12,8},{16,20},{20,16},{24,28},{28,24},{1,5},{5... | collective-permute-start | bytes 700424 | tf_op jit(solution)/shard_map/ppermute | solution.py:16
  14.6 0.2 convolution_convert_fusion.2
  14.8 0.2 convolution_convert_fusion.4
  15.0 0.4 collective-permute-start.5
  15.4 1.8 %collective-permute-start.4 = (bf16[2,232,256]{2,1,0:T(8,128)(2,1)S(1)}, bf16[2,232,256]{2,1,0:T(8,128)(2,1)S(1)}, u32[]{:S(2)}, u32[]{:S(2)}) collective-permute-start(bf16[2,232,256]{2,1,0:T(8,128)(2,1)S(1)} %convolution_convert_fusion), channel_id=1, source_target_pairs={{0,8},{4,12},{8,0},{12,4},{16,24},{20,28},{24,16},{28,20},{1,9},{5... | collective-permute-start | bytes 712712 | tf_op jit(solution)/shard_map/ppermute | solution.py:121
  17.2 4.2 %collective-permute-done.3 = bf16[456,256]{1,0:T(8,128)(2,1)S(1)} collective-permute-done((bf16[456,256]{1,0:T(8,128)(2,1)S(1)}, bf16[456,256]{1,0:T(8,128)(2,1)S(1)}, u32[]{:S(2)}, u32[]{:S(2)}) %collective-permute-start.3) | collective-permute-done | bytes 233504 | tf_op jit(solution)/shard_map/ppermute | solution.py:16
  21.4 0.2 fusion.2
  21.6 1.9 %collective-permute-start.6 = (bf16[224,256]{1,0:T(8,128)(2,1)S(1)}, bf16[224,256]{1,0:T(8,128)(2,1)S(1)}, u32[]{:S(2)}, u32[]{:S(2)}) collective-permute-start(bf16[224,256]{1,0:T(8,128)(2,1)S(1)} %fusion.2), channel_id=1, source_target_pairs={{0,8},{4,12},{8,0},{12,4},{16,24},{20,28},{24,16},{28,20},{1,9},{5... | collective-permute-start | bytes 344072 | tf_op jit(solution)/shard_map/ppermute | solution.py:121
  23.5 0.2 convolution_convert_fusion.3
  23.7 0.2 fusion.1
  24.0 0.3 fusion
  24.3 0.8 %collective-permute-start.8 = (bf16[232,256]{1,0:T(8,128)(2,1)S(1)}, bf16[232,256]{1,0:T(8,128)(2,1)S(1)}, u32[]{:S(2)}, u32[]{:S(2)}) collective-permute-start(bf16[232,256]{1,0:T(8,128)(2,1)S(1)} %fusion.1), channel_id=1, source_target_pairs={{0,8},{4,12},{8,0},{12,4},{16,24},{20,28},{24,16},{28,20},{1,9},{5... | collective-permute-start | bytes 356360 | tf_op jit(solution)/shard_map/ppermute | solution.py:121
  25.1 1.5 %collective-permute-start.7 = (bf16[232,256]{1,0:T(8,128)(2,1)S(1)}, bf16[232,256]{1,0:T(8,128)(2,1)S(1)}, u32[]{:S(2)}, u32[]{:S(2)}) collective-permute-start(bf16[232,256]{1,0:T(8,128)(2,1)S(1)} %convolution_convert_fusion.3), channel_id=1, source_target_pairs={{0,4},{4,0},{8,12},{12,8},{16,20},{20,16},{24,28},{28,24},{1,5},{5... | collective-permute-start | bytes 356360 | tf_op jit(solution)/shard_map/ppermute | solution.py:16
  26.6 0.5 %collective-permute-start.9 = (bf16[456,256]{1,0:T(8,128)(2,1)S(1)}, bf16[456,256]{1,0:T(8,128)(2,1)S(1)}, u32[]{:S(2)}, u32[]{:S(2)}) collective-permute-start(bf16[456,256]{1,0:T(8,128)(2,1)S(1)} %fusion), channel_id=1, source_target_pairs={{0,4},{4,0},{8,12},{12,8},{16,20},{20,16},{24,28},{28,24},{1,5},{5... | collective-permute-start | bytes 700424 | tf_op jit(solution)/shard_map/ppermute | solution.py:16
  27.4 0.3 collective-permute-done.6
  27.7 0.2 add_convert_fusion.1
  27.9 3.3 %collective-permute-start.12 = (bf16[224,256]{1,0:T(8,128)(2,1)S(1)}, bf16[224,256]{1,0:T(8,128)(2,1)S(1)}, u32[]{:S(2)}, u32[]{:S(2)}) collective-permute-start(bf16[224,256]{1,0:T(8,128)(2,1)S(1)} %add_convert_fusion.2), channel_id=1, source_target_pairs={{0,24},{4,28},{8,16},{12,20},{16,8},{20,12},{24,0},{28,4},{1,25},{... | collective-permute-start | bytes 344072 | tf_op jit(solution)/shard_map/ppermute | solution.py:121
  31.3 0.2 fusion.7
  31.6 3.0 %collective-permute-start.11 = (bf16[232,256]{1,0:T(8,128)(2,1)S(1)}, bf16[232,256]{1,0:T(8,128)(2,1)S(1)}, u32[]{:S(2)}, u32[]{:S(2)}) collective-permute-start(bf16[232,256]{1,0:T(8,128)(2,1)S(1)} %add_convert_fusion), channel_id=1, source_target_pairs={{0,24},{4,28},{8,16},{12,20},{16,8},{20,12},{24,0},{28,4},{1,25},{... | collective-permute-start | bytes 356360 | tf_op jit(solution)/shard_map/ppermute | solution.py:121
  34.6 0.2 fusion.16.own
  35.0 1.1 %collective-permute-done.12.refs_0_ = bf16[224,256]{1,0:T(8,128)(2,1)S(1)} collective-permute-done((bf16[224,256]{1,0:T(8,128)(2,1)S(1)}, bf16[224,256]{1,0:T(8,128)(2,1)S(1)}, u32[]{:S(2)}, u32[]{:S(2)}) %collective-permute-start.12) | collective-permute-done | bytes 114720 | tf_op jit(solution)/shard_map/ppermute | solution.py:121
  36.1 2.5 %adam_update.2 = (f32[456,256]{1,0:T(8,128)}, f32[456,256]{1,0:T(8,128)}, bf16[456,8192]{1,0:T(8,128)(2,1)}) custom-call(f32[224,256]{1,0:T(8,128)S(1)} %convolution_add_fusion.2.own, bf16[456,256]{1,0:T(8,128)(2,1)S(1)} %collective-permute-done.9.got, f32[456,256]{1,0:T(8,128)S(1)} %bitcast.29, f32[456,256]{1,0:T(8,128)S(1)} %bitcast.31, ...), custom_call_target="tpu_custom_call" | custom-call | flops 939524096 | bytes 7864320 | tf_op jit(solution)/shard_map/adam_update/pallas_call | solution.py:225
  38.7 0.2 collective-permute-done.11.refs_1_
  38.9 2.6 %adam_update.3 = (f32[456,256]{1,0:T(8,128)}, f32[456,256]{1,0:T(8,128)}, bf16[456,8192]{1,0:T(8,128)(2,1)}) custom-call(f32[232,256]{1,0:T(8,128)S(1)} %fusion.16.own, bf16[456,256]{1,0:T(8,128)(2,1)S(1)} %collective-permute-done.9.got, f32[456,256]{1,0:T(8,128)S(1)} %bitcast.30, ...), custom_call_target="tpu_custom_call", output_to_operand_aliasing={{0}: (7, {}), {1}: (8, {}), {2}: (9, {})} | custom-call | flops 973078528 | bytes 7995392 | tf_op jit(solution)/shard_map/adam_update/pallas_call | solution.py:225
  (26 shorter events, 0.8 us)
Async XLA Ops:
  0.6 11.6 %copy-start = (bf16[384,3648]{0,1:T(8,128)(2,1)S(1)}, bf16[384,3648]{0,1:T(8,128)(2,1)}, u32[]{:S(2)}) copy-start(bf16[384,3648]{0,1:T(8,128)(2,1)} %param.7) | copy-start | bytes 8404996
  3.2 1.5 %collective-permute-start = (bf16[192,256]{1,0:T(8,128)(2,1)S(1)}, bf16[192,256]{1,0:T(8,128)(2,1)S(1)}, u32[]{:S(2)}, u32[]{:S(2)}) collective-permute-start(bf16[192,256]{1,0:T(8,128)(2,1)S(1)} %get-tuple-element.29), channel_id=1, source_target_pairs={{0,1},{1,0},{2,3},{3,2},{4,5},{5,4},{6,7},{7,6},{8,9},{9,8},{10,11... | collective-permute-start | bytes 294920 | tf_op jit(solution)/shard_map/ppermute | solution.py:16
  4.7 6.0 %collective-permute-start.1 = (bf16[192,256]{1,0:T(8,128)(2,1)S(1)}, bf16[192,256]{1,0:T(8,128)(2,1)S(1)}, u32[]{:S(2)}, u32[]{:S(2)}) collective-permute-start(bf16[192,256]{1,0:T(8,128)(2,1)S(1)} %fusion.23), channel_id=1, source_target_pairs={{0,2},{1,3},{2,0},{3,1},{4,6},{5,7},{6,4},{7,5},{8,10},{9,11},{10,... | collective-permute-start | bytes 294920 | tf_op jit(solution)/shard_map/ppermute | solution.py:16
  10.8 1.4 %collective-permute-start.2 = (bf16[192,256]{1,0:T(8,128)(2,1)S(1)}, bf16[192,256]{1,0:T(8,128)(2,1)S(1)}, u32[]{:S(2)}, u32[]{:S(2)}) collective-permute-start(bf16[192,256]{1,0:T(8,128)(2,1)S(1)} %add_convert_fusion.3), channel_id=1, source_target_pairs={{0,1},{1,0},{2,3},{3,2},{4,5},{5,4},{6,7},{7,6},{8,9},{9,8},{10,11... | collective-permute-start | bytes 294920 | tf_op jit(solution)/shard_map/ppermute | solution.py:16
  12.8 8.6 %collective-permute-start.3 = (bf16[456,256]{1,0:T(8,128)(2,1)S(1)}, bf16[456,256]{1,0:T(8,128)(2,1)S(1)}, u32[]{:S(2)}, u32[]{:S(2)}) collective-permute-start(bf16[456,256]{1,0:T(8,128)(2,1)S(1)} %convolution_convert_fusion.1), channel_id=1, source_target_pairs={{0,4},{4,0},{8,12},{12,8},{16,20},{20,16},{24,28},{28,24},{1,5},{5... | collective-permute-start | bytes 700424 | tf_op jit(solution)/shard_map/ppermute | solution.py:16
  15.0 12.3 %collective-permute-start.5 = (bf16[456,256]{1,0:T(8,128)(2,1)S(1)}, bf16[456,256]{1,0:T(8,128)(2,1)S(1)}, u32[]{:S(2)}, u32[]{:S(2)}) collective-permute-start(bf16[456,256]{1,0:T(8,128)(2,1)S(1)} %pad_maximum_fusion), channel_id=1, source_target_pairs={{0,4},{4,0},{8,12},{12,8},{16,20},{20,16},{24,28},{28,24},{1,5},{5... | collective-permute-start | bytes 700424 | tf_op jit(solution)/shard_map/ppermute | solution.py:16
  15.4 8.3 %collective-permute-start.4 = (bf16[2,232,256]{2,1,0:T(8,128)(2,1)S(1)}, bf16[2,232,256]{2,1,0:T(8,128)(2,1)S(1)}, u32[]{:S(2)}, u32[]{:S(2)}) collective-permute-start(bf16[2,232,256]{2,1,0:T(8,128)(2,1)S(1)} %convolution_convert_fusion), channel_id=1, source_target_pairs={{0,8},{4,12},{8,0},{12,4},{16,24},{20,28},{24,16},{28,20},{1,9},{5... | collective-permute-start | bytes 712712 | tf_op jit(solution)/shard_map/ppermute | solution.py:121
  21.6 6.1 %collective-permute-start.6 = (bf16[224,256]{1,0:T(8,128)(2,1)S(1)}, bf16[224,256]{1,0:T(8,128)(2,1)S(1)}, u32[]{:S(2)}, u32[]{:S(2)}) collective-permute-start(bf16[224,256]{1,0:T(8,128)(2,1)S(1)} %fusion.2), channel_id=1, source_target_pairs={{0,8},{4,12},{8,0},{12,4},{16,24},{20,28},{24,16},{28,20},{1,9},{5... | collective-permute-start | bytes 344072 | tf_op jit(solution)/shard_map/ppermute | solution.py:121
  23.9 12.2 %copy-start.1 = (bf16[8192,256]{1,0:T(8,128)(2,1)S(1)}, bf16[8192,256]{1,0:T(8,128)(2,1)}, u32[]{:S(2)}) copy-start(bf16[8192,256]{1,0:T(8,128)(2,1)} %basis.5) | copy-start | bytes 12582916
  23.9 12.2 %copy-start.2 = (f32[1,456,256]{2,1,0:T(8,128)S(1)}, f32[1,456,256]{2,1,0:T(8,128)}, u32[]{:S(2)}) copy-start(f32[1,456,256]{2,1,0:T(8,128)} %param.8) | copy-start | bytes 1400836
  24.0 12.2 %copy-start.3 = (f32[1,456,256]{2,1,0:T(8,128)S(1)}, f32[1,456,256]{2,1,0:T(8,128)}, u32[]{:S(2)}) copy-start(f32[1,456,256]{2,1,0:T(8,128)} %param.9) | copy-start | bytes 1400836
  24.3 7.2 %collective-permute-start.8 = (bf16[232,256]{1,0:T(8,128)(2,1)S(1)}, bf16[232,256]{1,0:T(8,128)(2,1)S(1)}, u32[]{:S(2)}, u32[]{:S(2)}) collective-permute-start(bf16[232,256]{1,0:T(8,128)(2,1)S(1)} %fusion.1), channel_id=1, source_target_pairs={{0,8},{4,12},{8,0},{12,4},{16,24},{20,28},{24,16},{28,20},{1,9},{5... | collective-permute-start | bytes 356360 | tf_op jit(solution)/shard_map/ppermute | solution.py:121
  25.1 6.4 %collective-permute-start.7 = (bf16[232,256]{1,0:T(8,128)(2,1)S(1)}, bf16[232,256]{1,0:T(8,128)(2,1)S(1)}, u32[]{:S(2)}, u32[]{:S(2)}) collective-permute-start(bf16[232,256]{1,0:T(8,128)(2,1)S(1)} %convolution_convert_fusion.3), channel_id=1, source_target_pairs={{0,4},{4,0},{8,12},{12,8},{16,20},{20,16},{24,28},{28,24},{1,5},{5... | collective-permute-start | bytes 356360 | tf_op jit(solution)/shard_map/ppermute | solution.py:16
  26.6 9.5 %collective-permute-start.9 = (bf16[456,256]{1,0:T(8,128)(2,1)S(1)}, bf16[456,256]{1,0:T(8,128)(2,1)S(1)}, u32[]{:S(2)}, u32[]{:S(2)}) collective-permute-start(bf16[456,256]{1,0:T(8,128)(2,1)S(1)} %fusion), channel_id=1, source_target_pairs={{0,4},{4,0},{8,12},{12,8},{16,20},{20,16},{24,28},{28,24},{1,5},{5... | collective-permute-start | bytes 700424 | tf_op jit(solution)/shard_map/ppermute | solution.py:16
  27.9 8.1 %collective-permute-start.12 = (bf16[224,256]{1,0:T(8,128)(2,1)S(1)}, bf16[224,256]{1,0:T(8,128)(2,1)S(1)}, u32[]{:S(2)}, u32[]{:S(2)}) collective-permute-start(bf16[224,256]{1,0:T(8,128)(2,1)S(1)} %add_convert_fusion.2), channel_id=1, source_target_pairs={{0,24},{4,28},{8,16},{12,20},{16,8},{20,12},{24,0},{28,4},{1,25},{... | collective-permute-start | bytes 344072 | tf_op jit(solution)/shard_map/ppermute | solution.py:121
  31.3 7.4 %collective-permute-start.10 = (bf16[232,256]{1,0:T(8,128)(2,1)S(1)}, bf16[232,256]{1,0:T(8,128)(2,1)S(1)}, u32[]{:S(2)}, u32[]{:S(2)}) collective-permute-start(bf16[232,256]{1,0:T(8,128)(2,1)S(1)} %add_convert_fusion.1), channel_id=1, source_target_pairs={{0,8},{4,12},{8,0},{12,4},{16,24},{20,28},{24,16},{28,20},{1,9},{5... | collective-permute-start | bytes 356360 | tf_op jit(solution)/shard_map/ppermute | solution.py:121
  31.6 7.3 %collective-permute-start.11 = (bf16[232,256]{1,0:T(8,128)(2,1)S(1)}, bf16[232,256]{1,0:T(8,128)(2,1)S(1)}, u32[]{:S(2)}, u32[]{:S(2)}) collective-permute-start(bf16[232,256]{1,0:T(8,128)(2,1)S(1)} %add_convert_fusion), channel_id=1, source_target_pairs={{0,24},{4,28},{8,16},{12,20},{16,8},{20,12},{24,0},{28,4},{1,25},{... | collective-permute-start | bytes 356360 | tf_op jit(solution)/shard_map/ppermute | solution.py:121

commit v7 on v5

--- a/solution.py
+++ b/solution.py
@@ -158,6 +158,7 @@
 
     code, total_a = total(z ^ 3, first, code, got31[:n_first], passed[0])
     far_a = hop(total_a, 3)
+    code, got31, passed[1] = lax.optimization_barrier((code, got31, passed[1]))
     code, late = total(z ^ 1, second, code, got31[n_first:])
     late = hop(late, 1)
     code, total_b = total(z ^ 3, second, code, got3, passed[1])

time: 41 us -> 41 us (level)
  no operation moved by 1% of the time
where the time goes in v7:
time: 41 us; the launch traced here: 40.8 us
  starting transfers between devices  18.4 us (45%)
  waiting for transfers between devices  10.5 us (26%)
  Pallas kernels  7.65 us (19%)
  matrix products  2.94 us (7%)
  between operations  0.98 us (2%)
    ppermute x6, starting transfers between devices, hop(): return lax.ppermute(value.astype(BF), 'dp', full)  10.6 us
    ppermute x7, waiting for transfers between devices, swap(): return lax.ppermute(value, axis, [(i, i ^ bit) for i in range(count)])  9.43 us
    ppermute x7, starting transfers between devices, swap(): return lax.ppermute(value, axis, [(i, i ^ bit) for i in range(count)])  7.84 us
    pallas_call x2, Pallas kernels, adam_update(): pl.pallas_call(functools.partial(adam_update_kernel, cut, len(terms), len...  5.1 us
    dot_general x12, matrix products, term(): return jnp.dot(part, code, preferred_element_type=F32)  2.67 us
    pallas_call x1, Pallas kernels, partial_code(): pl.pallas_call(partial_code_kernel, out_shape=(jax.ShapeDtypeStruct((rows...  2.55 us
    ppermute x6, waiting for transfers between devices, hop(): return lax.ppermute(value.astype(BF), 'dp', full)  1.07 us
  transfers between devices with their start and end apart: 13, of which 7 were waited for; matrix products, arithmetic and copies ran while one was open for 6% of the time, Pallas kernels for 6%

profile of v7, /device:TPU:0, one launch (start us, length us, event | category | flops | bytes accessed | tf_op | source)
XLA Modules:
  0.0 40.8 jit_solution(6122838830726605508)
XLA Ops:
  0.6 2.5 %partial_code.1 = (f32[192,256]{1,0:T(8,128)S(1)}, bf16[192,256]{1,0:T(8,128)(2,1)S(1)}) custom-call(bf16[384,2048]{1,0:T(8,128)(2,1)} %activations.1, bf16[8192,256]{1,0:T(8,128)(2,1)} %basis.5), custom_call_target="tpu_custom_call" | custom-call | flops 402653184 | bytes 2621440 | tf_op jit(solution)/shard_map/partial_code/pallas_call | solution.py:58
  3.2 0.5 %collective-permute-start = (bf16[192,256]{1,0:T(8,128)(2,1)S(1)}, bf16[192,256]{1,0:T(8,128)(2,1)S(1)}, u32[]{:S(2)}, u32[]{:S(2)}) collective-permute-start(bf16[192,256]{1,0:T(8,128)(2,1)S(1)} %get-tuple-element.31), channel_id=1, source_target_pairs={{0,1},{1,0},{2,3},{3,2},{4,5},{5,4},{6,7},{7,6},{8,9},{9,8},{10,11... | collective-permute-start | bytes 294920 | tf_op jit(solution)/shard_map/ppermute | solution.py:16
  3.7 0.9 %collective-permute-done = bf16[192,256]{1,0:T(8,128)(2,1)S(1)} collective-permute-done((bf16[192,256]{1,0:T(8,128)(2,1)S(1)}, bf16[192,256]{1,0:T(8,128)(2,1)S(1)}, u32[]{:S(2)}, u32[]{:S(2)}) %collective-permute-start) | collective-permute-done | bytes 98336 | tf_op jit(solution)/shard_map/ppermute | solution.py:16
  4.7 2.9 %collective-permute-start.1 = (bf16[192,256]{1,0:T(8,128)(2,1)S(1)}, bf16[192,256]{1,0:T(8,128)(2,1)S(1)}, u32[]{:S(2)}, u32[]{:S(2)}) collective-permute-start(bf16[192,256]{1,0:T(8,128)(2,1)S(1)} %fusion.21), channel_id=1, source_target_pairs={{0,2},{1,3},{2,0},{3,1},{4,6},{5,7},{6,4},{7,5},{8,10},{9,11},{10,... | collective-permute-start | bytes 294920 | tf_op jit(solution)/shard_map/ppermute | solution.py:16
  7.6 3.1 %collective-permute-done.1 = bf16[192,256]{1,0:T(8,128)(2,1)S(1)} collective-permute-done((bf16[192,256]{1,0:T(8,128)(2,1)S(1)}, bf16[192,256]{1,0:T(8,128)(2,1)S(1)}, u32[]{:S(2)}, u32[]{:S(2)}) %collective-permute-start.1) | collective-permute-done | bytes 98336 | tf_op jit(solution)/shard_map/ppermute | solution.py:16
  11.0 1.2 %collective-permute-done.2 = bf16[192,256]{1,0:T(8,128)(2,1)S(1)} collective-permute-done((bf16[192,256]{1,0:T(8,128)(2,1)S(1)}, bf16[192,256]{1,0:T(8,128)(2,1)S(1)}, u32[]{:S(2)}, u32[]{:S(2)}) %collective-permute-start.2) | collective-permute-done | bytes 98336 | tf_op jit(solution)/shard_map/ppermute | solution.py:16
  12.2 0.3 convolution_convert_fusion.1
  12.5 0.3 convolution_convert_fusion
  12.8 1.8 %collective-permute-start.3 = (bf16[456,256]{1,0:T(8,128)(2,1)S(1)}, bf16[456,256]{1,0:T(8,128)(2,1)S(1)}, u32[]{:S(2)}, u32[]{:S(2)}) collective-permute-start(bf16[456,256]{1,0:T(8,128)(2,1)S(1)} %convolution_convert_fusion.1), channel_id=1, source_target_pairs={{0,4},{4,0},{8,12},{12,8},{16,20},{20,16},{24,28},{28,24},{1,5},{5... | collective-permute-start | bytes 700424 | tf_op jit(solution)/shard_map/ppermute | solution.py:16
  14.6 0.2 convolution_convert_fusion.2
  14.8 0.2 convolution_convert_fusion.4
  15.0 0.4 collective-permute-start.5
  15.4 1.8 %collective-permute-start.4 = (bf16[2,232,256]{2,1,0:T(8,128)(2,1)S(1)}, bf16[2,232,256]{2,1,0:T(8,128)(2,1)S(1)}, u32[]{:S(2)}, u32[]{:S(2)}) collective-permute-start(bf16[2,232,256]{2,1,0:T(8,128)(2,1)S(1)} %convolution_convert_fusion), channel_id=1, source_target_pairs={{0,8},{4,12},{8,0},{12,4},{16,24},{20,28},{24,16},{28,20},{1,9},{5... | collective-permute-start | bytes 712712 | tf_op jit(solution)/shard_map/ppermute | solution.py:121
  17.2 4.2 %collective-permute-done.3 = bf16[456,256]{1,0:T(8,128)(2,1)S(1)} collective-permute-done((bf16[456,256]{1,0:T(8,128)(2,1)S(1)}, bf16[456,256]{1,0:T(8,128)(2,1)S(1)}, u32[]{:S(2)}, u32[]{:S(2)}) %collective-permute-start.3) | collective-permute-done | bytes 233504 | tf_op jit(solution)/shard_map/ppermute | solution.py:16
  21.4 0.2 fusion.1
  21.6 0.2 fusion.3
  21.8 1.9 %collective-permute-start.6 = (bf16[224,256]{1,0:T(8,128)(2,1)S(1)}, bf16[224,256]{1,0:T(8,128)(2,1)S(1)}, u32[]{:S(2)}, u32[]{:S(2)}) collective-permute-start(bf16[224,256]{1,0:T(8,128)(2,1)S(1)} %fusion.3), channel_id=1, source_target_pairs={{0,8},{4,12},{8,0},{12,4},{16,24},{20,28},{24,16},{28,20},{1,9},{5... | collective-permute-start | bytes 344072 | tf_op jit(solution)/shard_map/ppermute | solution.py:121
  23.7 0.2 collective-permute-start.7
  23.9 0.2 convolution_convert_fusion.3
  24.1 1.8 %collective-permute-start.8 = (bf16[232,256]{1,0:T(8,128)(2,1)S(1)}, bf16[232,256]{1,0:T(8,128)(2,1)S(1)}, u32[]{:S(2)}, u32[]{:S(2)}) collective-permute-start(bf16[232,256]{1,0:T(8,128)(2,1)S(1)} %convolution_convert_fusion.3), channel_id=1, source_target_pairs={{0,4},{4,0},{8,12},{12,8},{16,20},{20,16},{24,28},{28,24},{1,5},{5... | collective-permute-start | bytes 356360 | tf_op jit(solution)/shard_map/ppermute | solution.py:16
  26.0 0.3 fusion
  26.3 0.4 collective-permute-start.9
  26.7 0.2 fusion.18
  27.1 3.7 %collective-permute-start.12 = (bf16[224,256]{1,0:T(8,128)(2,1)S(1)}, bf16[224,256]{1,0:T(8,128)(2,1)S(1)}, u32[]{:S(2)}, u32[]{:S(2)}) collective-permute-start(bf16[224,256]{1,0:T(8,128)(2,1)S(1)} %add_convert_fusion.1), channel_id=1, source_target_pairs={{0,24},{4,28},{8,16},{12,20},{16,8},{20,12},{24,0},{28,4},{1,25},{... | collective-permute-start | bytes 344072 | tf_op jit(solution)/shard_map/ppermute | solution.py:121
  30.8 0.2 fusion.2
  31.1 0.2 fusion.8
  31.4 2.9 %collective-permute-start.11 = (bf16[232,256]{1,0:T(8,128)(2,1)S(1)}, bf16[232,256]{1,0:T(8,128)(2,1)S(1)}, u32[]{:S(2)}, u32[]{:S(2)}) collective-permute-start(bf16[232,256]{1,0:T(8,128)(2,1)S(1)} %add_convert_fusion), channel_id=1, source_target_pairs={{0,24},{4,28},{8,16},{12,20},{16,8},{20,12},{24,0},{28,4},{1,25},{... | collective-permute-start | bytes 356360 | tf_op jit(solution)/shard_map/ppermute | solution.py:121
  34.3 0.2 fusion.14.own
  34.7 0.3 collective-permute-done.12.refs_0_
  35.1 2.5 %adam_update.2 = (f32[456,256]{1,0:T(8,128)}, f32[456,256]{1,0:T(8,128)}, bf16[456,8192]{1,0:T(8,128)(2,1)}) custom-call(f32[224,256]{1,0:T(8,128)S(1)} %convolution_add_fusion.3.own, bf16[456,256]{1,0:T(8,128)(2,1)S(1)} %collective-permute-done.9.got, f32[456,256]{1,0:T(8,128)S(1)} %bitcast.29, f32[456,256]{1,0:T(8,128)S(1)} %bitcast.31, ...), custom_call_target="tpu_custom_call" | custom-call | flops 939524096 | bytes 7864320 | tf_op jit(solution)/shard_map/adam_update/pallas_call | solution.py:221
  37.6 0.6 %collective-permute-done.11.refs_1_ = bf16[232,256]{1,0:T(8,128)(2,1)S(1)} collective-permute-done((bf16[232,256]{1,0:T(8,128)(2,1)S(1)}, bf16[232,256]{1,0:T(8,128)(2,1)S(1)}, u32[]{:S(2)}, u32[]{:S(2)}) %collective-permute-start.11) | collective-permute-done | bytes 118816 | tf_op jit(solution)/shard_map/ppermute | solution.py:121
  38.2 2.6 %adam_update.3 = (f32[456,256]{1,0:T(8,128)}, f32[456,256]{1,0:T(8,128)}, bf16[456,8192]{1,0:T(8,128)(2,1)}) custom-call(f32[232,256]{1,0:T(8,128)S(1)} %fusion.14.own, bf16[456,256]{1,0:T(8,128)(2,1)S(1)} %collective-permute-done.9.got, f32[456,256]{1,0:T(8,128)S(1)} %bitcast.30, ...), custom_call_target="tpu_custom_call", output_to_operand_aliasing={{0}: (7, {}), {1}: (8, {}), {2}: (9, {})} | custom-call | flops 973078528 | bytes 7995392 | tf_op jit(solution)/shard_map/adam_update/pallas_call | solution.py:221
  (26 shorter events, 0.8 us)
Async XLA Ops:
  0.6 11.6 %copy-start = (bf16[384,3648]{0,1:T(8,128)(2,1)S(1)}, bf16[384,3648]{0,1:T(8,128)(2,1)}, u32[]{:S(2)}) copy-start(bf16[384,3648]{0,1:T(8,128)(2,1)} %param.7) | copy-start | bytes 8404996
  3.2 1.5 %collective-permute-start = (bf16[192,256]{1,0:T(8,128)(2,1)S(1)}, bf16[192,256]{1,0:T(8,128)(2,1)S(1)}, u32[]{:S(2)}, u32[]{:S(2)}) collective-permute-start(bf16[192,256]{1,0:T(8,128)(2,1)S(1)} %get-tuple-element.31), channel_id=1, source_target_pairs={{0,1},{1,0},{2,3},{3,2},{4,5},{5,4},{6,7},{7,6},{8,9},{9,8},{10,11... | collective-permute-start | bytes 294920 | tf_op jit(solution)/shard_map/ppermute | solution.py:16
  4.7 6.0 %collective-permute-start.1 = (bf16[192,256]{1,0:T(8,128)(2,1)S(1)}, bf16[192,256]{1,0:T(8,128)(2,1)S(1)}, u32[]{:S(2)}, u32[]{:S(2)}) collective-permute-start(bf16[192,256]{1,0:T(8,128)(2,1)S(1)} %fusion.21), channel_id=1, source_target_pairs={{0,2},{1,3},{2,0},{3,1},{4,6},{5,7},{6,4},{7,5},{8,10},{9,11},{10,... | collective-permute-start | bytes 294920 | tf_op jit(solution)/shard_map/ppermute | solution.py:16
  10.8 1.4 %collective-permute-start.2 = (bf16[192,256]{1,0:T(8,128)(2,1)S(1)}, bf16[192,256]{1,0:T(8,128)(2,1)S(1)}, u32[]{:S(2)}, u32[]{:S(2)}) collective-permute-start(bf16[192,256]{1,0:T(8,128)(2,1)S(1)} %add_convert_fusion.2), channel_id=1, source_target_pairs={{0,1},{1,0},{2,3},{3,2},{4,5},{5,4},{6,7},{7,6},{8,9},{9,8},{10,11... | collective-permute-start | bytes 294920 | tf_op jit(solution)/shard_map/ppermute | solution.py:16
  12.8 8.6 %collective-permute-start.3 = (bf16[456,256]{1,0:T(8,128)(2,1)S(1)}, bf16[456,256]{1,0:T(8,128)(2,1)S(1)}, u32[]{:S(2)}, u32[]{:S(2)}) collective-permute-start(bf16[456,256]{1,0:T(8,128)(2,1)S(1)} %convolution_convert_fusion.1), channel_id=1, source_target_pairs={{0,4},{4,0},{8,12},{12,8},{16,20},{20,16},{24,28},{28,24},{1,5},{5... | collective-permute-start | bytes 700424 | tf_op jit(solution)/shard_map/ppermute | solution.py:16
  15.0 11.9 %collective-permute-start.5 = (bf16[456,256]{1,0:T(8,128)(2,1)S(1)}, bf16[456,256]{1,0:T(8,128)(2,1)S(1)}, u32[]{:S(2)}, u32[]{:S(2)}) collective-permute-start(bf16[456,256]{1,0:T(8,128)(2,1)S(1)} %pad_maximum_fusion), channel_id=1, source_target_pairs={{0,4},{4,0},{8,12},{12,8},{16,20},{20,16},{24,28},{28,24},{1,5},{5... | collective-permute-start | bytes 700424 | tf_op jit(solution)/shard_map/ppermute | solution.py:16
  15.4 8.7 %collective-permute-start.4 = (bf16[2,232,256]{2,1,0:T(8,128)(2,1)S(1)}, bf16[2,232,256]{2,1,0:T(8,128)(2,1)S(1)}, u32[]{:S(2)}, u32[]{:S(2)}) collective-permute-start(bf16[2,232,256]{2,1,0:T(8,128)(2,1)S(1)} %convolution_convert_fusion), channel_id=1, source_target_pairs={{0,8},{4,12},{8,0},{12,4},{16,24},{20,28},{24,16},{28,20},{1,9},{5... | collective-permute-start | bytes 712712 | tf_op jit(solution)/shard_map/ppermute | solution.py:121
  21.8 5.2 %collective-permute-start.6 = (bf16[224,256]{1,0:T(8,128)(2,1)S(1)}, bf16[224,256]{1,0:T(8,128)(2,1)S(1)}, u32[]{:S(2)}, u32[]{:S(2)}) collective-permute-start(bf16[224,256]{1,0:T(8,128)(2,1)S(1)} %fusion.3), channel_id=1, source_target_pairs={{0,8},{4,12},{8,0},{12,4},{16,24},{20,28},{24,16},{28,20},{1,9},{5... | collective-permute-start | bytes 344072 | tf_op jit(solution)/shard_map/ppermute | solution.py:121
  23.7 7.1 %collective-permute-start.7 = (bf16[232,256]{1,0:T(8,128)(2,1)S(1)}, bf16[232,256]{1,0:T(8,128)(2,1)S(1)}, u32[]{:S(2)}, u32[]{:S(2)}) collective-permute-start(bf16[232,256]{1,0:T(8,128)(2,1)S(1)} %fusion.1), channel_id=1, source_target_pairs={{0,8},{4,12},{8,0},{12,4},{16,24},{20,28},{24,16},{28,20},{1,9},{5... | collective-permute-start | bytes 356360 | tf_op jit(solution)/shard_map/ppermute | solution.py:121
  24.1 7.2 %collective-permute-start.8 = (bf16[232,256]{1,0:T(8,128)(2,1)S(1)}, bf16[232,256]{1,0:T(8,128)(2,1)S(1)}, u32[]{:S(2)}, u32[]{:S(2)}) collective-permute-start(bf16[232,256]{1,0:T(8,128)(2,1)S(1)} %convolution_convert_fusion.3), channel_id=1, source_target_pairs={{0,4},{4,0},{8,12},{12,8},{16,20},{20,16},{24,28},{28,24},{1,5},{5... | collective-permute-start | bytes 356360 | tf_op jit(solution)/shard_map/ppermute | solution.py:16
  25.9 9.1 %copy-start.1 = (bf16[8192,256]{1,0:T(8,128)(2,1)S(1)}, bf16[8192,256]{1,0:T(8,128)(2,1)}, u32[]{:S(2)}) copy-start(bf16[8192,256]{1,0:T(8,128)(2,1)} %basis.5) | copy-start | bytes 12582916
  26.0 9.1 %copy-start.2 = (f32[1,456,256]{2,1,0:T(8,128)S(1)}, f32[1,456,256]{2,1,0:T(8,128)}, u32[]{:S(2)}) copy-start(f32[1,456,256]{2,1,0:T(8,128)} %param.8) | copy-start | bytes 1400836
  26.0 9.1 %copy-start.3 = (f32[1,456,256]{2,1,0:T(8,128)S(1)}, f32[1,456,256]{2,1,0:T(8,128)}, u32[]{:S(2)}) copy-start(f32[1,456,256]{2,1,0:T(8,128)} %param.9) | copy-start | bytes 1400836
  26.3 8.8 %collective-permute-start.9 = (bf16[456,256]{1,0:T(8,128)(2,1)S(1)}, bf16[456,256]{1,0:T(8,128)(2,1)S(1)}, u32[]{:S(2)}, u32[]{:S(2)}) collective-permute-start(bf16[456,256]{1,0:T(8,128)(2,1)S(1)} %fusion), channel_id=1, source_target_pairs={{0,4},{4,0},{8,12},{12,8},{16,20},{20,16},{24,28},{28,24},{1,5},{5... | collective-permute-start | bytes 700424 | tf_op jit(solution)/shard_map/ppermute | solution.py:16
  27.1 8.0 %collective-permute-start.12 = (bf16[224,256]{1,0:T(8,128)(2,1)S(1)}, bf16[224,256]{1,0:T(8,128)(2,1)S(1)}, u32[]{:S(2)}, u32[]{:S(2)}) collective-permute-start(bf16[224,256]{1,0:T(8,128)(2,1)S(1)} %add_convert_fusion.1), channel_id=1, source_target_pairs={{0,24},{4,28},{8,16},{12,20},{16,8},{20,12},{24,0},{28,4},{1,25},{... | collective-permute-start | bytes 344072 | tf_op jit(solution)/shard_map/ppermute | solution.py:121
  31.1 6.6 %collective-permute-start.10 = (bf16[232,256]{1,0:T(8,128)(2,1)S(1)}, bf16[232,256]{1,0:T(8,128)(2,1)S(1)}, u32[]{:S(2)}, u32[]{:S(2)}) collective-permute-start(bf16[232,256]{1,0:T(8,128)(2,1)S(1)} %fusion.2), channel_id=1, source_target_pairs={{0,8},{4,12},{8,0},{12,4},{16,24},{20,28},{24,16},{28,20},{1,9},{5... | collective-permute-start | bytes 356360 | tf_op jit(solution)/shard_map/ppermute | solution.py:121
  31.4 6.8 %collective-permute-start.11 = (bf16[232,256]{1,0:T(8,128)(2,1)S(1)}, bf16[232,256]{1,0:T(8,128)(2,1)S(1)}, u32[]{:S(2)}, u32[]{:S(2)}) collective-permute-start(bf16[232,256]{1,0:T(8,128)(2,1)S(1)} %add_convert_fusion), channel_id=1, source_target_pairs={{0,24},{4,28},{8,16},{12,20},{16,8},{20,12},{24,0},{28,4},{1,25},{... | collective-permute-start | bytes 356360 | tf_op jit(solution)/shard_map/ppermute | solution.py:121

commit v8 on v7

--- a/solution.py
+++ b/solution.py
@@ -126,9 +126,6 @@
     def piece(value, cut):
         return value[cut[0] : cut[1]].astype(F32)
 
-    def padded(value):
-        return jnp.pad(value, ((0, rows - value.shape[0]), (0, 0)))
-
     got2 = pair(term(z ^ 2, 1 - x, coded))
     out1 = both(z ^ 1, coded, (0, first[1] + spare)).astype(BF)
     code, out1 = lax.optimization_barrier((coded, out1))
@@ -145,10 +142,11 @@
     out3 = term(z ^ 3, 1 - x, code, second).astype(BF)
     code, out3, near1 = lax.optimization_barrier((code, out3, near1))
     got3 = pair(out3)
-    near1 = near1[:, : first[1]]
-    own_in = (term(z, 1 - x, code) + padded(parity(near1, 1 - x))).astype(BF)
-    code, own_in = lax.optimization_barrier((coded, own_in))
-    own = pair(own_in)
+    near1 = near1[:, :n_first]
+    own_a = (term(z, 1 - x, code, first) + parity(near1, 1 - x)).astype(BF)
+    own_a = jnp.pad(own_a, ((0, 2 * spare), (0, 0)))
+    code, own_a = lax.optimization_barrier((coded, own_a))
+    own_a = pair(own_a)
 
     def total(block, cut, code, *parts):
         value = term(block, x, code, cut)
@@ -161,23 +159,24 @@
     code, got31, passed[1] = lax.optimization_barrier((code, got31, passed[1]))
     code, late = total(z ^ 1, second, code, got31[n_first:])
     late = hop(late, 1)
+    own_b = pair(term(z, 1 - x, code, second))
     code, total_b = total(z ^ 3, second, code, got3, passed[1])
     far_b = hop(total_b, 3)
     kept = [term(z, x, code, first) + parity(near1, x), term(z, x, code, second)]
-    return kept, own, [(far_a,), (late, far_b)]
+    return kept, [(far_a, own_a), (late, far_b, own_b)]
 
 
 WIDE = 512
 
 
-def adam_update_kernel(cut, n_terms, n_olds, own, got, first, second, basis, *refs):
+def adam_update_kernel(cut, n_terms, n_olds, own, first, second, basis, *refs):
     terms, refs = refs[:n_terms], refs[n_terms + n_olds :]
     new_first, new_second, update = refs[:3]
     first_buf, second_buf, direction, blocks, moment_sem, block_sem = refs[3:]
     here = pl.ds(cut[0], cut[1] - cut[0])
-    grad = own[...] + got[here, :].astype(F32)
+    grad = own[...]
     for term in terms:
-        grad = grad + term[...].astype(F32)
+        grad = grad + term[: cut[1] - cut[0], :].astype(F32)
     first_buf[...] = 0.9 * first[here, :] + 0.1 * grad
     second_buf[...] = 0.999 * second[here, :] + 0.001 * grad * grad
     moments = [
@@ -211,13 +210,13 @@
         copy.wait()
 
 
-def adam_update(cut, own, got, terms, first, second, basis, olds):
+def adam_update(cut, own, terms, first, second, basis, olds):
     rows, rank = first.shape
     feats = basis.shape[0]
     here = cut[1] - cut[0]
     vmem = pl.BlockSpec(memory_space=pltpu.VMEM)
     hbm = pl.BlockSpec(memory_space=pl.ANY)
-    n_inputs = 5 + len(terms)
+    n_inputs = 4 + len(terms)
     return pl.pallas_call(
         functools.partial(adam_update_kernel, cut, len(terms), len(olds)),
         out_shape=(
@@ -243,7 +242,7 @@
             transcendentals=here * rank,
         ),
         name="adam_update",
-    )(own, got, first, second, basis, *terms, *olds)
+    )(own, first, second, basis, *terms, *olds)
 
 
 def on_device(activations, basis, out_grad, first_moment, second_moment):
@@ -255,11 +254,11 @@
         rows = first_moment.shape[1]
         middle = rows // 32 * 16
         cuts = ((0, middle), (middle, rows))
-        kept, got, fars = line_total(out_grad.T, coded_rows, n_dp, cuts)
+        kept, others = line_total(out_grad.T, coded_rows, n_dp, cuts)
         outs = ()
-        for cut, own, terms in zip(cuts, kept, fars):
+        for cut, own, terms in zip(cuts, kept, others):
             outs = adam_update(
-                cut, own, got, terms, first_moment[0], second_moment[0], basis, outs
+                cut, own, terms, first_moment[0], second_moment[0], basis, outs
             )
         return tuple(out[None] for out in outs)
     term = jnp.dot(out_grad.T, coded_rows, preferred_element_type=F32)

time: 41 us -> 42.6 us (1.039)
  starting transfers between devices: 18.4 us -> 19.7 us
    ppermute x7 -> x8, starting transfers between devices: 7.84 us -> 9.39 us  [swap(): return lax.ppermute(value, axis, [(i, i ^ bit) for i in range(count)])]
    dot_general x12 -> x13, matrix products: 2.67 us -> 2.82 us  [term(): return jnp.dot(part, code, preferred_element_type=F32)]
    ppermute x7 -> x8, waiting for transfers between devices: 9.43 us -> 9.42 us  [swap(): return lax.ppermute(value, axis, [(i, i ^ bit) for i in range(count)])]
  transfers between devices with their start and end apart: 13 -> 14, of which waited for: 7 -> 6; matrix products, arithmetic and copies ran while one was open for 6% -> 6% of each run, Pallas kernels for 6% -> 6%
where the time goes in v8:
time: 42.6 us; the launch traced here: 42.4 us
  starting transfers between devices  19.7 us (46%)
  waiting for transfers between devices  10.6 us (25%)
  Pallas kernels  7.66 us (18%)
  matrix products  3.09 us (7%)
  between operations  1.02 us (2%)
    ppermute x6, starting transfers between devices, hop(): return lax.ppermute(value.astype(BF), 'dp', full)  10.3 us
    ppermute x8, waiting for transfers between devices, swap(): return lax.ppermute(value, axis, [(i, i ^ bit) for i in range(count)])  9.42 us
    ppermute x8, starting transfers between devices, swap(): return lax.ppermute(value, axis, [(i, i ^ bit) for i in range(count)])  9.39 us
    pallas_call x2, Pallas kernels, adam_update(): pl.pallas_call(functools.partial(adam_update_kernel, cut, len(terms), len...  5.11 us
    dot_general x13, matrix products, term(): return jnp.dot(part, code, preferred_element_type=F32)  2.82 us
    pallas_call x1, Pallas kernels, partial_code(): pl.pallas_call(partial_code_kernel, out_shape=(jax.ShapeDtypeStruct((rows...  2.55 us
    ppermute x6, waiting for transfers between devices, hop(): return lax.ppermute(value.astype(BF), 'dp', full)  1.21 us
  transfers between devices with their start and end apart: 14, of which 6 were waited for; matrix products, arithmetic and copies ran while one was open for 6% of the time, Pallas kernels for 6%

profile of v8, /device:TPU:0, one launch (start us, length us, event | category | flops | bytes accessed | tf_op | source)
XLA Modules:
  0.0 42.4 jit_solution(4424590196036904360)
XLA Ops:
  0.6 2.5 %partial_code.1 = (f32[192,256]{1,0:T(8,128)S(1)}, bf16[192,256]{1,0:T(8,128)(2,1)S(1)}) custom-call(bf16[384,2048]{1,0:T(8,128)(2,1)} %activations.1, bf16[8192,256]{1,0:T(8,128)(2,1)} %basis.5), custom_call_target="tpu_custom_call" | custom-call | flops 402653184 | bytes 2621440 | tf_op jit(solution)/shard_map/partial_code/pallas_call | solution.py:58
  3.2 0.5 %collective-permute-start = (bf16[192,256]{1,0:T(8,128)(2,1)S(1)}, bf16[192,256]{1,0:T(8,128)(2,1)S(1)}, u32[]{:S(2)}, u32[]{:S(2)}) collective-permute-start(bf16[192,256]{1,0:T(8,128)(2,1)S(1)} %get-tuple-element.31), channel_id=1, source_target_pairs={{0,1},{1,0},{2,3},{3,2},{4,5},{5,4},{6,7},{7,6},{8,9},{9,8},{10,11... | collective-permute-start | bytes 294920 | tf_op jit(solution)/shard_map/ppermute | solution.py:16
  3.7 0.9 %collective-permute-done = bf16[192,256]{1,0:T(8,128)(2,1)S(1)} collective-permute-done((bf16[192,256]{1,0:T(8,128)(2,1)S(1)}, bf16[192,256]{1,0:T(8,128)(2,1)S(1)}, u32[]{:S(2)}, u32[]{:S(2)}) %collective-permute-start) | collective-permute-done | bytes 98336 | tf_op jit(solution)/shard_map/ppermute | solution.py:16
  4.7 2.9 %collective-permute-start.1 = (bf16[192,256]{1,0:T(8,128)(2,1)S(1)}, bf16[192,256]{1,0:T(8,128)(2,1)S(1)}, u32[]{:S(2)}, u32[]{:S(2)}) collective-permute-start(bf16[192,256]{1,0:T(8,128)(2,1)S(1)} %fusion.22), channel_id=1, source_target_pairs={{0,2},{1,3},{2,0},{3,1},{4,6},{5,7},{6,4},{7,5},{8,10},{9,11},{10,... | collective-permute-start | bytes 294920 | tf_op jit(solution)/shard_map/ppermute | solution.py:16
  7.6 3.1 %collective-permute-done.1 = bf16[192,256]{1,0:T(8,128)(2,1)S(1)} collective-permute-done((bf16[192,256]{1,0:T(8,128)(2,1)S(1)}, bf16[192,256]{1,0:T(8,128)(2,1)S(1)}, u32[]{:S(2)}, u32[]{:S(2)}) %collective-permute-start.1) | collective-permute-done | bytes 98336 | tf_op jit(solution)/shard_map/ppermute | solution.py:16
  11.0 1.2 %collective-permute-done.2 = bf16[192,256]{1,0:T(8,128)(2,1)S(1)} collective-permute-done((bf16[192,256]{1,0:T(8,128)(2,1)S(1)}, bf16[192,256]{1,0:T(8,128)(2,1)S(1)}, u32[]{:S(2)}, u32[]{:S(2)}) %collective-permute-start.2) | collective-permute-done | bytes 98336 | tf_op jit(solution)/shard_map/ppermute | solution.py:16
  12.2 0.3 convolution_convert_fusion.1
  12.5 0.3 convolution_convert_fusion
  12.8 1.8 %collective-permute-start.3 = (bf16[456,256]{1,0:T(8,128)(2,1)S(1)}, bf16[456,256]{1,0:T(8,128)(2,1)S(1)}, u32[]{:S(2)}, u32[]{:S(2)}) collective-permute-start(bf16[456,256]{1,0:T(8,128)(2,1)S(1)} %convolution_convert_fusion.1), channel_id=1, source_target_pairs={{0,4},{4,0},{8,12},{12,8},{16,20},{20,16},{24,28},{28,24},{1,5},{5... | collective-permute-start | bytes 700424 | tf_op jit(solution)/shard_map/ppermute | solution.py:16
  14.6 0.2 convolution_convert_fusion.3
  14.8 0.2 convolution_convert_fusion.5
  15.0 0.4 collective-permute-start.5
  15.4 1.8 %collective-permute-start.4 = (bf16[2,232,256]{2,1,0:T(8,128)(2,1)S(1)}, bf16[2,232,256]{2,1,0:T(8,128)(2,1)S(1)}, u32[]{:S(2)}, u32[]{:S(2)}) collective-permute-start(bf16[2,232,256]{2,1,0:T(8,128)(2,1)S(1)} %convolution_convert_fusion), channel_id=1, source_target_pairs={{0,8},{4,12},{8,0},{12,4},{16,24},{20,28},{24,16},{28,20},{1,9},{5... | collective-permute-start | bytes 712712 | tf_op jit(solution)/shard_map/ppermute | solution.py:121
  17.2 4.2 %collective-permute-done.3 = bf16[456,256]{1,0:T(8,128)(2,1)S(1)} collective-permute-done((bf16[456,256]{1,0:T(8,128)(2,1)S(1)}, bf16[456,256]{1,0:T(8,128)(2,1)S(1)}, u32[]{:S(2)}, u32[]{:S(2)}) %collective-permute-start.3) | collective-permute-done | bytes 233504 | tf_op jit(solution)/shard_map/ppermute | solution.py:16
  21.4 0.2 fusion
  21.6 0.2 fusion.2
  21.8 1.9 %collective-permute-start.6 = (bf16[224,256]{1,0:T(8,128)(2,1)S(1)}, bf16[224,256]{1,0:T(8,128)(2,1)S(1)}, u32[]{:S(2)}, u32[]{:S(2)}) collective-permute-start(bf16[224,256]{1,0:T(8,128)(2,1)S(1)} %fusion.2), channel_id=1, source_target_pairs={{0,8},{4,12},{8,0},{12,4},{16,24},{20,28},{24,16},{28,20},{1,9},{5... | collective-permute-start | bytes 344072 | tf_op jit(solution)/shard_map/ppermute | solution.py:121
  23.7 0.2 collective-permute-start.7
  23.9 0.2 convolution_convert_fusion.4
  24.1 1.8 %collective-permute-start.8 = (bf16[232,256]{1,0:T(8,128)(2,1)S(1)}, bf16[232,256]{1,0:T(8,128)(2,1)S(1)}, u32[]{:S(2)}, u32[]{:S(2)}) collective-permute-start(bf16[232,256]{1,0:T(8,128)(2,1)S(1)} %convolution_convert_fusion.4), channel_id=1, source_target_pairs={{0,4},{4,0},{8,12},{12,8},{16,20},{20,16},{24,28},{28,24},{1,5},{5... | collective-permute-start | bytes 356360 | tf_op jit(solution)/shard_map/ppermute | solution.py:16
  26.0 0.2 fusion.3
  26.2 0.4 collective-permute-start.13
  26.8 0.2 collective-permute-done.6
  27.1 3.7 %collective-permute-start.12 = (bf16[224,256]{1,0:T(8,128)(2,1)S(1)}, bf16[224,256]{1,0:T(8,128)(2,1)S(1)}, u32[]{:S(2)}, u32[]{:S(2)}) collective-permute-start(bf16[224,256]{1,0:T(8,128)(2,1)S(1)} %add_convert_fusion.1), channel_id=1, source_target_pairs={{0,24},{4,28},{8,16},{12,20},{16,8},{20,12},{24,0},{28,4},{1,25},{... | collective-permute-start | bytes 344072 | tf_op jit(solution)/shard_map/ppermute | solution.py:121
  30.8 0.2 fusion.1
  31.0 0.2 convolution_convert_fusion.2
  31.2 1.6 %collective-permute-start.11 = (bf16[232,256]{1,0:T(8,128)(2,1)S(1)}, bf16[232,256]{1,0:T(8,128)(2,1)S(1)}, u32[]{:S(2)}, u32[]{:S(2)}) collective-permute-start(bf16[232,256]{1,0:T(8,128)(2,1)S(1)} %convolution_convert_fusion.2), channel_id=1, source_target_pairs={{0,4},{4,0},{8,12},{12,8},{16,20},{20,16},{24,28},{28,24},{1,5},{5... | collective-permute-start | bytes 356360 | tf_op jit(solution)/shard_map/ppermute | solution.py:16
  32.8 0.2 fusion.8
  33.0 2.8 %collective-permute-start.10 = (bf16[232,256]{1,0:T(8,128)(2,1)S(1)}, bf16[232,256]{1,0:T(8,128)(2,1)S(1)}, u32[]{:S(2)}, u32[]{:S(2)}) collective-permute-start(bf16[232,256]{1,0:T(8,128)(2,1)S(1)} %add_convert_fusion), channel_id=1, source_target_pairs={{0,24},{4,28},{8,16},{12,20},{16,8},{20,12},{24,0},{28,4},{1,25},{... | collective-permute-start | bytes 356360 | tf_op jit(solution)/shard_map/ppermute | solution.py:121
  36.3 2.5 %adam_update.2 = (f32[456,256]{1,0:T(8,128)}, f32[456,256]{1,0:T(8,128)}, bf16[456,8192]{1,0:T(8,128)(2,1)}) custom-call(f32[224,256]{1,0:T(8,128)S(1)} %convolution_add_fusion.2.own, f32[456,256]{1,0:T(8,128)S(1)} %bitcast.31, f32[456,256]{1,0:T(8,128)S(1)} %bitcast.33, bf16[8192,256]{1,0:T(8,128)(2,1)S(1)} %copy-done.1, ...), custom_call_target="tpu_custom_call" | custom-call | flops 939524096 | bytes 7864320 | tf_op jit(solution)/shard_map/adam_update/pallas_call | solution.py:220
  38.9 1.0 %collective-permute-done.10.refs_1_ = bf16[232,256]{1,0:T(8,128)(2,1)S(1)} collective-permute-done((bf16[232,256]{1,0:T(8,128)(2,1)S(1)}, bf16[232,256]{1,0:T(8,128)(2,1)S(1)}, u32[]{:S(2)}, u32[]{:S(2)}) %collective-permute-start.10) | collective-permute-done | bytes 118816 | tf_op jit(solution)/shard_map/ppermute | solution.py:121
  39.8 2.6 %adam_update.3 = (f32[456,256]{1,0:T(8,128)}, f32[456,256]{1,0:T(8,128)}, bf16[456,8192]{1,0:T(8,128)(2,1)}) custom-call(f32[232,256]{1,0:T(8,128)S(1)} %fusion.14.own, f32[456,256]{1,0:T(8,128)S(1)} %bitcast.32, f32[456,256]{1,0:T(8,128)S(1)} %bitcast.34, ...), custom_call_target="tpu_custom_call", output_to_operand_aliasing={{0}: (7, {}), {1}: (8, {}), {2}: (9, {})} | custom-call | flops 973078528 | bytes 7995392 | tf_op jit(solution)/shard_map/adam_update/pallas_call | solution.py:220
  (29 shorter events, 1.0 us)
Async XLA Ops:
  0.6 11.6 %copy-start = (bf16[384,3648]{0,1:T(8,128)(2,1)S(1)}, bf16[384,3648]{0,1:T(8,128)(2,1)}, u32[]{:S(2)}) copy-start(bf16[384,3648]{0,1:T(8,128)(2,1)} %param.7) | copy-start | bytes 8404996
  3.2 1.5 %collective-permute-start = (bf16[192,256]{1,0:T(8,128)(2,1)S(1)}, bf16[192,256]{1,0:T(8,128)(2,1)S(1)}, u32[]{:S(2)}, u32[]{:S(2)}) collective-permute-start(bf16[192,256]{1,0:T(8,128)(2,1)S(1)} %get-tuple-element.31), channel_id=1, source_target_pairs={{0,1},{1,0},{2,3},{3,2},{4,5},{5,4},{6,7},{7,6},{8,9},{9,8},{10,11... | collective-permute-start | bytes 294920 | tf_op jit(solution)/shard_map/ppermute | solution.py:16
  4.7 6.0 %collective-permute-start.1 = (bf16[192,256]{1,0:T(8,128)(2,1)S(1)}, bf16[192,256]{1,0:T(8,128)(2,1)S(1)}, u32[]{:S(2)}, u32[]{:S(2)}) collective-permute-start(bf16[192,256]{1,0:T(8,128)(2,1)S(1)} %fusion.22), channel_id=1, source_target_pairs={{0,2},{1,3},{2,0},{3,1},{4,6},{5,7},{6,4},{7,5},{8,10},{9,11},{10,... | collective-permute-start | bytes 294920 | tf_op jit(solution)/shard_map/ppermute | solution.py:16
  10.8 1.4 %collective-permute-start.2 = (bf16[192,256]{1,0:T(8,128)(2,1)S(1)}, bf16[192,256]{1,0:T(8,128)(2,1)S(1)}, u32[]{:S(2)}, u32[]{:S(2)}) collective-permute-start(bf16[192,256]{1,0:T(8,128)(2,1)S(1)} %add_convert_fusion.2), channel_id=1, source_target_pairs={{0,1},{1,0},{2,3},{3,2},{4,5},{5,4},{6,7},{7,6},{8,9},{9,8},{10,11... | collective-permute-start | bytes 294920 | tf_op jit(solution)/shard_map/ppermute | solution.py:16
  12.8 8.6 %collective-permute-start.3 = (bf16[456,256]{1,0:T(8,128)(2,1)S(1)}, bf16[456,256]{1,0:T(8,128)(2,1)S(1)}, u32[]{:S(2)}, u32[]{:S(2)}) collective-permute-start(bf16[456,256]{1,0:T(8,128)(2,1)S(1)} %convolution_convert_fusion.1), channel_id=1, source_target_pairs={{0,4},{4,0},{8,12},{12,8},{16,20},{20,16},{24,28},{28,24},{1,5},{5... | collective-permute-start | bytes 700424 | tf_op jit(solution)/shard_map/ppermute | solution.py:16
  15.0 11.8 %collective-permute-start.5 = (bf16[456,256]{1,0:T(8,128)(2,1)S(1)}, bf16[456,256]{1,0:T(8,128)(2,1)S(1)}, u32[]{:S(2)}, u32[]{:S(2)}) collective-permute-start(bf16[456,256]{1,0:T(8,128)(2,1)S(1)} %pad_maximum_fusion), channel_id=1, source_target_pairs={{0,4},{4,0},{8,12},{12,8},{16,20},{20,16},{24,28},{28,24},{1,5},{5... | collective-permute-start | bytes 700424 | tf_op jit(solution)/shard_map/ppermute | solution.py:16
  15.4 8.7 %collective-permute-start.4 = (bf16[2,232,256]{2,1,0:T(8,128)(2,1)S(1)}, bf16[2,232,256]{2,1,0:T(8,128)(2,1)S(1)}, u32[]{:S(2)}, u32[]{:S(2)}) collective-permute-start(bf16[2,232,256]{2,1,0:T(8,128)(2,1)S(1)} %convolution_convert_fusion), channel_id=1, source_target_pairs={{0,8},{4,12},{8,0},{12,4},{16,24},{20,28},{24,16},{28,20},{1,9},{5... | collective-permute-start | bytes 712712 | tf_op jit(solution)/shard_map/ppermute | solution.py:121
  21.8 5.2 %collective-permute-start.6 = (bf16[224,256]{1,0:T(8,128)(2,1)S(1)}, bf16[224,256]{1,0:T(8,128)(2,1)S(1)}, u32[]{:S(2)}, u32[]{:S(2)}) collective-permute-start(bf16[224,256]{1,0:T(8,128)(2,1)S(1)} %fusion.2), channel_id=1, source_target_pairs={{0,8},{4,12},{8,0},{12,4},{16,24},{20,28},{24,16},{28,20},{1,9},{5... | collective-permute-start | bytes 344072 | tf_op jit(solution)/shard_map/ppermute | solution.py:121
  23.7 7.1 %collective-permute-start.7 = (bf16[232,256]{1,0:T(8,128)(2,1)S(1)}, bf16[232,256]{1,0:T(8,128)(2,1)S(1)}, u32[]{:S(2)}, u32[]{:S(2)}) collective-permute-start(bf16[232,256]{1,0:T(8,128)(2,1)S(1)} %fusion), channel_id=1, source_target_pairs={{0,8},{4,12},{8,0},{12,4},{16,24},{20,28},{24,16},{28,20},{1,9},{5... | collective-permute-start | bytes 356360 | tf_op jit(solution)/shard_map/ppermute | solution.py:121
  24.1 8.8 %collective-permute-start.8 = (bf16[232,256]{1,0:T(8,128)(2,1)S(1)}, bf16[232,256]{1,0:T(8,128)(2,1)S(1)}, u32[]{:S(2)}, u32[]{:S(2)}) collective-permute-start(bf16[232,256]{1,0:T(8,128)(2,1)S(1)} %convolution_convert_fusion.4), channel_id=1, source_target_pairs={{0,4},{4,0},{8,12},{12,8},{16,20},{20,16},{24,28},{28,24},{1,5},{5... | collective-permute-start | bytes 356360 | tf_op jit(solution)/shard_map/ppermute | solution.py:16
  25.9 10.3 %copy-start.1 = (bf16[8192,256]{1,0:T(8,128)(2,1)S(1)}, bf16[8192,256]{1,0:T(8,128)(2,1)}, u32[]{:S(2)}) copy-start(bf16[8192,256]{1,0:T(8,128)(2,1)} %basis.5) | copy-start | bytes 12582916
  26.0 10.3 %copy-start.2 = (f32[1,456,256]{2,1,0:T(8,128)S(1)}, f32[1,456,256]{2,1,0:T(8,128)}, u32[]{:S(2)}) copy-start(f32[1,456,256]{2,1,0:T(8,128)} %param.8) | copy-start | bytes 1400836
  26.0 10.3 %copy-start.3 = (f32[1,456,256]{2,1,0:T(8,128)S(1)}, f32[1,456,256]{2,1,0:T(8,128)}, u32[]{:S(2)}) copy-start(f32[1,456,256]{2,1,0:T(8,128)} %param.9) | copy-start | bytes 1400836
  26.2 10.0 %collective-permute-start.13 = (bf16[240,256]{1,0:T(8,128)(2,1)S(1)}, bf16[240,256]{1,0:T(8,128)(2,1)S(1)}, u32[]{:S(2)}, u32[]{:S(2)}) collective-permute-start(bf16[240,256]{1,0:T(8,128)(2,1)S(1)} %pad.4), channel_id=1, source_target_pairs={{0,4},{4,0},{8,12},{12,8},{16,20},{20,16},{24,28},{28,24},{1,5},{5... | collective-permute-start | bytes 368648 | tf_op jit(solution)/shard_map/ppermute | solution.py:16
  27.1 9.2 %collective-permute-start.12 = (bf16[224,256]{1,0:T(8,128)(2,1)S(1)}, bf16[224,256]{1,0:T(8,128)(2,1)S(1)}, u32[]{:S(2)}, u32[]{:S(2)}) collective-permute-start(bf16[224,256]{1,0:T(8,128)(2,1)S(1)} %add_convert_fusion.1), channel_id=1, source_target_pairs={{0,24},{4,28},{8,16},{12,20},{16,8},{20,12},{24,0},{28,4},{1,25},{... | collective-permute-start | bytes 344072 | tf_op jit(solution)/shard_map/ppermute | solution.py:121
  31.2 7.6 %collective-permute-start.11 = (bf16[232,256]{1,0:T(8,128)(2,1)S(1)}, bf16[232,256]{1,0:T(8,128)(2,1)S(1)}, u32[]{:S(2)}, u32[]{:S(2)}) collective-permute-start(bf16[232,256]{1,0:T(8,128)(2,1)S(1)} %convolution_convert_fusion.2), channel_id=1, source_target_pairs={{0,4},{4,0},{8,12},{12,8},{16,20},{20,16},{24,28},{28,24},{1,5},{5... | collective-permute-start | bytes 356360 | tf_op jit(solution)/shard_map/ppermute | solution.py:16
  32.8 6.1 %collective-permute-start.9 = (bf16[232,256]{1,0:T(8,128)(2,1)S(1)}, bf16[232,256]{1,0:T(8,128)(2,1)S(1)}, u32[]{:S(2)}, u32[]{:S(2)}) collective-permute-start(bf16[232,256]{1,0:T(8,128)(2,1)S(1)} %fusion.1), channel_id=1, source_target_pairs={{0,8},{4,12},{8,0},{12,4},{16,24},{20,28},{24,16},{28,20},{1,9},{5... | collective-permute-start | bytes 356360 | tf_op jit(solution)/shard_map/ppermute | solution.py:121
  33.0 6.8 %collective-permute-start.10 = (bf16[232,256]{1,0:T(8,128)(2,1)S(1)}, bf16[232,256]{1,0:T(8,128)(2,1)S(1)}, u32[]{:S(2)}, u32[]{:S(2)}) collective-permute-start(bf16[232,256]{1,0:T(8,128)(2,1)S(1)} %add_convert_fusion), channel_id=1, source_target_pairs={{0,24},{4,28},{8,16},{12,20},{16,8},{20,12},{24,0},{28,4},{1,25},{... | collective-permute-start | bytes 356360 | tf_op jit(solution)/shard_map/ppermute | solution.py:121

commit v9 on v7

--- a/solution.py
+++ b/solution.py
@@ -16,7 +16,7 @@
     return lax.ppermute(value, axis, [(i, i ^ bit) for i in range(count)])
 
 
-DEEP = 4
+DEEP = 8
 
 
 def partial_code_kernel(activations, basis, keep, send, act_buf, basis_buf, total, sems):
@@ -167,7 +167,7 @@
     return kept, own, [(far_a,), (late, far_b)]
 
 
-WIDE = 512
+WIDE = 256
 
 
 def adam_update_kernel(cut, n_terms, n_olds, own, got, first, second, basis, *refs):

time: 41 us -> 41.2 us (level)
  Pallas kernels: 7.65 us -> 8.08 us
  transfers between devices with their start and end apart: 13 -> 13, of which waited for: 7 -> 7; matrix products, arithmetic and copies ran while one was open for 6% -> 6% of each run, Pallas kernels for 6% -> 7%
where the time goes in v9:
time: 41.2 us; the launch traced here: 41.1 us
  starting transfers between devices  18.4 us (45%)
  waiting for transfers between devices  10.3 us (25%)
  Pallas kernels  8.08 us (20%)
  matrix products  2.96 us (7%)
  between operations  0.98 us (2%)
    ppermute x6, starting transfers between devices, hop(): return lax.ppermute(value.astype(BF), 'dp', full)  10.6 us
    ppermute x7, waiting for transfers between devices, swap(): return lax.ppermute(value, axis, [(i, i ^ bit) for i in range(count)])  9.43 us
    ppermute x7, starting transfers between devices, swap(): return lax.ppermute(value, axis, [(i, i ^ bit) for i in range(count)])  7.83 us
    pallas_call x2, Pallas kernels, adam_update(): pl.pallas_call(functools.partial(adam_update_kernel, cut, len(terms), len...  5.38 us
    pallas_call x1, Pallas kernels, partial_code(): pl.pallas_call(partial_code_kernel, out_shape=(jax.ShapeDtypeStruct((rows...  2.69 us
    dot_general x12, matrix products, term(): return jnp.dot(part, code, preferred_element_type=F32)  2.68 us
    ppermute x6, waiting for transfers between devices, hop(): return lax.ppermute(value.astype(BF), 'dp', full)  0.91 us
  transfers between devices with their start and end apart: 13, of which 7 were waited for; matrix products, arithmetic and copies ran while one was open for 6% of the time, Pallas kernels for 7%

profile of v9, /device:TPU:0, one launch (start us, length us, event | category | flops | bytes accessed | tf_op | source)
XLA Modules:
  0.0 41.1 jit_solution(8394309058731746818)
XLA Ops:
  0.6 2.7 %partial_code.1 = (f32[192,256]{1,0:T(8,128)S(1)}, bf16[192,256]{1,0:T(8,128)(2,1)S(1)}) custom-call(bf16[384,2048]{1,0:T(8,128)(2,1)} %activations.1, bf16[8192,256]{1,0:T(8,128)(2,1)} %basis.5), custom_call_target="tpu_custom_call" | custom-call | flops 402653184 | bytes 2621440 | tf_op jit(solution)/shard_map/partial_code/pallas_call | solution.py:58
  3.3 0.5 %collective-permute-start = (bf16[192,256]{1,0:T(8,128)(2,1)S(1)}, bf16[192,256]{1,0:T(8,128)(2,1)S(1)}, u32[]{:S(2)}, u32[]{:S(2)}) collective-permute-start(bf16[192,256]{1,0:T(8,128)(2,1)S(1)} %get-tuple-element.31), channel_id=1, source_target_pairs={{0,1},{1,0},{2,3},{3,2},{4,5},{5,4},{6,7},{7,6},{8,9},{9,8},{10,11... | collective-permute-start | bytes 294920 | tf_op jit(solution)/shard_map/ppermute | solution.py:16
  3.9 0.9 %collective-permute-done = bf16[192,256]{1,0:T(8,128)(2,1)S(1)} collective-permute-done((bf16[192,256]{1,0:T(8,128)(2,1)S(1)}, bf16[192,256]{1,0:T(8,128)(2,1)S(1)}, u32[]{:S(2)}, u32[]{:S(2)}) %collective-permute-start) | collective-permute-done | bytes 98336 | tf_op jit(solution)/shard_map/ppermute | solution.py:16
  4.8 2.9 %collective-permute-start.1 = (bf16[192,256]{1,0:T(8,128)(2,1)S(1)}, bf16[192,256]{1,0:T(8,128)(2,1)S(1)}, u32[]{:S(2)}, u32[]{:S(2)}) collective-permute-start(bf16[192,256]{1,0:T(8,128)(2,1)S(1)} %fusion.21), channel_id=1, source_target_pairs={{0,2},{1,3},{2,0},{3,1},{4,6},{5,7},{6,4},{7,5},{8,10},{9,11},{10,... | collective-permute-start | bytes 294920 | tf_op jit(solution)/shard_map/ppermute | solution.py:16
  7.8 3.1 %collective-permute-done.1 = bf16[192,256]{1,0:T(8,128)(2,1)S(1)} collective-permute-done((bf16[192,256]{1,0:T(8,128)(2,1)S(1)}, bf16[192,256]{1,0:T(8,128)(2,1)S(1)}, u32[]{:S(2)}, u32[]{:S(2)}) %collective-permute-start.1) | collective-permute-done | bytes 98336 | tf_op jit(solution)/shard_map/ppermute | solution.py:16
  11.1 1.2 %collective-permute-done.2 = bf16[192,256]{1,0:T(8,128)(2,1)S(1)} collective-permute-done((bf16[192,256]{1,0:T(8,128)(2,1)S(1)}, bf16[192,256]{1,0:T(8,128)(2,1)S(1)}, u32[]{:S(2)}, u32[]{:S(2)}) %collective-permute-start.2) | collective-permute-done | bytes 98336 | tf_op jit(solution)/shard_map/ppermute | solution.py:16
  12.4 0.3 convolution_convert_fusion.1
  12.6 0.3 convolution_convert_fusion
  12.9 1.8 %collective-permute-start.3 = (bf16[456,256]{1,0:T(8,128)(2,1)S(1)}, bf16[456,256]{1,0:T(8,128)(2,1)S(1)}, u32[]{:S(2)}, u32[]{:S(2)}) collective-permute-start(bf16[456,256]{1,0:T(8,128)(2,1)S(1)} %convolution_convert_fusion.1), channel_id=1, source_target_pairs={{0,4},{4,0},{8,12},{12,8},{16,20},{20,16},{24,28},{28,24},{1,5},{5... | collective-permute-start | bytes 700424 | tf_op jit(solution)/shard_map/ppermute | solution.py:16
  14.7 0.2 convolution_convert_fusion.2
  14.9 0.2 convolution_convert_fusion.4
  15.2 0.4 collective-permute-start.5
  15.5 1.8 %collective-permute-start.4 = (bf16[2,232,256]{2,1,0:T(8,128)(2,1)S(1)}, bf16[2,232,256]{2,1,0:T(8,128)(2,1)S(1)}, u32[]{:S(2)}, u32[]{:S(2)}) collective-permute-start(bf16[2,232,256]{2,1,0:T(8,128)(2,1)S(1)} %convolution_convert_fusion), channel_id=1, source_target_pairs={{0,8},{4,12},{8,0},{12,4},{16,24},{20,28},{24,16},{28,20},{1,9},{5... | collective-permute-start | bytes 712712 | tf_op jit(solution)/shard_map/ppermute | solution.py:121
  17.3 4.2 %collective-permute-done.3 = bf16[456,256]{1,0:T(8,128)(2,1)S(1)} collective-permute-done((bf16[456,256]{1,0:T(8,128)(2,1)S(1)}, bf16[456,256]{1,0:T(8,128)(2,1)S(1)}, u32[]{:S(2)}, u32[]{:S(2)}) %collective-permute-start.3) | collective-permute-done | bytes 233504 | tf_op jit(solution)/shard_map/ppermute | solution.py:16
  21.5 0.2 fusion.1
  21.7 0.2 fusion.3
  22.0 1.9 %collective-permute-start.6 = (bf16[224,256]{1,0:T(8,128)(2,1)S(1)}, bf16[224,256]{1,0:T(8,128)(2,1)S(1)}, u32[]{:S(2)}, u32[]{:S(2)}) collective-permute-start(bf16[224,256]{1,0:T(8,128)(2,1)S(1)} %fusion.3), channel_id=1, source_target_pairs={{0,8},{4,12},{8,0},{12,4},{16,24},{20,28},{24,16},{28,20},{1,9},{5... | collective-permute-start | bytes 344072 | tf_op jit(solution)/shard_map/ppermute | solution.py:121
  23.8 0.2 collective-permute-start.7
  24.1 0.2 convolution_convert_fusion.3
  24.3 1.8 %collective-permute-start.8 = (bf16[232,256]{1,0:T(8,128)(2,1)S(1)}, bf16[232,256]{1,0:T(8,128)(2,1)S(1)}, u32[]{:S(2)}, u32[]{:S(2)}) collective-permute-start(bf16[232,256]{1,0:T(8,128)(2,1)S(1)} %convolution_convert_fusion.3), channel_id=1, source_target_pairs={{0,4},{4,0},{8,12},{12,8},{16,20},{20,16},{24,28},{28,24},{1,5},{5... | collective-permute-start | bytes 356360 | tf_op jit(solution)/shard_map/ppermute | solution.py:16
  26.1 0.3 fusion
  26.4 0.4 collective-permute-start.9
  27.2 3.8 %collective-permute-start.12 = (bf16[224,256]{1,0:T(8,128)(2,1)S(1)}, bf16[224,256]{1,0:T(8,128)(2,1)S(1)}, u32[]{:S(2)}, u32[]{:S(2)}) collective-permute-start(bf16[224,256]{1,0:T(8,128)(2,1)S(1)} %add_convert_fusion.1), channel_id=1, source_target_pairs={{0,24},{4,28},{8,16},{12,20},{16,8},{20,12},{24,0},{28,4},{1,25},{... | collective-permute-start | bytes 344072 | tf_op jit(solution)/shard_map/ppermute | solution.py:121
  31.0 0.2 fusion.2
  31.3 0.2 fusion.8
  31.6 2.9 %collective-permute-start.11 = (bf16[232,256]{1,0:T(8,128)(2,1)S(1)}, bf16[232,256]{1,0:T(8,128)(2,1)S(1)}, u32[]{:S(2)}, u32[]{:S(2)}) collective-permute-start(bf16[232,256]{1,0:T(8,128)(2,1)S(1)} %add_convert_fusion), channel_id=1, source_target_pairs={{0,24},{4,28},{8,16},{12,20},{16,8},{20,12},{24,0},{28,4},{1,25},{... | collective-permute-start | bytes 356360 | tf_op jit(solution)/shard_map/ppermute | solution.py:121
  34.5 0.2 fusion.14.own
  34.7 0.2 convolution_add_fusion.3.own
  34.9 0.3 collective-permute-done.12.refs_0_
  35.2 2.7 %adam_update.2 = (f32[456,256]{1,0:T(8,128)}, f32[456,256]{1,0:T(8,128)}, bf16[456,8192]{1,0:T(8,128)(2,1)}) custom-call(f32[224,256]{1,0:T(8,128)S(1)} %convolution_add_fusion.3.own, bf16[456,256]{1,0:T(8,128)(2,1)S(1)} %collective-permute-done.9.got, f32[456,256]{1,0:T(8,128)S(1)} %bitcast.29, f32[456,256]{1,0:T(8,128)S(1)} %bitcast.31, ...), custom_call_target="tpu_custom_call" | custom-call | flops 939524096 | bytes 7864320 | tf_op jit(solution)/shard_map/adam_update/pallas_call | solution.py:221
  37.9 0.5 %collective-permute-done.11.refs_1_ = bf16[232,256]{1,0:T(8,128)(2,1)S(1)} collective-permute-done((bf16[232,256]{1,0:T(8,128)(2,1)S(1)}, bf16[232,256]{1,0:T(8,128)(2,1)S(1)}, u32[]{:S(2)}, u32[]{:S(2)}) %collective-permute-start.11) | collective-permute-done | bytes 118816 | tf_op jit(solution)/shard_map/ppermute | solution.py:121
  38.4 2.7 %adam_update.3 = (f32[456,256]{1,0:T(8,128)}, f32[456,256]{1,0:T(8,128)}, bf16[456,8192]{1,0:T(8,128)(2,1)}) custom-call(f32[232,256]{1,0:T(8,128)S(1)} %fusion.14.own, bf16[456,256]{1,0:T(8,128)(2,1)S(1)} %collective-permute-done.9.got, f32[456,256]{1,0:T(8,128)S(1)} %bitcast.30, ...), custom_call_target="tpu_custom_call", output_to_operand_aliasing={{0}: (7, {}), {1}: (8, {}), {2}: (9, {})} | custom-call | flops 973078528 | bytes 7995392 | tf_op jit(solution)/shard_map/adam_update/pallas_call | solution.py:221
  (26 shorter events, 0.8 us)
Async XLA Ops:
  0.6 11.7 %copy-start = (bf16[384,3648]{0,1:T(8,128)(2,1)S(1)}, bf16[384,3648]{0,1:T(8,128)(2,1)}, u32[]{:S(2)}) copy-start(bf16[384,3648]{0,1:T(8,128)(2,1)} %param.7) | copy-start | bytes 8404996
  3.3 1.5 %collective-permute-start = (bf16[192,256]{1,0:T(8,128)(2,1)S(1)}, bf16[192,256]{1,0:T(8,128)(2,1)S(1)}, u32[]{:S(2)}, u32[]{:S(2)}) collective-permute-start(bf16[192,256]{1,0:T(8,128)(2,1)S(1)} %get-tuple-element.31), channel_id=1, source_target_pairs={{0,1},{1,0},{2,3},{3,2},{4,5},{5,4},{6,7},{7,6},{8,9},{9,8},{10,11... | collective-permute-start | bytes 294920 | tf_op jit(solution)/shard_map/ppermute | solution.py:16
  4.8 6.0 %collective-permute-start.1 = (bf16[192,256]{1,0:T(8,128)(2,1)S(1)}, bf16[192,256]{1,0:T(8,128)(2,1)S(1)}, u32[]{:S(2)}, u32[]{:S(2)}) collective-permute-start(bf16[192,256]{1,0:T(8,128)(2,1)S(1)} %fusion.21), channel_id=1, source_target_pairs={{0,2},{1,3},{2,0},{3,1},{4,6},{5,7},{6,4},{7,5},{8,10},{9,11},{10,... | collective-permute-start | bytes 294920 | tf_op jit(solution)/shard_map/ppermute | solution.py:16
  10.9 1.4 %collective-permute-start.2 = (bf16[192,256]{1,0:T(8,128)(2,1)S(1)}, bf16[192,256]{1,0:T(8,128)(2,1)S(1)}, u32[]{:S(2)}, u32[]{:S(2)}) collective-permute-start(bf16[192,256]{1,0:T(8,128)(2,1)S(1)} %add_convert_fusion.2), channel_id=1, source_target_pairs={{0,1},{1,0},{2,3},{3,2},{4,5},{5,4},{6,7},{7,6},{8,9},{9,8},{10,11... | collective-permute-start | bytes 294920 | tf_op jit(solution)/shard_map/ppermute | solution.py:16
  12.9 8.6 %collective-permute-start.3 = (bf16[456,256]{1,0:T(8,128)(2,1)S(1)}, bf16[456,256]{1,0:T(8,128)(2,1)S(1)}, u32[]{:S(2)}, u32[]{:S(2)}) collective-permute-start(bf16[456,256]{1,0:T(8,128)(2,1)S(1)} %convolution_convert_fusion.1), channel_id=1, source_target_pairs={{0,4},{4,0},{8,12},{12,8},{16,20},{20,16},{24,28},{28,24},{1,5},{5... | collective-permute-start | bytes 700424 | tf_op jit(solution)/shard_map/ppermute | solution.py:16
  15.2 11.9 %collective-permute-start.5 = (bf16[456,256]{1,0:T(8,128)(2,1)S(1)}, bf16[456,256]{1,0:T(8,128)(2,1)S(1)}, u32[]{:S(2)}, u32[]{:S(2)}) collective-permute-start(bf16[456,256]{1,0:T(8,128)(2,1)S(1)} %pad_maximum_fusion), channel_id=1, source_target_pairs={{0,4},{4,0},{8,12},{12,8},{16,20},{20,16},{24,28},{28,24},{1,5},{5... | collective-permute-start | bytes 700424 | tf_op jit(solution)/shard_map/ppermute | solution.py:16
  15.5 8.7 %collective-permute-start.4 = (bf16[2,232,256]{2,1,0:T(8,128)(2,1)S(1)}, bf16[2,232,256]{2,1,0:T(8,128)(2,1)S(1)}, u32[]{:S(2)}, u32[]{:S(2)}) collective-permute-start(bf16[2,232,256]{2,1,0:T(8,128)(2,1)S(1)} %convolution_convert_fusion), channel_id=1, source_target_pairs={{0,8},{4,12},{8,0},{12,4},{16,24},{20,28},{24,16},{28,20},{1,9},{5... | collective-permute-start | bytes 712712 | tf_op jit(solution)/shard_map/ppermute | solution.py:121
  22.0 5.2 %collective-permute-start.6 = (bf16[224,256]{1,0:T(8,128)(2,1)S(1)}, bf16[224,256]{1,0:T(8,128)(2,1)S(1)}, u32[]{:S(2)}, u32[]{:S(2)}) collective-permute-start(bf16[224,256]{1,0:T(8,128)(2,1)S(1)} %fusion.3), channel_id=1, source_target_pairs={{0,8},{4,12},{8,0},{12,4},{16,24},{20,28},{24,16},{28,20},{1,9},{5... | collective-permute-start | bytes 344072 | tf_op jit(solution)/shard_map/ppermute | solution.py:121
  23.8 7.2 %collective-permute-start.7 = (bf16[232,256]{1,0:T(8,128)(2,1)S(1)}, bf16[232,256]{1,0:T(8,128)(2,1)S(1)}, u32[]{:S(2)}, u32[]{:S(2)}) collective-permute-start(bf16[232,256]{1,0:T(8,128)(2,1)S(1)} %fusion.1), channel_id=1, source_target_pairs={{0,8},{4,12},{8,0},{12,4},{16,24},{20,28},{24,16},{28,20},{1,9},{5... | collective-permute-start | bytes 356360 | tf_op jit(solution)/shard_map/ppermute | solution.py:121
  24.3 7.2 %collective-permute-start.8 = (bf16[232,256]{1,0:T(8,128)(2,1)S(1)}, bf16[232,256]{1,0:T(8,128)(2,1)S(1)}, u32[]{:S(2)}, u32[]{:S(2)}) collective-permute-start(bf16[232,256]{1,0:T(8,128)(2,1)S(1)} %convolution_convert_fusion.3), channel_id=1, source_target_pairs={{0,4},{4,0},{8,12},{12,8},{16,20},{20,16},{24,28},{28,24},{1,5},{5... | collective-permute-start | bytes 356360 | tf_op jit(solution)/shard_map/ppermute | solution.py:16
  26.1 9.1 %copy-start.1 = (bf16[8192,256]{1,0:T(8,128)(2,1)S(1)}, bf16[8192,256]{1,0:T(8,128)(2,1)}, u32[]{:S(2)}) copy-start(bf16[8192,256]{1,0:T(8,128)(2,1)} %basis.5) | copy-start | bytes 12582916
  26.1 9.1 %copy-start.2 = (f32[1,456,256]{2,1,0:T(8,128)S(1)}, f32[1,456,256]{2,1,0:T(8,128)}, u32[]{:S(2)}) copy-start(f32[1,456,256]{2,1,0:T(8,128)} %param.8) | copy-start | bytes 1400836
  26.1 9.1 %copy-start.3 = (f32[1,456,256]{2,1,0:T(8,128)S(1)}, f32[1,456,256]{2,1,0:T(8,128)}, u32[]{:S(2)}) copy-start(f32[1,456,256]{2,1,0:T(8,128)} %param.9) | copy-start | bytes 1400836
  26.4 8.8 %collective-permute-start.9 = (bf16[456,256]{1,0:T(8,128)(2,1)S(1)}, bf16[456,256]{1,0:T(8,128)(2,1)S(1)}, u32[]{:S(2)}, u32[]{:S(2)}) collective-permute-start(bf16[456,256]{1,0:T(8,128)(2,1)S(1)} %fusion), channel_id=1, source_target_pairs={{0,4},{4,0},{8,12},{12,8},{16,20},{20,16},{24,28},{28,24},{1,5},{5... | collective-permute-start | bytes 700424 | tf_op jit(solution)/shard_map/ppermute | solution.py:16
  27.2 8.0 %collective-permute-start.12 = (bf16[224,256]{1,0:T(8,128)(2,1)S(1)}, bf16[224,256]{1,0:T(8,128)(2,1)S(1)}, u32[]{:S(2)}, u32[]{:S(2)}) collective-permute-start(bf16[224,256]{1,0:T(8,128)(2,1)S(1)} %add_convert_fusion.1), channel_id=1, source_target_pairs={{0,24},{4,28},{8,16},{12,20},{16,8},{20,12},{24,0},{28,4},{1,25},{... | collective-permute-start | bytes 344072 | tf_op jit(solution)/shard_map/ppermute | solution.py:121
  31.2 6.7 %collective-permute-start.10 = (bf16[232,256]{1,0:T(8,128)(2,1)S(1)}, bf16[232,256]{1,0:T(8,128)(2,1)S(1)}, u32[]{:S(2)}, u32[]{:S(2)}) collective-permute-start(bf16[232,256]{1,0:T(8,128)(2,1)S(1)} %fusion.2), channel_id=1, source_target_pairs={{0,8},{4,12},{8,0},{12,4},{16,24},{20,28},{24,16},{28,20},{1,9},{5... | collective-permute-start | bytes 356360 | tf_op jit(solution)/shard_map/ppermute | solution.py:121
  31.6 6.8 %collective-permute-start.11 = (bf16[232,256]{1,0:T(8,128)(2,1)S(1)}, bf16[232,256]{1,0:T(8,128)(2,1)S(1)}, u32[]{:S(2)}, u32[]{:S(2)}) collective-permute-start(bf16[232,256]{1,0:T(8,128)(2,1)S(1)} %add_convert_fusion), channel_id=1, source_target_pairs={{0,24},{4,28},{8,16},{12,20},{16,8},{20,12},{24,0},{28,4},{1,25},{... | collective-permute-start | bytes 356360 | tf_op jit(solution)/shard_map/ppermute | solution.py:121
